TPU v7x, 128 devices: a whole 4x4x4 slice. The times are simulated.
128 devices in a mesh: ctx: 16 (over y, x), ffn: 4 (over z_lo, core), dp: 2 (over z_hi).
Axes of the slice: x: 4, y: 4, z: 4 (z_hi: 2, z_lo: 2; z = z_hi * 2 + z_lo), core: 2. Of those that a mesh axis runs over, the one named last changes fastest.
Arguments:
- q_raw: bfloat16 [8192, 4096], P(('dp', 'ctx'), 'ffn'), parts along dimension 0, may hold values from -90 to 90, as said below
- key_raw_projections: bfloat16 [8192, 1024], P(('dp', 'ctx'), 'ffn'), parts along dimension 0, may hold values from -90 to 90, as said below
- value_projections: bfloat16 [8192, 1024], P(('dp', 'ctx'), 'ffn'), parts along dimension 0, may hold values from -6 to 6
- q_gain: float32 [128], replicated, may hold values from 0.5 to 7
- k_gain: float32 [128], replicated, may hold values from 0.5 to 7
- block_tags: int32 [128], P('dp'), parts along dimension 0, may hold values from 0 to 63, each once
- w_out: bfloat16 [4096, 4096], P('ffn'), may hold values from -0.125 to 0.125
- d_out: bfloat16 [8192, 4096], P(('dp', 'ctx'), 'ffn'), parts along dimension 0, may hold values from -48 to 48
Outputs:
- attn_out: bfloat16 [8192, 4096], P(('dp', 'ctx'), 'ffn'), parts along dimension 0
- d_q: float32 [8192, 4096], P(('dp', 'ctx'), 'ffn'), parts along dimension 0
- key_raw_gradient: float32 [8192, 1024], P(('dp', 'ctx'), 'ffn'), parts along dimension 0
- value_projection_gradient: float32 [8192, 1024], P(('dp', 'ctx'), 'ffn'), parts along dimension 0
There are 2 independent parts, one for each index of `dp`. A program takes and returns all parts, laid end to end along the dimension named above; an argument that names none is the same for every part. Nothing has to cross between parts.
Inputs may be any that keep to these rules, and one draw needn't show every extreme that they name: `q_raw`: query projections; magnitudes vary over tokens, heads and channels. `key_raw_projections`: key projections; magnitudes vary over tokens, heads and channels.
All inputs are finite; a program needn't handle non-finite values.
Results may differ from a plain program's by a relative error of at most 0.03.
The roundings to bfloat16 on the way count: a program that leaves them out, or rounds other values in their place, can miss the bound.
Values may be sent and summed in bfloat16 or wider, within the bound.
No kernel may reach another device: no remote copies, remote signals or barrier semaphores. Data moves between devices by JAX's collectives and lax.ppermute only.
A program may use at most 128 MiB of HBM per device.

v0:
```python
import math

import jax
import jax.numpy as jnp
from jax import lax
from jax.sharding import PartitionSpec as P

HEAD_SIZE = 128
BLK = 64


ROPE_BASE = 1000000.0
EPS = 1e-06
NEG = -1e30


def from_behind(value, axis, steps):
    count = lax.axis_size(axis)
    pairs = [(source, (source + steps) % count) for source in range(count)]
    return lax.ppermute(value, axis, pairs)


def rope_tables(position, width):
    freq = ROPE_BASE ** (-(jnp.arange(width // 2, dtype=jnp.float32) * 2.0 / width))
    angle = position.astype(jnp.float32)[:, None] * freq[None, :]
    cosine = jnp.concatenate([jnp.cos(angle), jnp.cos(angle)], axis=-1)
    sine = jnp.concatenate([jnp.sin(angle), jnp.sin(angle)], axis=-1)
    return (cosine, sine)


def norm_rope(values, gain, cosine, sine):
    scale_inv = lax.rsqrt(jnp.mean(values * values, axis=-1, keepdims=True) + EPS)
    normed = values * scale_inv * gain
    half = normed.shape[-1] // 2
    turned = jnp.concatenate([-normed[..., half:], normed[..., :half]], axis=-1)
    return normed * cosine[:, None, :] + turned * sine[:, None, :]


def visible_pairs(copy_q, index_q, copy_k, index_k):
    first = (copy_q == 0) & (copy_k == 0) & (index_k == index_q)
    second = (copy_q == 0) & (copy_k == 1) & (index_k < index_q)
    third = (copy_q == 1) & (copy_k == 1) & (index_k <= index_q)
    return first | second | third


def token_info(block_tags, start, count):
    nblk = block_tags.shape[0]
    where_tok = start + jnp.arange(count, dtype=jnp.int32)
    block_num = where_tok // BLK
    hits = block_num[:, None] == jnp.arange(nblk, dtype=jnp.int32)[None, :]
    tags = jnp.sum(jnp.where(hits, block_tags[None, :], 0), axis=1)
    copy = (tags >= nblk // 2).astype(jnp.int32)
    index = tags - copy * (nblk // 2)
    return (copy, index, index * BLK + where_tok % BLK)


def per_device(
    q_raw, key_raw_projections, value_projections, q_gain, k_gain, block_tags, w_out, d_out
):
    tok = q_raw.shape[0]
    nctx = lax.axis_size("ctx")
    here = lax.axis_index("ctx")
    q_heads = q_raw.shape[1] // HEAD_SIZE
    k_heads = key_raw_projections.shape[1] // HEAD_SIZE
    head_group = q_heads // k_heads
    scale = HEAD_SIZE ** (-0.5)
    copy_q, index_q, position = token_info(block_tags, here * tok, tok)
    copy_rows = jnp.tile(copy_q, head_group)
    index_rows = jnp.tile(index_q, head_group)
    cosine, sine = rope_tables(position, HEAD_SIZE)
    q_float = q_raw.astype(jnp.float32).reshape(tok, q_heads, HEAD_SIZE)
    keys_single_precision = key_raw_projections.astype(jnp.float32).reshape(tok, k_heads, HEAD_SIZE)
    q_rot, q_back = jax.vjp(lambda x: norm_rope(x, q_gain, cosine, sine), q_float)
    k_rot, keys_backward = jax.vjp(
        lambda x: norm_rope(x, k_gain, cosine, sine), keys_single_precision
    )
    query_groups = (
        q_rot.astype(jnp.bfloat16)
        .reshape(tok, k_heads, head_group, HEAD_SIZE)
        .transpose(1, 2, 0, 3)
    )
    query_groups = query_groups.reshape(k_heads, head_group * tok, HEAD_SIZE)
    k_flat = k_rot.astype(jnp.bfloat16).reshape(tok, k_heads * HEAD_SIZE)
    row_indices = head_group * tok

    def tile_mask(start, count):
        copy_k, index_k, unused = token_info(block_tags, start, count)
        return visible_pairs(
            copy_rows[:, None], index_rows[:, None], copy_k[None, :], index_k[None, :]
        )

    def forward_tile(carry, k_piece, v_piece, start):
        count = k_piece.shape[0]
        mask = tile_mask(start, count)
        top, total, accum = carry
        k_grp = k_piece.reshape(count, k_heads, HEAD_SIZE)
        v_grp = v_piece.reshape(count, k_heads, HEAD_SIZE)
        scores = (
            jnp.einsum("gqd,kgd->gqk", query_groups, k_grp, preferred_element_type=jnp.float32)
            * scale
        )
        scores = jnp.where(mask[None], scores, NEG)
        new_top = jnp.maximum(top, jnp.max(scores, axis=-1))
        expo = jnp.where(mask[None], jnp.exp(scores - new_top[..., None]), 0.0)
        factor = jnp.exp(top - new_top)
        new_total = total * factor + jnp.sum(expo, axis=-1)
        added = jnp.einsum(
            "gqk,kgd->gqd", expo.astype(jnp.bfloat16), v_grp, preferred_element_type=jnp.float32
        )
        return (new_top, new_total, accum * factor[..., None] + added)

    begin = (
        jnp.full((k_heads, row_indices), NEG, jnp.float32),
        jnp.zeros((k_heads, row_indices), jnp.float32),
        jnp.zeros((k_heads, row_indices, HEAD_SIZE), jnp.float32),
    )
    k_piece = lax.all_gather(k_flat, "ctx", axis=0, tiled=True)
    v_piece = lax.all_gather(value_projections, "ctx", axis=0, tiled=True)
    count = k_piece.shape[0]
    step = math.gcd(count, 512)

    def inner(turn, state):
        offset = turn * step
        k_part = lax.dynamic_slice_in_dim(k_piece, offset, step, 0)
        v_part = lax.dynamic_slice_in_dim(v_piece, offset, step, 0)
        return forward_tile(state, k_part, v_part, offset)

    top, total, accum = lax.fori_loop(0, count // step, inner, begin)
    out_bf = (accum / total[..., None]).astype(jnp.bfloat16)
    log_total = top + jnp.log(total)
    attn = (
        out_bf.reshape(k_heads, head_group, tok, HEAD_SIZE)
        .transpose(2, 0, 1, 3)
        .reshape(tok, q_heads * HEAD_SIZE)
    )
    partial_out = jnp.dot(attn, w_out, preferred_element_type=jnp.float32)
    attn_out = lax.psum_scatter(
        partial_out.astype(jnp.bfloat16), "ffn", scatter_dimension=1, tiled=True
    )
    attention_gradient = lax.dot_general(
        lax.all_gather(d_out, "ffn", axis=1, tiled=True),
        w_out,
        (((1,), (1,)), ((), ())),
        preferred_element_type=jnp.float32,
    )
    gradient_groups = (
        attention_gradient.astype(jnp.bfloat16)
        .reshape(tok, k_heads, head_group, HEAD_SIZE)
        .transpose(1, 2, 0, 3)
    )
    gradient_groups = gradient_groups.reshape(k_heads, row_indices, HEAD_SIZE)
    delta = jnp.sum(gradient_groups.astype(jnp.float32) * out_bf.astype(jnp.float32), axis=-1)

    def back_tile(k_piece, v_piece, start):
        count = k_piece.shape[0]
        mask = tile_mask(start, count)
        k_grp = k_piece.reshape(count, k_heads, HEAD_SIZE)
        v_grp = v_piece.reshape(count, k_heads, HEAD_SIZE)
        scores = (
            jnp.einsum("gqd,kgd->gqk", query_groups, k_grp, preferred_element_type=jnp.float32)
            * scale
        )
        probs = jnp.where(mask[None], jnp.exp(scores - log_total[..., None]), 0.0)
        value_gradient_total = jnp.einsum(
            "gqk,gqd->kgd",
            probs.astype(jnp.bfloat16),
            gradient_groups,
            preferred_element_type=jnp.float32,
        )
        grad_p = jnp.einsum(
            "gqd,kgd->gqk", gradient_groups, v_grp, preferred_element_type=jnp.float32
        )
        grad_s = (probs * (grad_p - delta[..., None])).astype(jnp.bfloat16)
        grad_q = (
            jnp.einsum("gqk,kgd->gqd", grad_s, k_grp, preferred_element_type=jnp.float32) * scale
        )
        key_gradient_total = (
            jnp.einsum("gqk,gqd->kgd", grad_s, query_groups, preferred_element_type=jnp.float32)
            * scale
        )
        return (
            grad_q,
            key_gradient_total.reshape(count, k_heads * HEAD_SIZE),
            value_gradient_total.reshape(count, k_heads * HEAD_SIZE),
        )

    width = k_heads * HEAD_SIZE

    def turn(step, carry):
        k_piece, v_piece, acc_k, acc_v, grad_q = carry
        start = (here - step) % nctx * tok
        term_q, term_k, term_v = back_tile(k_piece, v_piece, start)
        k_piece, v_piece = from_behind((k_piece, v_piece), "ctx", 1)
        acc_k, acc_v = (
            from_behind((acc_k + term_k).astype(jnp.bfloat16), "ctx", 1).astype(jnp.float32),
            from_behind((acc_v + term_v).astype(jnp.bfloat16), "ctx", 1).astype(jnp.float32),
        )
        return (k_piece, v_piece, acc_k, acc_v, grad_q + term_q)

    start_state = (
        k_flat,
        value_projections,
        jnp.zeros((tok, width), jnp.float32),
        jnp.zeros((tok, width), jnp.float32),
        jnp.zeros((k_heads, row_indices, HEAD_SIZE), jnp.float32),
    )
    unused_k, unused_v, key_gradient_total, value_gradient_total, grad_q = lax.fori_loop(
        0, nctx, turn, start_state
    )
    grad_q = (
        grad_q.reshape(k_heads, head_group, tok, HEAD_SIZE)
        .transpose(2, 0, 1, 3)
        .reshape(tok, q_heads, HEAD_SIZE)
    )
    d_q = q_back(grad_q)[0].reshape(tok, q_heads * HEAD_SIZE)
    key_raw_gradient = keys_backward(key_gradient_total.reshape(tok, k_heads, HEAD_SIZE))[
        0
    ].reshape(tok, width)
    return (attn_out, d_q, key_raw_gradient, value_gradient_total)


def solution(mesh):
    placed = (
        P(("dp", "ctx"), "ffn"),
        P(("dp", "ctx"), "ffn"),
        P(("dp", "ctx"), "ffn"),
        P(),
        P(),
        P("dp"),
        P("ffn", None),
        P(("dp", "ctx"), "ffn"),
    )
    return jax.shard_map(
        per_device,
        mesh=mesh,
        in_specs=placed,
        out_specs=(
            P(("dp", "ctx"), "ffn"),
            P(("dp", "ctx"), "ffn"),
            P(("dp", "ctx"), "ffn"),
            P(("dp", "ctx"), "ffn"),
        ),
        check_vma=False,
    )
```

profile of v0, /device:TPU:96, one launch (start us, length us, event | category | flops | bytes accessed | tf_op | source)
XLA Modules:
  0.0 695.6 jit_solution(8082654131733500830)
XLA Ops:
  32.9 6.3 all-gather.8.cloned.1.call-done
  39.2 6.4 convolution_convert_fusion.1
  48.1 39.9 %all-gather.4.cloned.1.call-done = bf16[4096,256]{1,0:T(8,128)(2,1)} async-done(((bf16[256,256]{1,0:T(8,128)(2,1)}), bf16[4096,256]{1,0:T(8,128)(2,1)}) %all-gather.4.cloned.1.call-update) | async-done | bytes 2097168 | tf_op jit(solution)/shard_map/all_gather | solution.py:117
  88.0 49.1 %all-gather.6.cloned.1.call-done = bf16[4096,256]{0,1:T(8,128)(2,1)} async-done(((bf16[256,256]{0,1:T(8,128)(2,1)}), bf16[4096,256]{0,1:T(8,128)(2,1)}) %all-gather.6.cloned.1.call-update) | async-done | bytes 2097168 | tf_op jit(solution)/shard_map/all_gather | solution.py:118
  137.1 119.3 %while.44 = (s32[]{:T(128)}, f32[2,1024]{1,0:T(2,128)S(1)}, f32[2,1024]{1,0:T(2,128)S(1)}, f32[2,1024,128]{2,1,0:T(8,128)}, s32[64]{0:T(128)S(1)}, /*index=5*/bf...) while((s32[]{:T(128)}, f32[2,1024]{1,0:T(2,128)S(1)}, ...), condition=%wide.region_7.8_spmd.clone, body=%wide.region_3.7_spmd.clone.sunk | while | flops 557176320 | bytes 44740124 | solution.py:128
  140.5 4.1 fusion.95
  144.5 3.4 fusion.97
  155.4 4.1 fusion.95
  159.4 3.4 fusion.97
  170.3 4.1 fusion.95
  185.2 4.1 fusion.95
  189.3 3.4 fusion.97
  200.1 4.1 fusion.95
  204.2 3.4 fusion.97
  215.0 4.1 fusion.95
  230.0 4.1 fusion.95
  244.9 4.1 fusion.95
  260.1 7.3 %convolution_convert_fusion = bf16[256,4096]{1,0:T(8,128)(2,1)} fusion(bf16[256,1024]{0,1:T(8,128)(2,1)} %bitcast.181, bf16[1024,4096]{1,0:T(8,128)(2,1)} %param.18), kind=kOutput, calls=%fused_computation.73 | convolution fusion | flops 2148532224 | bytes 11010048 | tf_op jit(solution)/shard_map/dot_general | solution.py:136
  267.5 407.4 %while.45 = (s32[]{:T(128)}, bf16[256,256]{1,0:T(8,128)(2,1)S(1)}, bf16[256,256]{1,0:T(8,128)(2,1)}, f32[256,256]{0,1:T(8,128)}, f32[256,256]{0,1:T(8,128)}, /*i...) while((s32[]{:T(128)}, bf16[256,256]{1,0:T(8,128)(2,1)S(1)}, ...), condition=%wide.region_12.13_spmd.clone, body=%wide.region_10.12_spmd.clone.sunk | while | flops 679073792 | bytes 21942040 | solution.py:207
  287.0 4.0 collective-permute-done.2
  312.7 3.5 collective-permute-done.2
  333.2 3.5 collective-permute-start.3
  362.3 4.0 collective-permute-done.2
  388.1 5.5 collective-permute-done.2
  412.0 4.6 collective-permute-start.3
  443.3 4.0 collective-permute-done.2
  468.3 3.5 collective-permute-done.2
  539.1 4.5 collective-permute-start.3
  565.3 4.1 collective-permute-start.3
  594.5 3.6 collective-permute-done.2
  619.0 3.5 collective-permute-done.2
  664.6 3.5 collective-permute-start.3
  (874 shorter events, 471.9 us)
Async XLA Ops:
  7.2 32.0 %all-gather.8.cloned.1.call-start = ((), (), s32[]{:S(2)}) async-start(), calls=%async_computation.4 | async-start | bytes 2621440 | tf_op jit(solution)/shard_map/all_gather | solution.py:141
  8.9 79.1 %all-gather.4.cloned.1.call-start = ((), (), s32[]{:S(2)}) async-start(), calls=%async_computation.1 | async-start | bytes 2228224 | tf_op jit(solution)/shard_map/all_gather | solution.py:117
  15.7 121.4 %all-gather.6.cloned.1.call-start = ((), (), s32[]{:S(2)}) async-start(), calls=%async_computation.2 | async-start | bytes 2228224 | tf_op jit(solution)/shard_map/all_gather | solution.py:118
  17.4 671.6 %reduce-scatter.2.cloned.1.call-start = ((), (), s32[]{:S(2)}) async-start(), calls=%async_computation.3 | async-start | bytes 2621440 | tf_op jit(solution)/shard_map/reduce_scatter | solution.py:137
  267.5 27.6 %collective-permute-start = (bf16[256,256]{1,0:T(8,128)(2,1)S(1)}, bf16[256,256]{1,0:T(8,128)(2,1)S(1)}, u32[]{:S(2)}, u32[]{:S(2)}) collective-permute-start(bf16[256,256]{1,0:T(8,128)(2,1)S(1)} %copy.254), channel_id=1, source_target_pairs={{0,8},{8,16},{16,24},{24,32},{32,40},{40,48},{48,56},{56,64},{64,7... | collective-permute-start | bytes 393224 | tf_op jit(solution)/shard_map/while/body/eval_jaxpr/ppermute | solution.py:20
  269.6 25.5 %collective-permute-start.1 = (bf16[256,256]{1,0:T(8,128)(2,1)S(1)}, bf16[256,256]{1,0:T(8,128)(2,1)}, u32[]{:S(2)}, u32[]{:S(2)}) collective-permute-start(bf16[256,256]{1,0:T(8,128)(2,1)S(1)} %copy.255), channel_id=1, source_target_pairs={{0,8},{8,16},{16,24},{24,32},{32,40},{40,48},{48,56},{56,64},{64,7... | collective-permute-start | bytes 393224 | tf_op jit(solution)/shard_map/while/body/eval_jaxpr/ppermute | solution.py:20
  295.1 24.4 %collective-permute-start = (bf16[256,256]{1,0:T(8,128)(2,1)S(1)}, bf16[256,256]{1,0:T(8,128)(2,1)S(1)}, u32[]{:S(2)}, u32[]{:S(2)}) collective-permute-start(bf16[256,256]{1,0:T(8,128)(2,1)S(1)} %copy.254), channel_id=1, source_target_pairs={{0,8},{8,16},{16,24},{24,32},{32,40},{40,48},{48,56},{56,64},{64,7... | collective-permute-start | bytes 393224 | tf_op jit(solution)/shard_map/while/body/eval_jaxpr/ppermute | solution.py:20
  319.6 24.4 %collective-permute-start = (bf16[256,256]{1,0:T(8,128)(2,1)S(1)}, bf16[256,256]{1,0:T(8,128)(2,1)S(1)}, u32[]{:S(2)}, u32[]{:S(2)}) collective-permute-start(bf16[256,256]{1,0:T(8,128)(2,1)S(1)} %copy.254), channel_id=1, source_target_pairs={{0,8},{8,16},{16,24},{24,32},{32,40},{40,48},{48,56},{56,64},{64,7... | collective-permute-start | bytes 393224 | tf_op jit(solution)/shard_map/while/body/eval_jaxpr/ppermute | solution.py:20
  344.0 25.6 %collective-permute-start = (bf16[256,256]{1,0:T(8,128)(2,1)S(1)}, bf16[256,256]{1,0:T(8,128)(2,1)S(1)}, u32[]{:S(2)}, u32[]{:S(2)}) collective-permute-start(bf16[256,256]{1,0:T(8,128)(2,1)S(1)} %copy.254), channel_id=1, source_target_pairs={{0,8},{8,16},{16,24},{24,32},{32,40},{40,48},{48,56},{56,64},{64,7... | collective-permute-start | bytes 393224 | tf_op jit(solution)/shard_map/while/body/eval_jaxpr/ppermute | solution.py:20
  345.0 24.6 %collective-permute-start.1 = (bf16[256,256]{1,0:T(8,128)(2,1)S(1)}, bf16[256,256]{1,0:T(8,128)(2,1)}, u32[]{:S(2)}, u32[]{:S(2)}) collective-permute-start(bf16[256,256]{1,0:T(8,128)(2,1)S(1)} %copy.255), channel_id=1, source_target_pairs={{0,8},{8,16},{16,24},{24,32},{32,40},{40,48},{48,56},{56,64},{64,7... | collective-permute-start | bytes 393224 | tf_op jit(solution)/shard_map/while/body/eval_jaxpr/ppermute | solution.py:20
  369.7 28.4 %collective-permute-start = (bf16[256,256]{1,0:T(8,128)(2,1)S(1)}, bf16[256,256]{1,0:T(8,128)(2,1)S(1)}, u32[]{:S(2)}, u32[]{:S(2)}) collective-permute-start(bf16[256,256]{1,0:T(8,128)(2,1)S(1)} %copy.254), channel_id=1, source_target_pairs={{0,8},{8,16},{16,24},{24,32},{32,40},{40,48},{48,56},{56,64},{64,7... | collective-permute-start | bytes 393224 | tf_op jit(solution)/shard_map/while/body/eval_jaxpr/ppermute | solution.py:20
  370.7 27.4 %collective-permute-start.1 = (bf16[256,256]{1,0:T(8,128)(2,1)S(1)}, bf16[256,256]{1,0:T(8,128)(2,1)}, u32[]{:S(2)}, u32[]{:S(2)}) collective-permute-start(bf16[256,256]{1,0:T(8,128)(2,1)S(1)} %copy.255), channel_id=1, source_target_pairs={{0,8},{8,16},{16,24},{24,32},{32,40},{40,48},{48,56},{56,64},{64,7... | collective-permute-start | bytes 393224 | tf_op jit(solution)/shard_map/while/body/eval_jaxpr/ppermute | solution.py:20
  398.1 26.8 %collective-permute-start = (bf16[256,256]{1,0:T(8,128)(2,1)S(1)}, bf16[256,256]{1,0:T(8,128)(2,1)S(1)}, u32[]{:S(2)}, u32[]{:S(2)}) collective-permute-start(bf16[256,256]{1,0:T(8,128)(2,1)S(1)} %copy.254), channel_id=1, source_target_pairs={{0,8},{8,16},{16,24},{24,32},{32,40},{40,48},{48,56},{56,64},{64,7... | collective-permute-start | bytes 393224 | tf_op jit(solution)/shard_map/while/body/eval_jaxpr/ppermute | solution.py:20
  399.1 25.8 %collective-permute-start.1 = (bf16[256,256]{1,0:T(8,128)(2,1)S(1)}, bf16[256,256]{1,0:T(8,128)(2,1)}, u32[]{:S(2)}, u32[]{:S(2)}) collective-permute-start(bf16[256,256]{1,0:T(8,128)(2,1)S(1)} %copy.255), channel_id=1, source_target_pairs={{0,8},{8,16},{16,24},{24,32},{32,40},{40,48},{48,56},{56,64},{64,7... | collective-permute-start | bytes 393224 | tf_op jit(solution)/shard_map/while/body/eval_jaxpr/ppermute | solution.py:20
  424.9 25.7 %collective-permute-start = (bf16[256,256]{1,0:T(8,128)(2,1)S(1)}, bf16[256,256]{1,0:T(8,128)(2,1)S(1)}, u32[]{:S(2)}, u32[]{:S(2)}) collective-permute-start(bf16[256,256]{1,0:T(8,128)(2,1)S(1)} %copy.254), channel_id=1, source_target_pairs={{0,8},{8,16},{16,24},{24,32},{32,40},{40,48},{48,56},{56,64},{64,7... | collective-permute-start | bytes 393224 | tf_op jit(solution)/shard_map/while/body/eval_jaxpr/ppermute | solution.py:20
  425.9 24.8 %collective-permute-start.1 = (bf16[256,256]{1,0:T(8,128)(2,1)S(1)}, bf16[256,256]{1,0:T(8,128)(2,1)}, u32[]{:S(2)}, u32[]{:S(2)}) collective-permute-start(bf16[256,256]{1,0:T(8,128)(2,1)S(1)} %copy.255), channel_id=1, source_target_pairs={{0,8},{8,16},{16,24},{24,32},{32,40},{40,48},{48,56},{56,64},{64,7... | collective-permute-start | bytes 393224 | tf_op jit(solution)/shard_map/while/body/eval_jaxpr/ppermute | solution.py:20
  450.6 24.4 %collective-permute-start = (bf16[256,256]{1,0:T(8,128)(2,1)S(1)}, bf16[256,256]{1,0:T(8,128)(2,1)S(1)}, u32[]{:S(2)}, u32[]{:S(2)}) collective-permute-start(bf16[256,256]{1,0:T(8,128)(2,1)S(1)} %copy.254), channel_id=1, source_target_pairs={{0,8},{8,16},{16,24},{24,32},{32,40},{40,48},{48,56},{56,64},{64,7... | collective-permute-start | bytes 393224 | tf_op jit(solution)/shard_map/while/body/eval_jaxpr/ppermute | solution.py:20
  475.1 24.5 %collective-permute-start = (bf16[256,256]{1,0:T(8,128)(2,1)S(1)}, bf16[256,256]{1,0:T(8,128)(2,1)S(1)}, u32[]{:S(2)}, u32[]{:S(2)}) collective-permute-start(bf16[256,256]{1,0:T(8,128)(2,1)S(1)} %copy.254), channel_id=1, source_target_pairs={{0,8},{8,16},{16,24},{24,32},{32,40},{40,48},{48,56},{56,64},{64,7... | collective-permute-start | bytes 393224 | tf_op jit(solution)/shard_map/while/body/eval_jaxpr/ppermute | solution.py:20
  476.1 23.5 %collective-permute-start.1 = (bf16[256,256]{1,0:T(8,128)(2,1)S(1)}, bf16[256,256]{1,0:T(8,128)(2,1)}, u32[]{:S(2)}, u32[]{:S(2)}) collective-permute-start(bf16[256,256]{1,0:T(8,128)(2,1)S(1)} %copy.255), channel_id=1, source_target_pairs={{0,8},{8,16},{16,24},{24,32},{32,40},{40,48},{48,56},{56,64},{64,7... | collective-permute-start | bytes 393224 | tf_op jit(solution)/shard_map/while/body/eval_jaxpr/ppermute | solution.py:20
  499.6 24.6 %collective-permute-start = (bf16[256,256]{1,0:T(8,128)(2,1)S(1)}, bf16[256,256]{1,0:T(8,128)(2,1)S(1)}, u32[]{:S(2)}, u32[]{:S(2)}) collective-permute-start(bf16[256,256]{1,0:T(8,128)(2,1)S(1)} %copy.254), channel_id=1, source_target_pairs={{0,8},{8,16},{16,24},{24,32},{32,40},{40,48},{48,56},{56,64},{64,7... | collective-permute-start | bytes 393224 | tf_op jit(solution)/shard_map/while/body/eval_jaxpr/ppermute | solution.py:20
  500.6 23.6 %collective-permute-start.1 = (bf16[256,256]{1,0:T(8,128)(2,1)S(1)}, bf16[256,256]{1,0:T(8,128)(2,1)}, u32[]{:S(2)}, u32[]{:S(2)}) collective-permute-start(bf16[256,256]{1,0:T(8,128)(2,1)S(1)} %copy.255), channel_id=1, source_target_pairs={{0,8},{8,16},{16,24},{24,32},{32,40},{40,48},{48,56},{56,64},{64,7... | collective-permute-start | bytes 393224 | tf_op jit(solution)/shard_map/while/body/eval_jaxpr/ppermute | solution.py:20
  524.2 25.2 %collective-permute-start = (bf16[256,256]{1,0:T(8,128)(2,1)S(1)}, bf16[256,256]{1,0:T(8,128)(2,1)S(1)}, u32[]{:S(2)}, u32[]{:S(2)}) collective-permute-start(bf16[256,256]{1,0:T(8,128)(2,1)S(1)} %copy.254), channel_id=1, source_target_pairs={{0,8},{8,16},{16,24},{24,32},{32,40},{40,48},{48,56},{56,64},{64,7... | collective-permute-start | bytes 393224 | tf_op jit(solution)/shard_map/while/body/eval_jaxpr/ppermute | solution.py:20
  525.2 24.2 %collective-permute-start.1 = (bf16[256,256]{1,0:T(8,128)(2,1)S(1)}, bf16[256,256]{1,0:T(8,128)(2,1)}, u32[]{:S(2)}, u32[]{:S(2)}) collective-permute-start(bf16[256,256]{1,0:T(8,128)(2,1)S(1)} %copy.255), channel_id=1, source_target_pairs={{0,8},{8,16},{16,24},{24,32},{32,40},{40,48},{48,56},{56,64},{64,7... | collective-permute-start | bytes 393224 | tf_op jit(solution)/shard_map/while/body/eval_jaxpr/ppermute | solution.py:20
  549.4 26.2 %collective-permute-start = (bf16[256,256]{1,0:T(8,128)(2,1)S(1)}, bf16[256,256]{1,0:T(8,128)(2,1)S(1)}, u32[]{:S(2)}, u32[]{:S(2)}) collective-permute-start(bf16[256,256]{1,0:T(8,128)(2,1)S(1)} %copy.254), channel_id=1, source_target_pairs={{0,8},{8,16},{16,24},{24,32},{32,40},{40,48},{48,56},{56,64},{64,7... | collective-permute-start | bytes 393224 | tf_op jit(solution)/shard_map/while/body/eval_jaxpr/ppermute | solution.py:20
  551.5 24.0 %collective-permute-start.1 = (bf16[256,256]{1,0:T(8,128)(2,1)S(1)}, bf16[256,256]{1,0:T(8,128)(2,1)}, u32[]{:S(2)}, u32[]{:S(2)}) collective-permute-start(bf16[256,256]{1,0:T(8,128)(2,1)S(1)} %copy.255), channel_id=1, source_target_pairs={{0,8},{8,16},{16,24},{24,32},{32,40},{40,48},{48,56},{56,64},{64,7... | collective-permute-start | bytes 393224 | tf_op jit(solution)/shard_map/while/body/eval_jaxpr/ppermute | solution.py:20
  575.6 25.8 %collective-permute-start = (bf16[256,256]{1,0:T(8,128)(2,1)S(1)}, bf16[256,256]{1,0:T(8,128)(2,1)S(1)}, u32[]{:S(2)}, u32[]{:S(2)}) collective-permute-start(bf16[256,256]{1,0:T(8,128)(2,1)S(1)} %copy.254), channel_id=1, source_target_pairs={{0,8},{8,16},{16,24},{24,32},{32,40},{40,48},{48,56},{56,64},{64,7... | collective-permute-start | bytes 393224 | tf_op jit(solution)/shard_map/while/body/eval_jaxpr/ppermute | solution.py:20
  577.3 24.0 %collective-permute-start.1 = (bf16[256,256]{1,0:T(8,128)(2,1)S(1)}, bf16[256,256]{1,0:T(8,128)(2,1)}, u32[]{:S(2)}, u32[]{:S(2)}) collective-permute-start(bf16[256,256]{1,0:T(8,128)(2,1)S(1)} %copy.255), channel_id=1, source_target_pairs={{0,8},{8,16},{16,24},{24,32},{32,40},{40,48},{48,56},{56,64},{64,7... | collective-permute-start | bytes 393224 | tf_op jit(solution)/shard_map/while/body/eval_jaxpr/ppermute | solution.py:20
  601.3 24.4 %collective-permute-start = (bf16[256,256]{1,0:T(8,128)(2,1)S(1)}, bf16[256,256]{1,0:T(8,128)(2,1)S(1)}, u32[]{:S(2)}, u32[]{:S(2)}) collective-permute-start(bf16[256,256]{1,0:T(8,128)(2,1)S(1)} %copy.254), channel_id=1, source_target_pairs={{0,8},{8,16},{16,24},{24,32},{32,40},{40,48},{48,56},{56,64},{64,7... | collective-permute-start | bytes 393224 | tf_op jit(solution)/shard_map/while/body/eval_jaxpr/ppermute | solution.py:20
  625.8 24.5 %collective-permute-start = (bf16[256,256]{1,0:T(8,128)(2,1)S(1)}, bf16[256,256]{1,0:T(8,128)(2,1)S(1)}, u32[]{:S(2)}, u32[]{:S(2)}) collective-permute-start(bf16[256,256]{1,0:T(8,128)(2,1)S(1)} %copy.254), channel_id=1, source_target_pairs={{0,8},{8,16},{16,24},{24,32},{32,40},{40,48},{48,56},{56,64},{64,7... | collective-permute-start | bytes 393224 | tf_op jit(solution)/shard_map/while/body/eval_jaxpr/ppermute | solution.py:20
  626.8 23.5 %collective-permute-start.1 = (bf16[256,256]{1,0:T(8,128)(2,1)S(1)}, bf16[256,256]{1,0:T(8,128)(2,1)}, u32[]{:S(2)}, u32[]{:S(2)}) collective-permute-start(bf16[256,256]{1,0:T(8,128)(2,1)S(1)} %copy.255), channel_id=1, source_target_pairs={{0,8},{8,16},{16,24},{24,32},{32,40},{40,48},{48,56},{56,64},{64,7... | collective-permute-start | bytes 393224 | tf_op jit(solution)/shard_map/while/body/eval_jaxpr/ppermute | solution.py:20
  650.3 24.6 %collective-permute-start = (bf16[256,256]{1,0:T(8,128)(2,1)S(1)}, bf16[256,256]{1,0:T(8,128)(2,1)S(1)}, u32[]{:S(2)}, u32[]{:S(2)}) collective-permute-start(bf16[256,256]{1,0:T(8,128)(2,1)S(1)} %copy.254), channel_id=1, source_target_pairs={{0,8},{8,16},{16,24},{24,32},{32,40},{40,48},{48,56},{56,64},{64,7... | collective-permute-start | bytes 393224 | tf_op jit(solution)/shard_map/while/body/eval_jaxpr/ppermute | solution.py:20
  651.3 23.6 %collective-permute-start.1 = (bf16[256,256]{1,0:T(8,128)(2,1)S(1)}, bf16[256,256]{1,0:T(8,128)(2,1)}, u32[]{:S(2)}, u32[]{:S(2)}) collective-permute-start(bf16[256,256]{1,0:T(8,128)(2,1)S(1)} %copy.255), channel_id=1, source_target_pairs={{0,8},{8,16},{16,24},{24,32},{32,40},{40,48},{48,56},{56,64},{64,7... | collective-permute-start | bytes 393224 | tf_op jit(solution)/shard_map/while/body/eval_jaxpr/ppermute | solution.py:20
  (114 other events, 848.1 us)
Sparse Core Ops, SparseCore 0:
  9.7 29.4 all-gather.7
  41.4 46.6 all-gather.3
  90.1 46.8 all-gather.5
  267.6 26.9 reduce-scatter.1
where the time goes:
time: 700 us; the launch traced here: 696 us
  other arithmetic  203 us (29%)
  waiting for transfers between devices  154 us (22%)
  local copies, waits for them, and re-layouts  135 us (19%)
  matrix products  117 us (17%)
  starting transfers between devices  69.4 us (10%)
  between operations  14.3 us (2%)
    ppermute x64, starting transfers between devices, from_behind(): return lax.ppermute(value, axis, pairs)  69.2 us
    ppermute x64, waiting for transfers between devices, from_behind(): return lax.ppermute(value, axis, pairs)  58.6 us
    all_gather x1, waiting for transfers between devices, per_device(): v_piece = lax.all_gather(value_projections, 'ctx', axis=0, tiled=True)  49.1 us
    or x24, other arithmetic, visible_pairs(): return first | second | third  40.1 us
    all_gather x1, waiting for transfers between devices, per_device(): k_piece = lax.all_gather(k_flat, 'ctx', axis=0, tiled=True)  39.9 us
    dot_general x8, matrix products, forward_tile(): jnp.einsum('gqd,kgd->gqk', query_groups, k_grp, preferred_element_type=jn...  32.4 us
    another operation x48, local copies, waits for them, and re-layouts, per_device(): copy_rows = jnp.tile(copy_q, head_group)  27.7 us
    reduce_sum x8, other arithmetic, forward_tile(): new_total = total * factor + jnp.sum(expo, axis=-1)  27.6 us
  transfers between devices with their start and end apart: 68, of which 23 were waited for; matrix products, arithmetic and copies ran while one was open for 47% of the time, Pallas kernels for 0%

commit v1 on v0

v1 whole, which is shorter than its diff:
```python
import functools

import jax
import jax.numpy as jnp
import numpy as np
from jax import lax
from jax.experimental import pallas as pl
from jax.experimental.pallas import tpu as pltpu
from jax.sharding import PartitionSpec as P

HEAD = 128
BLK = 64
ROPE_BASE = 1000000.0
EPS = 1e-06
NEG = -1e30
SCALE = HEAD ** (-0.5)
SIDE = 4
VMEM = pl.BlockSpec(memory_space=pltpu.VMEM)
SMEM = pl.BlockSpec(memory_space=pltpu.SMEM)
LIMIT = 48 * 1024 * 1024


def shape(dims, dtype):
    return jax.ShapeDtypeStruct(dims, dtype)


def params():
    return pltpu.CompilerParams(vmem_limit_bytes=LIMIT)


def cost(flops, nbytes):
    return pl.CostEstimate(flops=flops, bytes_accessed=nbytes, transcendentals=0)


def angle_table(blocks):
    freq = ROPE_BASE ** (-(np.arange(HEAD // 2) * 2.0 / HEAD))
    freq = np.concatenate([freq, freq])[None, :]
    inner = np.arange(BLK)[:, None] * freq
    outer = (np.arange(blocks) * BLK)[:, None] * freq
    return np.concatenate([np.cos(inner), np.sin(inner), np.cos(outer), np.sin(outer)]).astype(np.float32)


def half_sign():
    lane = lax.broadcasted_iota(jnp.int32, (1, HEAD), 1)
    return jnp.where(lane < HEAD // 2, -1.0, 1.0).astype(jnp.float32)


def block_angles(table_ref, index, blocks):
    c_in, s_in = table_ref[0:BLK, :], table_ref[BLK : 2 * BLK, :]
    c_out = table_ref[pl.ds(2 * BLK + index, 1), :]
    s_out = table_ref[pl.ds(2 * BLK + blocks + index, 1), :]
    return c_in * c_out - s_in * s_out, s_in * c_out + c_in * s_out


def norm_rope(x, gain, cosine, sine_signed):
    normed = x * lax.rsqrt(jnp.mean(x * x, axis=-1, keepdims=True) + EPS) * gain
    return normed * cosine + pltpu.roll(normed, HEAD // 2, 1) * sine_signed


def norm_rope_back(x, dy, gain, cosine, sine_signed):
    inv = lax.rsqrt(jnp.mean(x * x, axis=-1, keepdims=True) + EPS)
    dn = (dy * cosine + pltpu.roll(dy * sine_signed, HEAD // 2, 1)) * gain
    inner = jnp.mean(x * dn, axis=-1, keepdims=True)
    return inv * dn - x * (inv * inv * inv * inner)


def key_kernel(tags_ref, key_ref, value_ref, gain_ref, table_ref, *outs, blocks):
    kv_refs, cos_ref, sin_ref = outs[:-2], outs[-2], outs[-1]
    gain, sign = gain_ref[...], half_sign()
    for j in range(key_ref.shape[0] // BLK):
        rows = slice(j * BLK, (j + 1) * BLK)
        cosine, sine = block_angles(table_ref, tags_ref[j] % blocks, blocks)
        sine = sine * sign
        cos_ref[rows, :] = cosine
        sin_ref[rows, :] = sine
        for g, kv in enumerate(kv_refs):
            cols = slice(g * HEAD, (g + 1) * HEAD)
            x = key_ref[rows, cols].astype(jnp.float32)
            kv[rows, 0:HEAD] = norm_rope(x, gain, cosine, sine).astype(jnp.bfloat16)
            kv[rows, HEAD:] = value_ref[rows, cols]


def key_prep(own_tags, keys, values, gain, table, heads):
    tok = keys.shape[0]
    blocks = (table.shape[0] - 2 * BLK) // 2
    return pl.pallas_call(
        functools.partial(key_kernel, blocks=blocks),
        in_specs=[SMEM, VMEM, VMEM, VMEM, VMEM],
        out_specs=[VMEM] * (heads + 2),
        out_shape=[shape((tok, 2 * HEAD), jnp.bfloat16)] * heads + [shape((tok, HEAD), jnp.float32)] * 2,
        compiler_params=params(),
        cost_estimate=cost(0, 1 << 20),
        name="key_prep",
    )(own_tags, keys, values, gain, table)


def query_kernel(q_ref, gain_ref, cos_ref, sin_ref, out_ref):
    gain, cosine, sine = gain_ref[...], cos_ref[...], sin_ref[...]
    for h in range(q_ref.shape[1] // HEAD):
        cols = slice(h * HEAD, (h + 1) * HEAD)
        x = q_ref[:, cols].astype(jnp.float32)
        out_ref[:, cols] = norm_rope(x, gain, cosine, sine).astype(jnp.bfloat16)


def query_prep(q_raw, gain, cosine, sine):
    return pl.pallas_call(
        query_kernel,
        in_specs=[VMEM] * 4,
        out_specs=VMEM,
        out_shape=shape(q_raw.shape, jnp.bfloat16),
        compiler_params=params(),
        cost_estimate=cost(0, 4 << 20),
        name="query_prep",
    )(q_raw, gain, cosine, sine)


def d_attn_kernel(me_ref, p0, p1, p2, p3, w_ref, out_ref, acc):
    k = pl.program_id(0)
    for i, piece in enumerate((p0, p1, p2, p3)):

        @pl.when(k == i)
        def _(i=i, piece=piece):
            term = lax.dot_general(piece[...], w_ref[...], (((1,), (1,)), ((), ())), preferred_element_type=jnp.float32)
            if i == 0:
                acc[...] = term
            elif i < 3:
                acc[...] += term
            else:
                out_ref[...] = (acc[...] + term).astype(jnp.bfloat16)


def d_attn_product(me, pieces, w_out):
    tok, width = pieces[0].shape
    feats = w_out.shape[0]
    whole = lambda k, me: (0, 0)
    return pl.pallas_call(
        d_attn_kernel,
        grid_spec=pltpu.PrefetchScalarGridSpec(
            num_scalar_prefetch=1,
            grid=(4,),
            in_specs=[pl.BlockSpec((tok, width), whole)] * 4
            + [pl.BlockSpec((feats, width), lambda k, me: (0, me[0] ^ k))],
            out_specs=pl.BlockSpec((tok, feats), whole),
            scratch_shapes=[pltpu.VMEM((tok, feats), jnp.float32)],
        ),
        out_shape=shape((tok, feats), jnp.bfloat16),
        compiler_params=params(),
        cost_estimate=cost(2 * tok * feats * width * 4, 12 << 20),
        name="d_attn_product",
    )(me, *pieces, w_out)


def out_kernel(me_ref, a0_ref, a1_ref, w_ref, send_ref, keep_ref):
    k = pl.program_id(0)
    half = a0_ref.shape[1]
    term = jnp.dot(a0_ref[...], w_ref[0:half, :], preferred_element_type=jnp.float32)
    term += jnp.dot(a1_ref[...], w_ref[half:, :], preferred_element_type=jnp.float32)

    @pl.when(k < 2)
    def _():
        send_ref[pl.ds(k, 1)] = term.astype(jnp.bfloat16)[None]

    @pl.when(k >= 2)
    def _():
        keep_ref[pl.ds(k - 2, 1)] = term.astype(jnp.bfloat16)[None]


def out_product(me, a0, a1, w_out):
    tok = a0.shape[0]
    feats, wide = w_out.shape
    width = wide // 4
    whole = lambda k, me: (0, 0)
    pair = lambda k, me: (0, 0, 0)
    return pl.pallas_call(
        out_kernel,
        grid_spec=pltpu.PrefetchScalarGridSpec(
            num_scalar_prefetch=1,
            grid=(4,),
            in_specs=[pl.BlockSpec(a0.shape, whole)] * 2
            + [pl.BlockSpec((feats, width), lambda k, me: (0, me[0] ^ (2 * (k % 2) + 1 - k // 2)))],
            out_specs=[pl.BlockSpec((2, tok, width), pair)] * 2,
        ),
        out_shape=[shape((2, tok, width), jnp.bfloat16)] * 2,
        compiler_params=params(),
        cost_estimate=cost(2 * tok * feats * wide, 12 << 20),
        name="out_product",
    )(me, a0, a1, w_out)


def attention_kernel(
    tags_ref, own_ref, q_ref, do_ref, p0, p1, p2, p3, attn_ref, dq_ref, d0, d1, d2, d3,
    ks, vs, kt, vt, dk, dv, st, *, first, nclean, own_blocks, group,
):
    temp = 2 * nclean
    rows = group * BLK
    for i, piece in enumerate((p0, p1, p2, p3)):
        for b in range(piece.shape[0] // BLK):
            tag = tags_ref[i * (piece.shape[0] // BLK) + b]
            ks[tag] = piece[b * BLK : (b + 1) * BLK, 0:HEAD]
            vs[tag] = piece[b * BLK : (b + 1) * BLK, HEAD:]

    def flip(x):
        return x.astype(jnp.float32).T.astype(jnp.bfloat16)

    def chunk(ref, start):
        return ref[pl.ds(start, 4)].reshape(4 * BLK, HEAD)

    for c in range(nclean // 4):
        kt[c] = flip(chunk(ks, nclean + 4 * c))
        vt[c] = flip(chunk(vs, nclean + 4 * c))
    dk[...] = jnp.zeros_like(dk)
    dv[...] = jnp.zeros_like(dv)

    def gather(ref, j):
        return jnp.concatenate(
            [ref[pl.ds(j * BLK, BLK), (first + h) * HEAD : (first + h + 1) * HEAD] for h in range(group)], axis=0
        )

    def one_block(j, unused):
        own = own_ref[j]
        noisy = own < nclean
        index = own % nclean
        last = index // 4
        place = index % 4
        sources = []
        for s in range(4):
            clean = nclean + 4 * last + s
            sources.append(jnp.where(jnp.logical_and(noisy, place == s), own, clean))
        for s in range(4):
            ks[temp + s] = ks[sources[s]]
            vs[temp + s] = vs[sources[s]]
            dk[temp + s] = jnp.zeros((BLK, HEAD), jnp.float32)
            dv[temp + s] = jnp.zeros((BLK, HEAD), jnp.float32)
        kt[nclean // 4] = flip(chunk(ks, temp))
        vt[nclean // 4] = flip(chunk(vs, temp))
        q = gather(q_ref, j)
        do = gather(do_ref, j)
        dot_t = do.astype(jnp.float32).T

        def where_of(c):
            final = c == last
            return jnp.where(final, temp, nclean + 4 * c), jnp.where(final, nclean // 4, c)

        def score(c, top):
            start, unused_index = where_of(c)
            s = lax.dot_general(chunk(ks, start), q, (((1,), (1,)), ((), ())), preferred_element_type=jnp.float32)
            for i in range(4):
                hidden = jnp.logical_and(c == last, i > place)
                part = s[i * BLK : (i + 1) * BLK] * SCALE + jnp.where(hidden, NEG, 0.0).astype(jnp.float32)
                st[c, i * BLK : (i + 1) * BLK, :] = part
                top = jnp.maximum(top, jnp.max(part.reshape(BLK // 8, 8, rows), axis=0))
            return top

        top = lax.fori_loop(0, last + 1, score, jnp.full((8, rows), NEG, jnp.float32))
        top = jnp.max(top, axis=0, keepdims=True)

        def weigh(c, carry):
            total, acc = carry
            unused_start, t_index = where_of(c)
            e = jnp.exp(st[c] - top)
            st[c] = e
            total = total + jnp.sum(e.reshape(4 * BLK // 8, 8, rows), axis=0)
            acc = acc + jnp.dot(vt[t_index], e.astype(jnp.bfloat16), preferred_element_type=jnp.float32)
            return total, acc

        total, acc = lax.fori_loop(
            0, last + 1, weigh, (jnp.zeros((8, rows), jnp.float32), jnp.zeros((HEAD, rows), jnp.float32))
        )
        total = jnp.sum(total, axis=0, keepdims=True)
        inv = 1.0 / total
        attn_t = (acc / total).astype(jnp.bfloat16).astype(jnp.float32)
        delta = jnp.sum(dot_t * attn_t, axis=0, keepdims=True)
        attn = attn_t.T.astype(jnp.bfloat16)
        for h in range(group):
            attn_ref[pl.ds(j * BLK, BLK), h * HEAD : (h + 1) * HEAD] = attn[h * BLK : (h + 1) * BLK]

        def back(c, acc):
            start, t_index = where_of(c)
            p = st[c] * inv
            dp = lax.dot_general(chunk(vs, start), do, (((1,), (1,)), ((), ())), preferred_element_type=jnp.float32)
            ds = (p * (dp - delta)).astype(jnp.bfloat16)
            dvc = jnp.dot(p.astype(jnp.bfloat16), do, preferred_element_type=jnp.float32)
            dkc = jnp.dot(ds, q, preferred_element_type=jnp.float32)
            dv[pl.ds(start, 4)] += dvc.reshape(4, BLK, HEAD)
            dk[pl.ds(start, 4)] += dkc.reshape(4, BLK, HEAD)
            return acc + jnp.dot(kt[t_index], ds, preferred_element_type=jnp.float32)

        acc = lax.fori_loop(0, last + 1, back, jnp.zeros((HEAD, rows), jnp.float32))
        dq = (acc * SCALE).T
        for h in range(group):
            dq_ref[pl.ds(j * BLK, BLK), h * HEAD : (h + 1) * HEAD] = dq[h * BLK : (h + 1) * BLK]
        for s in range(4):
            dk[sources[s]] += dk[temp + s]
            dv[sources[s]] += dv[temp + s]
        return unused

    lax.fori_loop(0, own_blocks, one_block, 0)
    for i, out in enumerate((d0, d1, d2, d3)):
        for b in range(out.shape[0] // BLK):
            tag = tags_ref[i * (out.shape[0] // BLK) + b]
            out[b * BLK : (b + 1) * BLK, 0:HEAD] = (dk[tag] * SCALE).astype(jnp.bfloat16)
            out[b * BLK : (b + 1) * BLK, HEAD:] = dv[tag].astype(jnp.bfloat16)


def attention(tags, own_tags, q, do, pieces, g, group):
    tok = q.shape[0]
    nclean = tags.shape[0] // 2
    rows = group * BLK
    chunks = nclean // 4 + 1
    blocks = 2 * nclean + 4
    return pl.pallas_call(
        functools.partial(
            attention_kernel, first=g * group, nclean=nclean, own_blocks=tok // BLK, group=group
        ),
        in_specs=[SMEM, SMEM] + [VMEM] * 6,
        out_specs=[VMEM] * 6,
        out_shape=[shape((tok, group * HEAD), jnp.bfloat16), shape((tok, group * HEAD), jnp.float32)]
        + [shape(pieces[0].shape, jnp.bfloat16)] * 4,
        scratch_shapes=[
            pltpu.VMEM((blocks, BLK, HEAD), jnp.bfloat16),
            pltpu.VMEM((blocks, BLK, HEAD), jnp.bfloat16),
            pltpu.VMEM((chunks, HEAD, 4 * BLK), jnp.bfloat16),
            pltpu.VMEM((chunks, HEAD, 4 * BLK), jnp.bfloat16),
            pltpu.VMEM((blocks, BLK, HEAD), jnp.float32),
            pltpu.VMEM((blocks, BLK, HEAD), jnp.float32),
            pltpu.VMEM((chunks - 1, 4 * BLK, rows), jnp.float32),
        ],
        compiler_params=params(),
        cost_estimate=cost(6 << 30, 4 << 20),
        name="attention",
    )(tags, own_tags, q, do, *pieces)


def query_back_kernel(q_ref, a_ref, b_ref, gain_ref, cos_ref, sin_ref, out_ref):
    gain, cosine, sine = gain_ref[...], cos_ref[...], sin_ref[...]
    heads = a_ref.shape[1] // HEAD
    for h in range(2 * heads):
        cols = slice(h * HEAD, (h + 1) * HEAD)
        source = (a_ref, b_ref)[h // heads]
        dy = source[:, (h % heads) * HEAD : (h % heads + 1) * HEAD]
        out_ref[:, cols] = norm_rope_back(q_ref[:, cols].astype(jnp.float32), dy, gain, cosine, sine)


def query_back(q_raw, dq0, dq1, gain, cosine, sine):
    return pl.pallas_call(
        query_back_kernel,
        in_specs=[VMEM] * 6,
        out_specs=VMEM,
        out_shape=shape(q_raw.shape, jnp.float32),
        compiler_params=params(),
        cost_estimate=cost(0, 8 << 20),
        name="query_back",
    )(q_raw, dq0, dq1, gain, cosine, sine)


def key_back_kernel(key_ref, gain_ref, cos_ref, sin_ref, *refs):
    parts, (dk_ref, dv_ref) = refs[:-2], refs[-2:]
    gain, cosine, sine = gain_ref[...], cos_ref[...], sin_ref[...]
    for g in range(2):
        total = sum(part[...].astype(jnp.float32) for part in parts[4 * g : 4 * g + 4])
        cols = slice(g * HEAD, (g + 1) * HEAD)
        dk_ref[:, cols] = norm_rope_back(
            key_ref[:, cols].astype(jnp.float32), total[:, 0:HEAD], gain, cosine, sine
        )
        dv_ref[:, cols] = total[:, HEAD:]


def key_back(keys, gain, cosine, sine, parts0, parts1):
    return pl.pallas_call(
        key_back_kernel,
        in_specs=[VMEM] * 12,
        out_specs=[VMEM] * 2,
        out_shape=[shape(keys.shape, jnp.float32)] * 2,
        compiler_params=params(),
        cost_estimate=cost(0, 2 << 20),
        name="key_back",
    )(keys, gain, cosine, sine, *parts0, *parts1)


def fold_kernel(a, b, c, d, *outs):
    rows = outs[0].shape[0]
    for i, out in enumerate(outs):
        part = slice(i * rows, (i + 1) * rows)
        total = a[part, :].astype(jnp.float32) + b[part, :].astype(jnp.float32)
        total += c[part, :].astype(jnp.float32) + d[part, :].astype(jnp.float32)
        out[...] = total.astype(jnp.bfloat16)


def fold(parts):
    rows, width = parts[0].shape
    return pl.pallas_call(
        fold_kernel,
        in_specs=[VMEM] * 4,
        out_specs=[VMEM] * SIDE,
        out_shape=[shape((rows // SIDE, width), jnp.bfloat16)] * SIDE,
        compiler_params=params(),
        cost_estimate=cost(0, 4 << 20),
        name="fold",
    )(*parts)


def torus(value, dx, dy):
    pairs = [
        (y * SIDE + x, ((y + dy) % SIDE) * SIDE + (x + dx) % SIDE) for y in range(SIDE) for x in range(SIDE)
    ]
    return lax.ppermute(value, "ctx", pairs)


def along(value, axis, steps):
    return torus(value, steps, 0) if axis == 0 else torus(value, 0, steps)


def across(value, mask):
    return lax.ppermute(value, "ffn", [(s, s ^ mask) for s in range(4)])


def spread(value, axis):
    return [value] + [along(value, axis, k) for k in range(1, SIDE)]


def per_device(q_raw, keys, values, q_gain, k_gain, block_tags, w_out, d_out):
    tok = q_raw.shape[0]
    own_blocks = tok // BLK
    nclean = block_tags.shape[0] // 2
    here = lax.axis_index("ctx")
    x, y = here % SIDE, here // SIDE
    me = lax.axis_index("ffn").astype(jnp.int32)[None]
    heads = keys.shape[1] // HEAD
    group = q_raw.shape[1] // keys.shape[1]
    q_gain, k_gain = q_gain[None, :], k_gain[None, :]
    table = jnp.asarray(angle_table(nclean))
    grid_tags = block_tags.reshape(SIDE, SIDE, own_blocks)
    steps = jnp.arange(SIDE)
    relative = grid_tags[(y - steps) % SIDE][:, (x - steps) % SIDE]
    own_tags = relative[0, 0]
    tag_lists = (relative.reshape(-1), relative.transpose(1, 0, 2).reshape(-1))

    *kv, cosine, sine = key_prep(own_tags, keys, values, k_gain, table, heads)
    near = [spread(kv[g], g) for g in range(2)]
    lines = [jnp.concatenate(n, axis=0) for n in near]
    pieces = [spread(lines[g], 1 - g) for g in range(2)]

    far = across(d_out, 2)
    d_pieces = [d_out, across(d_out, 1), far, across(far, 1)]
    q = query_prep(q_raw, q_gain, cosine, sine)
    do = d_attn_product(me, d_pieces, w_out)

    results = [attention(tag_lists[g], own_tags, q, do, pieces[g], g, group) for g in range(2)]
    attn = [r[0] for r in results]
    dq = [r[1] for r in results]
    back = []
    for g in range(2):
        out = results[g][2:]
        got = [out[0]] + [along(out[k], 1 - g, -k) for k in range(1, SIDE)]
        shares = fold(got)
        back.append([shares[0]] + [along(shares[k], g, -k) for k in range(1, SIDE)])

    send, keep = out_product(me, attn[0], attn[1], w_out)
    summed = keep.astype(jnp.float32) + across(send, 1).astype(jnp.float32)
    other = across(summed[1].astype(jnp.bfloat16), 2)
    attn_out = (summed[0] + other.astype(jnp.float32)).astype(jnp.bfloat16)
    d_q = query_back(q_raw, dq[0], dq[1], q_gain, cosine, sine)
    key_gradient, value_gradient = key_back(keys, k_gain, cosine, sine, back[0], back[1])
    return attn_out, d_q, key_gradient, value_gradient


def solution(mesh):
    split = P(("dp", "ctx"), "ffn")
    return jax.shard_map(
        per_device,
        mesh=mesh,
        in_specs=(split, split, split, P(), P(), P("dp"), P("ffn", None), split),
        out_specs=(split,) * 4,
        check_vma=False,
    )
```

time: 700 us -> 163 us (0.23)
  the two profiles are of different devices: /device:TPU:96 before, /device:TPU:72 now
where the time goes in v1:
time: 163 us; the launch traced here: 161 us
  Pallas kernels  68 us (42%)
  waiting for transfers between devices  46.4 us (28%)
  starting transfers between devices  33.6 us (21%)
  local copies, waits for them, and re-layouts  10.6 us (7%)
    pallas_call x2, Pallas kernels, attention(): pl.pallas_call(functools.partial(attention_kernel, first=g * group, nclea...  50.6 us
    ppermute x24, waiting for transfers between devices, torus(): return lax.ppermute(value, 'ctx', pairs)  45.9 us
    ppermute x24, starting transfers between devices, torus(): return lax.ppermute(value, 'ctx', pairs)  31.4 us
    unnamed x30, local copies, waits for them, and re-layouts  5.71 us
    pallas_call x1, Pallas kernels, out_product(): pl.pallas_call(out_kernel, grid_spec=pltpu.PrefetchScalarGridSpec(num_sca...  5.71 us
    pallas_call x1, Pallas kernels, d_attn_product(): pl.pallas_call(d_attn_kernel, grid_spec=pltpu.PrefetchScalarGridSpec(num_...  5.64 us
  transfers between devices with their start and end apart: 29, of which 12 were waited for; matrix products, arithmetic and copies ran while one was open for 3% of the time, Pallas kernels for 23%

profile of v1, /device:TPU:72, one launch (start us, length us, event | category | flops | bytes accessed | tf_op | source)
XLA Modules:
  0.0 161.0 jit_solution(13975465898754848419)
XLA Ops:
  0.6 1.7 %collective-permute-start.1 = (bf16[256,1024]{1,0:T(8,128)(2,1)}, bf16[256,1024]{1,0:T(8,128)(2,1)S(1)}, u32[]{:S(2)}, u32[]{:S(2)}) collective-permute-start(bf16[256,1024]{1,0:T(8,128)(2,1)} %p0.1), channel_id=1, source_target_pairs={{0,4},{2,6},{4,0},{6,2},{1,5},{3,7},{5,1},{7,3},{8,12},{10,14},{12... | collective-permute-start | bytes 1572872 | tf_op jit(solution)/shard_map/ppermute | solution.py:414
  8.3 1.1 key_prep.1
  9.3 1.6 %collective-permute-start.9 = (bf16[256,256]{1,0:T(8,128)(2,1)S(1)}, bf16[256,256]{1,0:T(8,128)(2,1)S(1)}, u32[]{:S(2)}, u32[]{:S(2)}) collective-permute-start(bf16[256,256]{1,0:T(8,128)(2,1)S(1)} %get-tuple-element.36), channel_id=1, source_target_pairs={{0,32},{8,40},{16,48},{24,56},{32,64},{40,72},{48,80},{56,88},{64,... | collective-permute-start | bytes 393224 | tf_op jit(solution)/shard_map/ppermute | solution.py:406
  11.0 0.9 collective-permute-start.10
  11.9 2.4 %collective-permute-start.11 = (bf16[256,256]{1,0:T(8,128)(2,1)S(1)}, bf16[256,256]{1,0:T(8,128)(2,1)S(1)}, u32[]{:S(2)}, u32[]{:S(2)}) collective-permute-start(bf16[256,256]{1,0:T(8,128)(2,1)S(1)} %get-tuple-element.36), channel_id=1, source_target_pairs={{0,96},{8,104},{16,112},{24,120},{32,0},{40,8},{48,16},{56,24},{64... | collective-permute-start | bytes 393224 | tf_op jit(solution)/shard_map/ppermute | solution.py:406
  15.2 1.3 copy.16
  17.3 1.0 copy-done
  19.0 1.1 query_prep.1.q_ref
  20.1 1.6 collective-permute-start.3
  21.7 2.8 %collective-permute-start.4 = (bf16[256,256]{1,0:T(8,128)(2,1)S(1)}, bf16[256,256]{1,0:T(8,128)(2,1)S(1)}, u32[]{:S(2)}, u32[]{:S(2)}) collective-permute-start(bf16[256,256]{1,0:T(8,128)(2,1)S(1)} %get-tuple-element.34), channel_id=1, source_target_pairs={{0,16},{8,24},{16,0},{24,8},{32,48},{40,56},{48,32},{56,40},{64,80... | collective-permute-start | bytes 393224 | tf_op jit(solution)/shard_map/ppermute | solution.py:406
  24.5 1.4 collective-permute-start.5
  26.0 1.3 collective-permute-done.3
  27.8 3.7 %collective-permute-done.4 = bf16[256,256]{1,0:T(8,128)(2,1)S(1)} collective-permute-done((bf16[256,256]{1,0:T(8,128)(2,1)S(1)}, bf16[256,256]{1,0:T(8,128)(2,1)S(1)}, u32[]{:S(2)}, u32[]{:S(2)}) %collective-permute-start.4) | collective-permute-done | bytes 131104 | tf_op jit(solution)/shard_map/ppermute | solution.py:406
  32.3 1.5 collective-permute-start.14
  34.0 3.4 %collective-permute-start.7 = (bf16[1024,256]{1,0:T(8,128)(2,1)S(1)}, bf16[1024,256]{1,0:T(8,128)(2,1)S(1)}, u32[]{:S(2)}, u32[]{:S(2)}) collective-permute-start(bf16[1024,256]{1,0:T(8,128)(2,1)S(1)} %constant_dynamic-update-slice_fusion.p0), channel_id=1, source_target_pairs={{0,64},{8,72},{16,80},{24,88},{32,96},{40,104},{48,112},{56,120},{... | collective-permute-start | bytes 1572872 | tf_op jit(solution)/shard_map/ppermute | solution.py:406
  37.4 5.6 %d_attn_product.1.do_ref = bf16[256,1024]{1,0:T(8,128)(2,1)S(1)} custom-call(s32[1]{0:T(128)} %bitcast.me_ref, bf16[256,1024]{1,0:T(8,128)(2,1)S(1)} %copy-done.2, bf16[256,1024]{1,0:T(8,128)(2,1)S(1)} %collective-permute-done.p1, bf16[256,1024]{1,0:T(8,128)(2,1)S(1)} %collective-permute-done.1.p2, bf16[256,1024]{1,0:T(8,128)(2,1)S(1)} %collective-permute-done.2.p3, ...), custom_call_target="tpu_custom_call" | custom-call | flops 2147483648 | bytes 12582912 | tf_op jit(solution)/shard_map/d_attn_product/pallas_call | solution.py:136
  43.6 1.3 collective-permute-start.8
  45.0 8.7 %collective-permute-done.13.p2 = bf16[1024,256]{1,0:T(8,128)(2,1)S(1)} collective-permute-done((bf16[1024,256]{1,0:T(8,128)(2,1)S(1)}, bf16[1024,256]{1,0:T(8,128)(2,1)S(1)}, u32[]{:S(2)}, u32[]{:S(2)}) %collective-permute-start.13) | collective-permute-done | bytes 524320 | tf_op jit(solution)/shard_map/ppermute | solution.py:406
  54.0 25.3 %attention.3 = (bf16[256,512]{1,0:T(8,128)(2,1)S(1)}, f32[256,512]{1,0:T(8,128)S(1)}, bf16[1024,256]{1,0:T(8,128)(2,1)S(1)}, bf16[1024,256]{1,0:T(8,128)(2,1)S(1...) custom-call(s32[64]{0:T(128)S(1)} %reshape.118.tags_ref, s32[4]{0:T(128)S(1)} %slice_bitcast_fusion.1.tags_ref.own_ref, ...), custom_call_target="tpu_custom_call" | custom-call | flops 6442450944 | bytes 4194304 | tf_op jit(solution)/shard_map/attention/pallas_call | solution.py:311
  79.3 25.3 %attention.2 = (bf16[256,512]{1,0:T(8,128)(2,1)S(1)}, f32[256,512]{1,0:T(8,128)S(1)}, bf16[1024,256]{1,0:T(8,128)(2,1)S(1)}, bf16[1024,256]{1,0:T(8,128)(2,1)S(1...) custom-call(s32[64]{0:T(128)S(1)} %reshape.117.tags_ref, s32[4]{0:T(128)S(1)} %slice_bitcast_fusion.1.tags_ref.own_ref, ...), custom_call_target="tpu_custom_call" | custom-call | flops 6442450944 | bytes 4194304 | tf_op jit(solution)/shard_map/attention/pallas_call | solution.py:311
  104.6 5.7 %out_product.1 = (bf16[2,256,1024]{2,1,0:T(8,128)(2,1)S(1)}, bf16[2,256,1024]{2,1,0:T(8,128)(2,1)S(1)}) custom-call(s32[1]{0:T(128)} %bitcast.me_ref, bf16[256,512]{1,0:T(8,128)(2,1)S(1)} %get-tuple-element.35.a0_ref, bf16[256,512]{1,0:T(8,128)(2,1)S(1)} %get-tuple-element.37.a1_ref, bf16[1024,4096]{1,0:T(8,128)(2,1)} %w_ref.3), custom_call_target="tpu_custom_call" | custom-call | flops 2147483648 | bytes 12582912 | tf_op jit(solution)/shard_map/out_product/pallas_call | solution.py:174
  110.5 1.5 collective-permute-start.24
  113.5 11.8 %collective-permute-done.23.b = bf16[1024,256]{1,0:T(8,128)(2,1)S(1)} collective-permute-done((bf16[1024,256]{1,0:T(8,128)(2,1)S(1)}, bf16[1024,256]{1,0:T(8,128)(2,1)S(1)}, u32[]{:S(2)}, u32[]{:S(2)}) %collective-permute-start.23) | collective-permute-done | bytes 524320 | tf_op jit(solution)/shard_map/ppermute | solution.py:406
  125.3 1.6 collective-permute-done.24.c
  127.3 10.2 %collective-permute-done.25.d = bf16[1024,256]{1,0:T(8,128)(2,1)S(1)} collective-permute-done((bf16[1024,256]{1,0:T(8,128)(2,1)S(1)}, bf16[1024,256]{1,0:T(8,128)(2,1)S(1)}, u32[]{:S(2)}, u32[]{:S(2)}) %collective-permute-start.25) | collective-permute-done | bytes 524320 | tf_op jit(solution)/shard_map/ppermute | solution.py:406
  138.0 2.0 %collective-permute-start.28 = (bf16[256,256]{1,0:T(8,128)(2,1)S(1)}, bf16[256,256]{1,0:T(8,128)(2,1)S(1)}, u32[]{:S(2)}, u32[]{:S(2)}) collective-permute-start(bf16[256,256]{1,0:T(8,128)(2,1)S(1)} %get-tuple-element.57), channel_id=1, source_target_pairs={{0,32},{8,40},{16,48},{24,56},{32,64},{40,72},{48,80},{56,88},{64,... | collective-permute-start | bytes 393224 | tf_op jit(solution)/shard_map/ppermute | solution.py:406
  140.2 2.1 %collective-permute-start.20 = (bf16[256,256]{1,0:T(8,128)(2,1)S(1)}, bf16[256,256]{1,0:T(8,128)(2,1)S(1)}, u32[]{:S(2)}, u32[]{:S(2)}) collective-permute-start(bf16[256,256]{1,0:T(8,128)(2,1)S(1)} %get-tuple-element.47), channel_id=1, source_target_pairs={{0,24},{8,0},{16,8},{24,16},{32,56},{40,32},{48,40},{56,48},{64,88... | collective-permute-start | bytes 393224 | tf_op jit(solution)/shard_map/ppermute | solution.py:406
  142.3 3.8 %collective-permute-done.26.refs_5_ = bf16[256,256]{1,0:T(8,128)(2,1)S(1)} collective-permute-done((bf16[256,256]{1,0:T(8,128)(2,1)S(1)}, bf16[256,256]{1,0:T(8,128)(2,1)S(1)}, u32[]{:S(2)}, u32[]{:S(2)}) %collective-permute-start.26) | collective-permute-done | bytes 131104 | tf_op jit(solution)/shard_map/ppermute | solution.py:406
  146.1 6.6 %collective-permute-start.21 = (bf16[256,256]{1,0:T(8,128)(2,1)S(1)}, bf16[256,256]{1,0:T(8,128)(2,1)S(1)}, u32[]{:S(2)}, u32[]{:S(2)}) collective-permute-start(bf16[256,256]{1,0:T(8,128)(2,1)S(1)} %get-tuple-element.48), channel_id=1, source_target_pairs={{0,16},{8,24},{16,0},{24,8},{32,48},{40,56},{48,32},{56,40},{64,80... | collective-permute-start | bytes 393224 | tf_op jit(solution)/shard_map/ppermute | solution.py:406
  152.7 2.2 %query_back.1 = f32[256,1024]{1,0:T(8,128)} custom-call(bf16[256,1024]{1,0:T(8,128)(2,1)S(1)} %copy-done.1, f32[256,512]{1,0:T(8,128)S(1)} %get-tuple-element.40.a_ref, f32[256,512]{1,0:T(8,128)S(1)} %get-tuple-element.41.b_ref, f32[1,128]{1,0:T(1,128)S(1)} %bitcast.19, f32[256,128]{1,0:T(8,128)S(1)} %get-tuple-element.32.cos_ref, ...), custom_call_target="tpu_custom_call" | custom-call | bytes 8388608 | tf_op jit(solution)/shard_map/query_back/pallas_call | solution.py:345
  155.7 3.1 %collective-permute-done.22.refs_3_ = bf16[256,256]{1,0:T(8,128)(2,1)S(1)} collective-permute-done((bf16[256,256]{1,0:T(8,128)(2,1)S(1)}, bf16[256,256]{1,0:T(8,128)(2,1)S(1)}, u32[]{:S(2)}, u32[]{:S(2)}) %collective-permute-start.22) | collective-permute-done | bytes 131104 | tf_op jit(solution)/shard_map/ppermute | solution.py:406
  158.9 1.1 key_back.1
  (82 shorter events, 15.1 us)
Async XLA Ops:
  0.6 36.8 %copy-start.2 = (bf16[256,1024]{1,0:T(8,128)(2,1)S(1)}, bf16[256,1024]{1,0:T(8,128)(2,1)}, u32[]{:S(2)}) copy-start(bf16[256,1024]{1,0:T(8,128)(2,1)} %p0.1) | copy-start | bytes 1572868
  0.6 25.3 %collective-permute-start.1 = (bf16[256,1024]{1,0:T(8,128)(2,1)}, bf16[256,1024]{1,0:T(8,128)(2,1)S(1)}, u32[]{:S(2)}, u32[]{:S(2)}) collective-permute-start(bf16[256,1024]{1,0:T(8,128)(2,1)} %p0.1), channel_id=1, source_target_pairs={{0,4},{2,6},{4,0},{6,2},{1,5},{3,7},{5,1},{7,3},{8,12},{10,14},{12... | collective-permute-start | bytes 1572872 | tf_op jit(solution)/shard_map/ppermute | solution.py:414
  9.3 10.8 %collective-permute-start.9 = (bf16[256,256]{1,0:T(8,128)(2,1)S(1)}, bf16[256,256]{1,0:T(8,128)(2,1)S(1)}, u32[]{:S(2)}, u32[]{:S(2)}) collective-permute-start(bf16[256,256]{1,0:T(8,128)(2,1)S(1)} %get-tuple-element.36), channel_id=1, source_target_pairs={{0,32},{8,40},{16,48},{24,56},{32,64},{40,72},{48,80},{56,88},{64,... | collective-permute-start | bytes 393224 | tf_op jit(solution)/shard_map/ppermute | solution.py:406
  11.0 10.7 %collective-permute-start.10 = (bf16[256,256]{1,0:T(8,128)(2,1)S(1)}, bf16[256,256]{1,0:T(8,128)(2,1)S(1)}, u32[]{:S(2)}, u32[]{:S(2)}) collective-permute-start(bf16[256,256]{1,0:T(8,128)(2,1)S(1)} %get-tuple-element.36), channel_id=1, source_target_pairs={{0,64},{8,72},{16,80},{24,88},{32,96},{40,104},{48,112},{56,120},{... | collective-permute-start | bytes 393224 | tf_op jit(solution)/shard_map/ppermute | solution.py:406
  11.9 12.6 %collective-permute-start.11 = (bf16[256,256]{1,0:T(8,128)(2,1)S(1)}, bf16[256,256]{1,0:T(8,128)(2,1)S(1)}, u32[]{:S(2)}, u32[]{:S(2)}) collective-permute-start(bf16[256,256]{1,0:T(8,128)(2,1)S(1)} %get-tuple-element.36), channel_id=1, source_target_pairs={{0,96},{8,104},{16,112},{24,120},{32,0},{40,8},{48,16},{56,24},{64... | collective-permute-start | bytes 393224 | tf_op jit(solution)/shard_map/ppermute | solution.py:406
  14.3 19.5 %collective-permute-start = (bf16[256,1024]{1,0:T(8,128)(2,1)}, bf16[256,1024]{1,0:T(8,128)(2,1)S(1)}, u32[]{:S(2)}, u32[]{:S(2)}) collective-permute-start(bf16[256,1024]{1,0:T(8,128)(2,1)} %p0.1), channel_id=1, source_target_pairs={{0,2},{2,0},{4,6},{6,4},{1,3},{3,1},{5,7},{7,5},{8,10},{10,8},{12,... | collective-permute-start | bytes 1572872 | tf_op jit(solution)/shard_map/ppermute | solution.py:414
  20.1 7.2 %collective-permute-start.3 = (bf16[256,256]{1,0:T(8,128)(2,1)S(1)}, bf16[256,256]{1,0:T(8,128)(2,1)S(1)}, u32[]{:S(2)}, u32[]{:S(2)}) collective-permute-start(bf16[256,256]{1,0:T(8,128)(2,1)S(1)} %get-tuple-element.34), channel_id=1, source_target_pairs={{0,8},{8,16},{16,24},{24,0},{32,40},{40,48},{48,56},{56,32},{64,72... | collective-permute-start | bytes 393224 | tf_op jit(solution)/shard_map/ppermute | solution.py:406
  21.7 9.8 %collective-permute-start.4 = (bf16[256,256]{1,0:T(8,128)(2,1)S(1)}, bf16[256,256]{1,0:T(8,128)(2,1)S(1)}, u32[]{:S(2)}, u32[]{:S(2)}) collective-permute-start(bf16[256,256]{1,0:T(8,128)(2,1)S(1)} %get-tuple-element.34), channel_id=1, source_target_pairs={{0,16},{8,24},{16,0},{24,8},{32,48},{40,56},{48,32},{56,40},{64,80... | collective-permute-start | bytes 393224 | tf_op jit(solution)/shard_map/ppermute | solution.py:406
  24.5 7.8 %collective-permute-start.5 = (bf16[256,256]{1,0:T(8,128)(2,1)S(1)}, bf16[256,256]{1,0:T(8,128)(2,1)S(1)}, u32[]{:S(2)}, u32[]{:S(2)}) collective-permute-start(bf16[256,256]{1,0:T(8,128)(2,1)S(1)} %get-tuple-element.34), channel_id=1, source_target_pairs={{0,24},{8,0},{16,8},{24,16},{32,56},{40,32},{48,40},{56,48},{64,88... | collective-permute-start | bytes 393224 | tf_op jit(solution)/shard_map/ppermute | solution.py:406
  25.9 8.0 %collective-permute-start.2 = (bf16[256,1024]{1,0:T(8,128)(2,1)S(1)}, bf16[256,1024]{1,0:T(8,128)(2,1)S(1)}, u32[]{:S(2)}, u32[]{:S(2)}) collective-permute-start(bf16[256,1024]{1,0:T(8,128)(2,1)S(1)} %collective-permute-done.1.p2), channel_id=1, source_target_pairs={{0,2},{2,0},{4,6},{6,4},{1,3},{3,1},{5,7},{7,5},{8,10},{10,8},{12,... | collective-permute-start | bytes 1572872 | tf_op jit(solution)/shard_map/ppermute | solution.py:414
  27.3 16.3 %collective-permute-start.12 = (bf16[1024,256]{1,0:T(8,128)(2,1)S(1)}, bf16[1024,256]{1,0:T(8,128)(2,1)S(1)}, u32[]{:S(2)}, u32[]{:S(2)}) collective-permute-start(bf16[1024,256]{1,0:T(8,128)(2,1)S(1)} %constant_dynamic-update-slice_fusion.4.p0), channel_id=1, source_target_pairs={{0,8},{8,16},{16,24},{24,0},{32,40},{40,48},{48,56},{56,32},{64,72... | collective-permute-start | bytes 1572872 | tf_op jit(solution)/shard_map/ppermute | solution.py:406
  31.5 22.1 %collective-permute-start.13 = (bf16[1024,256]{1,0:T(8,128)(2,1)S(1)}, bf16[1024,256]{1,0:T(8,128)(2,1)S(1)}, u32[]{:S(2)}, u32[]{:S(2)}) collective-permute-start(bf16[1024,256]{1,0:T(8,128)(2,1)S(1)} %constant_dynamic-update-slice_fusion.4.p0), channel_id=1, source_target_pairs={{0,16},{8,24},{16,0},{24,8},{32,48},{40,56},{48,32},{56,40},{64,80... | collective-permute-start | bytes 1572872 | tf_op jit(solution)/shard_map/ppermute | solution.py:406
  32.3 21.7 %collective-permute-start.14 = (bf16[1024,256]{1,0:T(8,128)(2,1)S(1)}, bf16[1024,256]{1,0:T(8,128)(2,1)S(1)}, u32[]{:S(2)}, u32[]{:S(2)}) collective-permute-start(bf16[1024,256]{1,0:T(8,128)(2,1)S(1)} %constant_dynamic-update-slice_fusion.4.p0), channel_id=1, source_target_pairs={{0,24},{8,0},{16,8},{24,16},{32,56},{40,32},{48,40},{56,48},{64,88... | collective-permute-start | bytes 1572872 | tf_op jit(solution)/shard_map/ppermute | solution.py:406
  33.9 45.4 %collective-permute-start.6 = (bf16[1024,256]{1,0:T(8,128)(2,1)S(1)}, bf16[1024,256]{1,0:T(8,128)(2,1)S(1)}, u32[]{:S(2)}, u32[]{:S(2)}) collective-permute-start(bf16[1024,256]{1,0:T(8,128)(2,1)S(1)} %constant_dynamic-update-slice_fusion.p0), channel_id=1, source_target_pairs={{0,32},{8,40},{16,48},{24,56},{32,64},{40,72},{48,80},{56,88},{64,... | collective-permute-start | bytes 1572872 | tf_op jit(solution)/shard_map/ppermute | solution.py:406
  34.0 45.3 %collective-permute-start.7 = (bf16[1024,256]{1,0:T(8,128)(2,1)S(1)}, bf16[1024,256]{1,0:T(8,128)(2,1)S(1)}, u32[]{:S(2)}, u32[]{:S(2)}) collective-permute-start(bf16[1024,256]{1,0:T(8,128)(2,1)S(1)} %constant_dynamic-update-slice_fusion.p0), channel_id=1, source_target_pairs={{0,64},{8,72},{16,80},{24,88},{32,96},{40,104},{48,112},{56,120},{... | collective-permute-start | bytes 1572872 | tf_op jit(solution)/shard_map/ppermute | solution.py:406
  43.6 35.7 %collective-permute-start.8 = (bf16[1024,256]{1,0:T(8,128)(2,1)S(1)}, bf16[1024,256]{1,0:T(8,128)(2,1)S(1)}, u32[]{:S(2)}, u32[]{:S(2)}) collective-permute-start(bf16[1024,256]{1,0:T(8,128)(2,1)S(1)} %constant_dynamic-update-slice_fusion.p0), channel_id=1, source_target_pairs={{0,96},{8,104},{16,112},{24,120},{32,0},{40,8},{48,16},{56,24},{64... | collective-permute-start | bytes 1572872 | tf_op jit(solution)/shard_map/ppermute | solution.py:406
  110.3 2.7 %collective-permute-start.15 = (bf16[2,256,1024]{2,1,0:T(8,128)(2,1)S(1)}, bf16[2,256,1024]{2,1,0:T(8,128)(2,1)S(1)}, u32[]{:S(2)}, u32[]{:S(2)}) collective-permute-start(bf16[2,256,1024]{2,1,0:T(8,128)(2,1)S(1)} %get-tuple-element.39), channel_id=1, source_target_pairs={{0,2},{2,0},{4,6},{6,4},{1,3},{3,1},{5,7},{7,5},{8,10},{10,8},{12,... | collective-permute-start | bytes 3145736 | tf_op jit(solution)/shard_map/ppermute | solution.py:414
  110.4 14.8 %collective-permute-start.23 = (bf16[1024,256]{1,0:T(8,128)(2,1)S(1)}, bf16[1024,256]{1,0:T(8,128)(2,1)S(1)}, u32[]{:S(2)}, u32[]{:S(2)}) collective-permute-start(bf16[1024,256]{1,0:T(8,128)(2,1)S(1)} %get-tuple-element.51), channel_id=1, source_target_pairs={{0,24},{8,0},{16,8},{24,16},{32,56},{40,32},{48,40},{56,48},{64,88... | collective-permute-start | bytes 1572872 | tf_op jit(solution)/shard_map/ppermute | solution.py:406
  110.5 16.4 %collective-permute-start.24 = (bf16[1024,256]{1,0:T(8,128)(2,1)S(1)}, bf16[1024,256]{1,0:T(8,128)(2,1)S(1)}, u32[]{:S(2)}, u32[]{:S(2)}) collective-permute-start(bf16[1024,256]{1,0:T(8,128)(2,1)S(1)} %get-tuple-element.52), channel_id=1, source_target_pairs={{0,16},{8,24},{16,0},{24,8},{32,48},{40,56},{48,32},{56,40},{64,80... | collective-permute-start | bytes 1572872 | tf_op jit(solution)/shard_map/ppermute | solution.py:406
  112.0 25.5 %collective-permute-start.25 = (bf16[1024,256]{1,0:T(8,128)(2,1)S(1)}, bf16[1024,256]{1,0:T(8,128)(2,1)S(1)}, u32[]{:S(2)}, u32[]{:S(2)}) collective-permute-start(bf16[1024,256]{1,0:T(8,128)(2,1)S(1)} %get-tuple-element.53), channel_id=1, source_target_pairs={{0,8},{8,16},{16,24},{24,0},{32,40},{40,48},{48,56},{56,32},{64,72... | collective-permute-start | bytes 1572872 | tf_op jit(solution)/shard_map/ppermute | solution.py:406
  112.5 25.3 %collective-permute-start.17 = (bf16[1024,256]{1,0:T(8,128)(2,1)S(1)}, bf16[1024,256]{1,0:T(8,128)(2,1)S(1)}, u32[]{:S(2)}, u32[]{:S(2)}) collective-permute-start(bf16[1024,256]{1,0:T(8,128)(2,1)S(1)} %get-tuple-element.43), channel_id=1, source_target_pairs={{0,96},{8,104},{16,112},{24,120},{32,0},{40,8},{48,16},{56,24},{64... | collective-permute-start | bytes 1572872 | tf_op jit(solution)/shard_map/ppermute | solution.py:406
  113.1 24.9 %collective-permute-start.18 = (bf16[1024,256]{1,0:T(8,128)(2,1)S(1)}, bf16[1024,256]{1,0:T(8,128)(2,1)S(1)}, u32[]{:S(2)}, u32[]{:S(2)}) collective-permute-start(bf16[1024,256]{1,0:T(8,128)(2,1)S(1)} %get-tuple-element.44), channel_id=1, source_target_pairs={{0,64},{8,72},{16,80},{24,88},{32,96},{40,104},{48,112},{56,120},{... | collective-permute-start | bytes 1572872 | tf_op jit(solution)/shard_map/ppermute | solution.py:406
  125.2 14.7 %collective-permute-start.19 = (bf16[1024,256]{1,0:T(8,128)(2,1)S(1)}, bf16[1024,256]{1,0:T(8,128)(2,1)S(1)}, u32[]{:S(2)}, u32[]{:S(2)}) collective-permute-start(bf16[1024,256]{1,0:T(8,128)(2,1)S(1)} %get-tuple-element.45), channel_id=1, source_target_pairs={{0,32},{8,40},{16,48},{24,56},{32,64},{40,72},{48,80},{56,88},{64,... | collective-permute-start | bytes 1572872 | tf_op jit(solution)/shard_map/ppermute | solution.py:406
  126.9 33.1 %collective-permute-start.16 = (bf16[256,1024]{1,0:T(8,128)(2,1)S(1)}, bf16[256,1024]{1,0:T(8,128)(2,1)S(1)}, u32[]{:S(2)}, u32[]{:S(2)}) collective-permute-start(bf16[256,1024]{1,0:T(8,128)(2,1)S(1)} %fusion.2), channel_id=1, source_target_pairs={{0,4},{2,6},{4,0},{6,2},{1,5},{3,7},{5,1},{7,3},{8,12},{10,14},{12... | collective-permute-start | bytes 1572872 | tf_op jit(solution)/shard_map/ppermute | solution.py:414
  137.8 8.3 %collective-permute-start.26 = (bf16[256,256]{1,0:T(8,128)(2,1)S(1)}, bf16[256,256]{1,0:T(8,128)(2,1)S(1)}, u32[]{:S(2)}, u32[]{:S(2)}) collective-permute-start(bf16[256,256]{1,0:T(8,128)(2,1)S(1)} %get-tuple-element.55), channel_id=1, source_target_pairs={{0,96},{8,104},{16,112},{24,120},{32,0},{40,8},{48,16},{56,24},{64... | collective-permute-start | bytes 393224 | tf_op jit(solution)/shard_map/ppermute | solution.py:406
  137.9 14.8 %collective-permute-start.27 = (bf16[256,256]{1,0:T(8,128)(2,1)S(1)}, bf16[256,256]{1,0:T(8,128)(2,1)S(1)}, u32[]{:S(2)}, u32[]{:S(2)}) collective-permute-start(bf16[256,256]{1,0:T(8,128)(2,1)S(1)} %get-tuple-element.56), channel_id=1, source_target_pairs={{0,64},{8,72},{16,80},{24,88},{32,96},{40,104},{48,112},{56,120},{... | collective-permute-start | bytes 393224 | tf_op jit(solution)/shard_map/ppermute | solution.py:406
  138.0 17.0 %collective-permute-start.28 = (bf16[256,256]{1,0:T(8,128)(2,1)S(1)}, bf16[256,256]{1,0:T(8,128)(2,1)S(1)}, u32[]{:S(2)}, u32[]{:S(2)}) collective-permute-start(bf16[256,256]{1,0:T(8,128)(2,1)S(1)} %get-tuple-element.57), channel_id=1, source_target_pairs={{0,32},{8,40},{16,48},{24,56},{32,64},{40,72},{48,80},{56,88},{64,... | collective-permute-start | bytes 393224 | tf_op jit(solution)/shard_map/ppermute | solution.py:406
  140.0 18.9 %copy-start.4 = (bf16[256,256]{1,0:T(8,128)(2,1)S(1)}, bf16[256,256]{1,0:T(8,128)(2,1)}, u32[]{:S(2)}) copy-start(bf16[256,256]{1,0:T(8,128)(2,1)} %key_ref.3) | copy-start | bytes 393220
  140.0 18.9 %copy-start.10 = (f32[128]{0:T(128)S(1)}, f32[128]{0:T(128)}, u32[]{:S(2)}) copy-start(f32[128]{0:T(128)} %param.13) | copy-start | bytes 1540
  140.2 14.7 %collective-permute-start.20 = (bf16[256,256]{1,0:T(8,128)(2,1)S(1)}, bf16[256,256]{1,0:T(8,128)(2,1)S(1)}, u32[]{:S(2)}, u32[]{:S(2)}) collective-permute-start(bf16[256,256]{1,0:T(8,128)(2,1)S(1)} %get-tuple-element.47), channel_id=1, source_target_pairs={{0,24},{8,0},{16,8},{24,16},{32,56},{40,32},{48,40},{56,48},{64,88... | collective-permute-start | bytes 393224 | tf_op jit(solution)/shard_map/ppermute | solution.py:406
  146.1 9.6 %collective-permute-start.21 = (bf16[256,256]{1,0:T(8,128)(2,1)S(1)}, bf16[256,256]{1,0:T(8,128)(2,1)S(1)}, u32[]{:S(2)}, u32[]{:S(2)}) collective-permute-start(bf16[256,256]{1,0:T(8,128)(2,1)S(1)} %get-tuple-element.48), channel_id=1, source_target_pairs={{0,16},{8,24},{16,0},{24,8},{32,48},{40,56},{48,32},{56,40},{64,80... | collective-permute-start | bytes 393224 | tf_op jit(solution)/shard_map/ppermute | solution.py:406
  152.7 6.2 %collective-permute-start.22 = (bf16[256,256]{1,0:T(8,128)(2,1)S(1)}, bf16[256,256]{1,0:T(8,128)(2,1)S(1)}, u32[]{:S(2)}, u32[]{:S(2)}) collective-permute-start(bf16[256,256]{1,0:T(8,128)(2,1)S(1)} %get-tuple-element.49), channel_id=1, source_target_pairs={{0,8},{8,16},{16,24},{24,0},{32,40},{40,48},{48,56},{56,32},{64,72... | collective-permute-start | bytes 393224 | tf_op jit(solution)/shard_map/ppermute | solution.py:406
  (9 other events, 36.0 us)

commit v2 on v1

v2 whole, which is shorter than its diff:
```python
import functools

import jax
import jax.numpy as jnp
import numpy as np
from jax import lax
from jax.experimental import pallas as pl
from jax.experimental.pallas import tpu as pltpu
from jax.sharding import PartitionSpec as P

HEAD = 128
BLK = 64
ROPE_BASE = 1000000.0
EPS = 1e-06
NEG = -1e30
SCALE = HEAD ** (-0.5)
SCALE2 = SCALE * 1.4426950408889634
WIDE = 8
SIDE = 4
VMEM = pl.BlockSpec(memory_space=pltpu.VMEM)
SMEM = pl.BlockSpec(memory_space=pltpu.SMEM)
HBM = pl.BlockSpec(memory_space=pltpu.HBM)
LIMIT = 32 * 1024 * 1024


def shape(dims, dtype):
    return jax.ShapeDtypeStruct(dims, dtype)


def params():
    return pltpu.CompilerParams(vmem_limit_bytes=LIMIT)


def cost(flops, nbytes):
    return pl.CostEstimate(flops=flops, bytes_accessed=nbytes, transcendentals=0)


def angle_table(blocks):
    freq = ROPE_BASE ** (-(np.arange(HEAD // 2) * 2.0 / HEAD))
    freq = np.concatenate([freq, freq])[None, :]
    inner = np.arange(BLK)[:, None] * freq
    outer = (np.arange(blocks) * BLK)[:, None] * freq
    return np.concatenate([np.cos(inner), np.sin(inner), np.cos(outer), np.sin(outer)]).astype(np.float32)


def half_sign():
    lane = lax.broadcasted_iota(jnp.int32, (1, HEAD), 1)
    return jnp.where(lane < HEAD // 2, -1.0, 1.0).astype(jnp.float32)


def block_angles(table_ref, index, blocks):
    c_in, s_in = table_ref[0:BLK, :], table_ref[BLK : 2 * BLK, :]
    c_out = table_ref[pl.ds(2 * BLK + index, 1), :]
    s_out = table_ref[pl.ds(2 * BLK + blocks + index, 1), :]
    return c_in * c_out - s_in * s_out, s_in * c_out + c_in * s_out


def norm_rope(x, gain, cosine, sine_signed):
    normed = x * lax.rsqrt(jnp.mean(x * x, axis=-1, keepdims=True) + EPS) * gain
    return normed * cosine + pltpu.roll(normed, HEAD // 2, 1) * sine_signed


def norm_rope_back(x, dy, gain, cosine, sine_signed):
    inv = lax.rsqrt(jnp.mean(x * x, axis=-1, keepdims=True) + EPS)
    dn = (dy * cosine + pltpu.roll(dy * sine_signed, HEAD // 2, 1)) * gain
    inner = jnp.mean(x * dn, axis=-1, keepdims=True)
    return inv * dn - x * (inv * inv * inv * inner)


def whole(*dims):
    return pl.BlockSpec(dims, lambda i: (0,) * len(dims))


def key_kernel(
    tags_ref, key_hbm, value_hbm, gain_hbm, table_hbm, out_ref, cos_ref, sin_ref, key_ref, gain_ref, table_ref, sems, *, blocks
):
    heads, tok = out_ref.shape[0], key_ref.shape[0]
    copies = [
        pltpu.make_async_copy(source, dest, sems.at[i])
        for i, (source, dest) in enumerate(((key_hbm, key_ref), (gain_hbm, gain_ref), (table_hbm, table_ref)))
    ]
    copies += [
        pltpu.make_async_copy(value_hbm.at[:, pl.ds(g * HEAD, HEAD)], out_ref.at[g, :, pl.ds(HEAD, HEAD)], sems.at[3 + g])
        for g in range(heads)
    ]
    for copy in copies:
        copy.start()
    for copy in copies[:3]:
        copy.wait()
    gain, sign = gain_ref[...], half_sign()
    own_blocks = tok // BLK
    base = place_of(0, 0) * own_blocks
    for j in range(own_blocks):
        rows = slice(j * BLK, (j + 1) * BLK)
        cosine, sine = block_angles(table_ref, tags_ref[base + j] % blocks, blocks)
        sine = sine * sign
        cos_ref[rows, :] = cosine
        sin_ref[rows, :] = sine
        for g in range(heads):
            x = key_ref[rows, g * HEAD : (g + 1) * HEAD].astype(jnp.float32)
            out_ref[g, rows, 0:HEAD] = norm_rope(x, gain, cosine, sine).astype(jnp.bfloat16)
    for copy in copies[3:]:
        copy.wait()


def key_prep(tags, keys, values, gain, table, heads):
    tok = keys.shape[0]
    blocks = (table.shape[0] - 2 * BLK) // 2
    return pl.pallas_call(
        functools.partial(key_kernel, blocks=blocks),
        in_specs=[SMEM] + [HBM] * 4,
        out_specs=[VMEM] * 3,
        out_shape=[shape((heads, tok, 2 * HEAD), jnp.bfloat16)] + [shape((tok, HEAD), jnp.float32)] * 2,
        scratch_shapes=[
            pltpu.VMEM(keys.shape, keys.dtype),
            pltpu.VMEM(gain.shape, gain.dtype),
            pltpu.VMEM(table.shape, table.dtype),
            pltpu.SemaphoreType.DMA((3 + heads,)),
        ],
        compiler_params=params(),
        cost_estimate=cost(0, 1 << 20),
        name="key_prep",
    )(tags, keys, values, gain, table)


def query_kernel(q_ref, gain_ref, cos_ref, sin_ref, out_ref):
    gain, cosine, sine = gain_ref[...], cos_ref[...], sin_ref[...]
    for h in range(q_ref.shape[1] // HEAD):
        cols = slice(h * HEAD, (h + 1) * HEAD)
        x = q_ref[:, cols].astype(jnp.float32)
        out_ref[:, cols] = norm_rope(x, gain, cosine, sine).astype(jnp.bfloat16)


def query_prep(q_raw, gain, cosine, sine):
    return pl.pallas_call(
        query_kernel,
        grid=(1,),
        in_specs=[whole(*q_raw.shape), whole(*gain.shape), VMEM, VMEM],
        out_specs=VMEM,
        out_shape=shape(q_raw.shape, jnp.bfloat16),
        compiler_params=params(),
        cost_estimate=cost(0, 4 << 20),
        name="query_prep",
    )(q_raw, gain, cosine, sine)


def d_attn_kernel(me_ref, p0, p1, p2, p3, w_ref, out_ref, acc):
    k = pl.program_id(0)
    for i, piece in enumerate((p0, p1, p2, p3)):

        @pl.when(k == i)
        def _(i=i, piece=piece):
            term = lax.dot_general(piece[...], w_ref[...], (((1,), (1,)), ((), ())), preferred_element_type=jnp.float32)
            if i == 0:
                acc[...] = term
            elif i < 3:
                acc[...] += term
            else:
                out_ref[...] = (acc[...] + term).astype(jnp.bfloat16)


def d_attn_product(me, pieces, w_out):
    tok, width = pieces[0].shape
    feats = w_out.shape[0]
    whole = lambda k, me: (0, 0)
    return pl.pallas_call(
        d_attn_kernel,
        grid_spec=pltpu.PrefetchScalarGridSpec(
            num_scalar_prefetch=1,
            grid=(4,),
            in_specs=[pl.BlockSpec((tok, width), whole)] * 4
            + [pl.BlockSpec((feats, width), lambda k, me: (0, me[0] ^ k))],
            out_specs=pl.BlockSpec((tok, feats), whole),
            scratch_shapes=[pltpu.VMEM((tok, feats), jnp.float32)],
        ),
        out_shape=shape((tok, feats), jnp.bfloat16),
        compiler_params=params(),
        cost_estimate=cost(2 * tok * feats * width * 4, 12 << 20),
        name="d_attn_product",
    )(me, *pieces, w_out)


def out_kernel(me_ref, a0_ref, a1_ref, w_ref, send_ref, keep_ref):
    k = pl.program_id(0)
    half = a0_ref.shape[1]
    term = jnp.dot(a0_ref[...], w_ref[0:half, :], preferred_element_type=jnp.float32)
    term += jnp.dot(a1_ref[...], w_ref[half:, :], preferred_element_type=jnp.float32)

    @pl.when(k < 2)
    def _():
        send_ref[pl.ds(k, 1)] = term.astype(jnp.bfloat16)[None]

    @pl.when(k >= 2)
    def _():
        keep_ref[pl.ds(k - 2, 1)] = term.astype(jnp.bfloat16)[None]


def out_product(me, a0, a1, w_out):
    tok = a0.shape[0]
    feats, wide = w_out.shape
    width = wide // 4
    whole = lambda k, me: (0, 0)
    pair = lambda k, me: (0, 0, 0)
    return pl.pallas_call(
        out_kernel,
        grid_spec=pltpu.PrefetchScalarGridSpec(
            num_scalar_prefetch=1,
            grid=(4,),
            in_specs=[pl.BlockSpec(a0.shape, whole)] * 2
            + [pl.BlockSpec((feats, width), lambda k, me: (0, me[0] ^ (2 * (k % 2) + 1 - k // 2)))],
            out_specs=[pl.BlockSpec((2, tok, width), pair)] * 2,
        ),
        out_shape=[shape((2, tok, width), jnp.bfloat16)] * 2,
        compiler_params=params(),
        cost_estimate=cost(2 * tok * feats * wide, 12 << 20),
        name="out_product",
    )(me, a0, a1, w_out)


def place_of(far, near):
    here = lax.axis_index("ctx")
    first = lax.axis_index("ffn") % 2 == 0
    dx = jnp.where(first, near, far)
    dy = jnp.where(first, far, near)
    return (here // SIDE - dy + SIDE) % SIDE * SIDE + (here % SIDE - dx + SIDE) % SIDE


def attention_kernel(tags_ref, q_ref, do_ref, *refs, first, nclean, own_blocks, group):
    pieces, (attn_ref, dq_ref), outs = refs[0:4], refs[4:6], refs[6:10]
    ks, vs, kt, vt, dk, dv, st = refs[10:]
    spare = 2 * nclean
    rows = group * BLK
    wide = WIDE * BLK
    own_base = place_of(0, 0) * own_blocks
    for far in range(SIDE):
        for near in range(SIDE):
            base = place_of(far, near) * own_blocks
            for b in range(own_blocks):
                tag = tags_ref[base + b]
                part = slice((near * own_blocks + b) * BLK, (near * own_blocks + b + 1) * BLK)
                ks[tag] = pieces[far][part, 0:HEAD]
                vs[tag] = pieces[far][part, HEAD:]

    def flip(ref, pair):
        return ref[pl.ds(nclean + 2 * pair, 2)].reshape(2 * BLK, HEAD).astype(jnp.float32).T.astype(jnp.bfloat16)

    def chunk(ref, c):
        return ref[pl.ds(nclean + WIDE * c, WIDE)].reshape(wide, HEAD)

    def chunk_t(ref, c):
        return jnp.concatenate([ref[WIDE // 2 * c + i] for i in range(WIDE // 2)], axis=1)

    for pair in range(nclean // 2):
        kt[pair] = flip(ks, pair)
        vt[pair] = flip(vs, pair)
    dk[...] = jnp.zeros_like(dk)
    dv[...] = jnp.zeros_like(dv)

    def gather(ref, j):
        return jnp.concatenate(
            [ref[pl.ds(j * BLK, BLK), (first + h) * HEAD : (first + h + 1) * HEAD] for h in range(group)], axis=0
        )

    def one_block(j, unused):
        own = tags_ref[own_base + j]
        noisy = own < nclean
        index = own % nclean
        slot = nclean + index
        pair = index // 2

        @pl.when(noisy)
        def _():
            for ref, ref_t, grad in ((ks, kt, dk), (vs, vt, dv)):
                ref[spare] = ref[slot]
                ref[slot] = ref[own]
                ref_t[nclean // 2] = ref_t[pair]
                ref_t[pair] = flip(ref, pair)
                grad[spare] = grad[slot]
                grad[slot] = jnp.zeros((BLK, HEAD), jnp.float32)

        q = gather(q_ref, j)
        do = gather(do_ref, j)
        do_t = do.astype(jnp.float32).T

        top = jnp.full((8, rows), NEG, jnp.float32)
        for c in range(nclean // WIDE):
            s = lax.dot_general(chunk(ks, c), q, (((1,), (1,)), ((), ())), preferred_element_type=jnp.float32)
            for i in range(WIDE):
                part = s[i * BLK : (i + 1) * BLK] * SCALE2
                part = part + jnp.where(WIDE * c + i > index, NEG, 0.0).astype(jnp.float32)
                st[c, i * BLK : (i + 1) * BLK, :] = part
                top = jnp.maximum(top, jnp.max(part.reshape(BLK // 8, 8, rows), axis=0))
        top = jnp.max(top, axis=0, keepdims=True)
        total = jnp.zeros((8, rows), jnp.float32)
        acc = jnp.zeros((HEAD, rows), jnp.float32)
        for c in range(nclean // WIDE):
            e = jnp.exp2(st[c] - top)
            total = total + jnp.sum(e.reshape(wide // 8, 8, rows), axis=0)
            acc = acc + jnp.dot(chunk_t(vt, c), e.astype(jnp.bfloat16), preferred_element_type=jnp.float32)
        total = jnp.sum(total, axis=0, keepdims=True)
        attn_t = (acc / total).astype(jnp.bfloat16).astype(jnp.float32)
        delta = jnp.sum(do_t * attn_t, axis=0, keepdims=True)
        attn = attn_t.T.astype(jnp.bfloat16)
        for h in range(group):
            attn_ref[pl.ds(j * BLK, BLK), h * HEAD : (h + 1) * HEAD] = attn[h * BLK : (h + 1) * BLK]
        top = top + jnp.log2(total)
        acc = jnp.zeros((HEAD, rows), jnp.float32)
        for c in range(nclean // WIDE):
            p = jnp.exp2(st[c] - top)
            dp = lax.dot_general(chunk(vs, c), do, (((1,), (1,)), ((), ())), preferred_element_type=jnp.float32)
            ds = (p * (dp - delta)).astype(jnp.bfloat16)
            dvc = jnp.dot(p.astype(jnp.bfloat16), do, preferred_element_type=jnp.float32)
            dkc = jnp.dot(ds, q, preferred_element_type=jnp.float32)
            dv[pl.ds(nclean + WIDE * c, WIDE)] += dvc.reshape(WIDE, BLK, HEAD)
            dk[pl.ds(nclean + WIDE * c, WIDE)] += dkc.reshape(WIDE, BLK, HEAD)
            acc = acc + jnp.dot(chunk_t(kt, c), ds, preferred_element_type=jnp.float32)
        dq = (acc * SCALE).T
        for h in range(group):
            dq_ref[pl.ds(j * BLK, BLK), h * HEAD : (h + 1) * HEAD] = dq[h * BLK : (h + 1) * BLK]

        @pl.when(noisy)
        def _():
            for ref, ref_t, grad in ((ks, kt, dk), (vs, vt, dv)):
                ref[slot] = ref[spare]
                ref_t[pair] = ref_t[nclean // 2]
                grad[own] = grad[slot]
                grad[slot] = grad[spare]

        return unused

    lax.fori_loop(0, own_blocks, one_block, 0)
    for far in range(SIDE):
        for near in range(SIDE):
            base = place_of(far, near) * own_blocks
            for b in range(own_blocks):
                tag = tags_ref[base + b]
                part = slice((near * own_blocks + b) * BLK, (near * own_blocks + b + 1) * BLK)
                outs[far][part, 0:HEAD] = (dk[tag] * SCALE).astype(jnp.bfloat16)
                outs[far][part, HEAD:] = dv[tag].astype(jnp.bfloat16)


def attention(tags, q, do, pieces, g, group):
    tok = q.shape[0]
    nclean = tags.shape[0] // 2
    rows = group * BLK
    blocks = 2 * nclean + 1
    return pl.pallas_call(
        functools.partial(
            attention_kernel, first=g * group, nclean=nclean, own_blocks=tok // BLK, group=group
        ),
        in_specs=[SMEM] + [VMEM] * 6,
        out_specs=[VMEM] * 6,
        out_shape=[shape((tok, group * HEAD), jnp.bfloat16), shape((tok, group * HEAD), jnp.float32)]
        + [shape(pieces[0].shape, jnp.bfloat16)] * 4,
        scratch_shapes=[
            pltpu.VMEM((blocks, BLK, HEAD), jnp.bfloat16),
            pltpu.VMEM((blocks, BLK, HEAD), jnp.bfloat16),
            pltpu.VMEM((nclean // 2 + 1, HEAD, 2 * BLK), jnp.bfloat16),
            pltpu.VMEM((nclean // 2 + 1, HEAD, 2 * BLK), jnp.bfloat16),
            pltpu.VMEM((blocks, BLK, HEAD), jnp.float32),
            pltpu.VMEM((blocks, BLK, HEAD), jnp.float32),
            pltpu.VMEM((nclean // WIDE, WIDE * BLK, rows), jnp.float32),
        ],
        compiler_params=params(),
        cost_estimate=cost(6 << 30, 4 << 20),
        name="attention",
    )(tags, q, do, *pieces)


def query_back_kernel(q_ref, a_ref, b_ref, gain_ref, cos_ref, sin_ref, out_ref):
    gain, cosine, sine = gain_ref[...], cos_ref[...], sin_ref[...]
    heads = a_ref.shape[1] // HEAD
    for h in range(2 * heads):
        cols = slice(h * HEAD, (h + 1) * HEAD)
        source = (a_ref, b_ref)[h // heads]
        dy = source[:, (h % heads) * HEAD : (h % heads + 1) * HEAD]
        out_ref[:, cols] = norm_rope_back(q_ref[:, cols].astype(jnp.float32), dy, gain, cosine, sine)


def query_back(q_raw, dq0, dq1, gain, cosine, sine):
    return pl.pallas_call(
        query_back_kernel,
        grid=(1,),
        in_specs=[whole(*q_raw.shape), VMEM, VMEM, whole(*gain.shape), VMEM, VMEM],
        out_specs=whole(*q_raw.shape),
        out_shape=shape(q_raw.shape, jnp.float32),
        compiler_params=params(),
        cost_estimate=cost(0, 8 << 20),
        name="query_back",
    )(q_raw, dq0, dq1, gain, cosine, sine)


def key_back_kernel(key_ref, gain_ref, cos_ref, sin_ref, a, b, c, d, dk_ref, dv_ref):
    gain, cosine, sine = gain_ref[...], cos_ref[...], sin_ref[...]
    for g in range(a.shape[0]):
        cols = slice(g * HEAD, (g + 1) * HEAD)
        total = a[g].astype(jnp.float32) + b[g].astype(jnp.float32)
        total += c[g].astype(jnp.float32) + d[g].astype(jnp.float32)
        x = key_ref[:, cols].astype(jnp.float32)
        dk_ref[:, cols] = norm_rope_back(x, total[:, 0:HEAD], gain, cosine, sine)
        dv_ref[:, cols] = total[:, HEAD:]


def key_back(keys, gain, cosine, sine, parts):
    return pl.pallas_call(
        key_back_kernel,
        grid=(1,),
        in_specs=[whole(*keys.shape), whole(*gain.shape)] + [VMEM] * 6,
        out_specs=[whole(*keys.shape)] * 2,
        out_shape=[shape(keys.shape, jnp.float32)] * 2,
        compiler_params=params(),
        cost_estimate=cost(0, 2 << 20),
        name="key_back",
    )(keys, gain, cosine, sine, *parts)


def fold_kernel(*refs):
    parts, outs = refs[:-SIDE], refs[-SIDE:]
    rows = outs[0].shape[1]
    for g in range(len(parts) // SIDE):
        a, b, c, d = parts[SIDE * g : SIDE * g + SIDE]
        for i, out in enumerate(outs):
            part = slice(i * rows, (i + 1) * rows)
            total = a[part, :].astype(jnp.float32) + b[part, :].astype(jnp.float32)
            total += c[part, :].astype(jnp.float32) + d[part, :].astype(jnp.float32)
            out[g] = total.astype(jnp.bfloat16)


def fold(heads):
    rows, width = heads[0][0].shape
    return pl.pallas_call(
        fold_kernel,
        in_specs=[VMEM] * (SIDE * len(heads)),
        out_specs=[VMEM] * SIDE,
        out_shape=[shape((len(heads), rows // SIDE, width), jnp.bfloat16)] * SIDE,
        compiler_params=params(),
        cost_estimate=cost(0, 4 << 20),
        name="fold",
    )(*(part for parts in heads for part in parts))


def hop(value, steps, phase):
    pairs = []
    for y in range(SIDE):
        for x in range(SIDE):
            for f in range(4):
                dx, dy = (steps, 0) if (f + phase) % 2 == 0 else (0, steps)
                there = (y + dy) % SIDE * SIDE + (x + dx) % SIDE
                pairs.append(((y * SIDE + x) * 4 + f, there * 4 + f))
    return lax.ppermute(value, ("ctx", "ffn"), pairs)


def across(value, mask):
    return lax.ppermute(value, "ffn", [(s, s ^ mask) for s in range(4)])


def spread(value, phase):
    return [value] + [hop(value, k, phase) for k in range(1, SIDE)]


def collect(values, phase):
    return [values[0]] + [hop(values[k], -k, phase) for k in range(1, SIDE)]


def per_device(q_raw, keys, values, q_gain, k_gain, block_tags, w_out, d_out):
    nclean = block_tags.shape[0] // 2
    me = lax.axis_index("ffn").astype(jnp.int32)[None]
    heads = keys.shape[1] // HEAD
    group = q_raw.shape[1] // keys.shape[1]
    q_gain, k_gain = q_gain[None, :], k_gain[None, :]
    table = jnp.asarray(angle_table(nclean))

    kv, cosine, sine = key_prep(block_tags, keys, values, k_gain, table, heads)
    near = spread(kv, 0)
    far = across(d_out, 2)
    d_pieces = [d_out, across(d_out, 1), far, across(far, 1)]
    q = query_prep(q_raw, q_gain, cosine, sine)
    do = d_attn_product(me, d_pieces, w_out)

    pieces = []
    for g in range(heads):
        line = jnp.concatenate([part[g] for part in near], axis=0)
        if g:
            line, do, pieces[g - 1] = lax.optimization_barrier((line, do, pieces[g - 1]))
        pieces.append(spread(line, 1))

    attn, dq, sums = [], [], []
    for g in range(heads):
        results = attention(block_tags, q, do, pieces[g], g, group)
        if g:
            results, sums[g - 1] = lax.optimization_barrier((results, sums[g - 1]))
        attn_g, dq_g, *grads = results
        attn.append(attn_g)
        dq.append(dq_g)
        sums.append(collect(grads, 1))
    parts = collect(fold(sums), 0)

    send, keep = out_product(me, attn[0], attn[1], w_out)
    summed = keep.astype(jnp.float32) + across(send, 1).astype(jnp.float32)
    other = across(summed[1].astype(jnp.bfloat16), 2)
    attn_out = (summed[0] + other.astype(jnp.float32)).astype(jnp.bfloat16)
    d_q = query_back(q_raw, dq[0], dq[1], q_gain, cosine, sine)
    key_gradient, value_gradient = key_back(keys, k_gain, cosine, sine, parts)
    return attn_out, d_q, key_gradient, value_gradient


def solution(mesh):
    split = P(("dp", "ctx"), "ffn")
    return jax.shard_map(
        per_device,
        mesh=mesh,
        in_specs=(split, split, split, P(), P(), P("dp"), P("ffn", None), split),
        out_specs=(split,) * 4,
        check_vma=False,
    )
```

time: 163 us -> 116 us (0.71)
  the two profiles are of different devices: /device:TPU:72 before, /device:TPU:96 now
where the time goes in v2:
time: 116 us
  waiting for transfers between devices  39.1 us (34%)
  Pallas kernels  38.4 us (33%)
  starting transfers between devices  25.3 us (22%)
  local copies, waits for them, and re-layouts  9.58 us (8%)
  other arithmetic  2.44 us (2%)
    ppermute x18, waiting for transfers between devices, hop(): return lax.ppermute(value, ('ctx', 'ffn'), pairs)  32.3 us
    pallas_call x2, Pallas kernels, attention(): pl.pallas_call(functools.partial(attention_kernel, first=g * group, nclea...  24.5 us
    ppermute x18, starting transfers between devices, hop(): return lax.ppermute(value, ('ctx', 'ffn'), pairs)  24.3 us
    unnamed x28, local copies, waits for them, and re-layouts  7.47 us
    ppermute x5, waiting for transfers between devices, across(): return lax.ppermute(value, 'ffn', [(s, s ^ mask) for s in range(4)])  6.82 us
    pallas_call x1, Pallas kernels, out_product(): pl.pallas_call(out_kernel, grid_spec=pltpu.PrefetchScalarGridSpec(num_sca...  3.8 us
    pallas_call x1, Pallas kernels, d_attn_product(): pl.pallas_call(d_attn_kernel, grid_spec=pltpu.PrefetchScalarGridSpec(num_...  3.66 us
  transfers between devices with their start and end apart: 23, of which 12 were waited for; matrix products, arithmetic and copies ran while one was open for 3% of the time, Pallas kernels for 29%

profile of v2, /device:TPU:96, one launch (start us, length us, event | category | flops | bytes accessed | tf_op | source)
XLA Modules:
  0.0 115.6 jit_solution(11245500847728439493)
XLA Ops:
  0.7 1.0 copy-done.3
  4.7 1.5 %key_prep.1 = (bf16[2,256,256]{2,1,0:T(8,128)(2,1)S(1)}, f32[256,128]{1,0:T(8,128)S(1)}, f32[256,128]{1,0:T(8,128)S(1)}) custom-call(s32[64]{0:T(128)S(1)} %copy-done.10, bf16[256,256]{1,0:T(8,128)(2,1)S(1)} %copy-done.3, bf16[256,256]{1,0:T(8,128)(2,1)S(1)} %copy-done.5, f32[1,128]{1,0:T(1,128)S(1)} %bitcast.31, f32[192,128]{1,0:T(8,128)S(1)} %copy-done.6), custom_call_target="tpu_custom_call" | custom-call | bytes 1048576 | tf_op jit(solution)/shard_map/key_prep/pallas_call | solution.py:109
  6.2 1.6 %collective-permute-start = (bf16[2,256,256]{2,1,0:T(8,128)(2,1)S(1)}, bf16[2,256,256]{2,1,0:T(8,128)(2,1)S(1)}, u32[]{:S(2)}, u32[]{:S(2)}) collective-permute-start(bf16[2,256,256]{2,1,0:T(8,128)(2,1)S(1)} %get-tuple-element.45), channel_id=1, source_target_pairs={{0,8},{2,34},{4,12},{6,38},{8,16},{10,42},{12,20},{14,46},{16,24},... | collective-permute-start | bytes 786440 | tf_op jit(solution)/shard_map/ppermute | solution.py:450
  7.7 2.7 %collective-permute-start.1 = (bf16[2,256,256]{2,1,0:T(8,128)(2,1)S(1)}, bf16[2,256,256]{2,1,0:T(8,128)(2,1)S(1)}, u32[]{:S(2)}, u32[]{:S(2)}) collective-permute-start(bf16[2,256,256]{2,1,0:T(8,128)(2,1)S(1)} %get-tuple-element.45), channel_id=1, source_target_pairs={{0,16},{2,66},{4,20},{6,70},{8,24},{10,74},{12,28},{14,78},{16,0},... | collective-permute-start | bytes 786440 | tf_op jit(solution)/shard_map/ppermute | solution.py:450
  10.5 1.4 %collective-permute-start.2 = (bf16[2,256,256]{2,1,0:T(8,128)(2,1)S(1)}, bf16[2,256,256]{2,1,0:T(8,128)(2,1)S(1)}, u32[]{:S(2)}, u32[]{:S(2)}) collective-permute-start(bf16[2,256,256]{2,1,0:T(8,128)(2,1)S(1)} %get-tuple-element.45), channel_id=1, source_target_pairs={{0,24},{2,98},{4,28},{6,102},{8,0},{10,106},{12,4},{14,110},{16,8}... | collective-permute-start | bytes 786440 | tf_op jit(solution)/shard_map/ppermute | solution.py:450
  12.3 1.5 %collective-permute-done = bf16[2,256,256]{2,1,0:T(8,128)(2,1)S(1)} collective-permute-done((bf16[2,256,256]{2,1,0:T(8,128)(2,1)S(1)}, bf16[2,256,256]{2,1,0:T(8,128)(2,1)S(1)}, u32[]{:S(2)}, u32[]{:S(2)}) %collective-permute-start) | collective-permute-done | bytes 262176 | tf_op jit(solution)/shard_map/ppermute | solution.py:450
  14.5 3.1 %collective-permute-done.1 = bf16[2,256,256]{2,1,0:T(8,128)(2,1)S(1)} collective-permute-done((bf16[2,256,256]{2,1,0:T(8,128)(2,1)S(1)}, bf16[2,256,256]{2,1,0:T(8,128)(2,1)S(1)}, u32[]{:S(2)}, u32[]{:S(2)}) %collective-permute-start.1) | collective-permute-done | bytes 262176 | tf_op jit(solution)/shard_map/ppermute | solution.py:450
  18.3 6.8 %collective-permute-done.4.p2 = bf16[256,1024]{1,0:T(8,128)(2,1)S(1)} collective-permute-done((bf16[256,1024]{1,0:T(8,128)(2,1)}, bf16[256,1024]{1,0:T(8,128)(2,1)S(1)}, u32[]{:S(2)}, u32[]{:S(2)}) %collective-permute-start.4) | collective-permute-done | bytes 524320 | tf_op jit(solution)/shard_map/ppermute | solution.py:454
  26.6 1.1 collective-permute-start.7
  27.6 1.7 %collective-permute-start.8 = (bf16[1024,256]{1,0:T(8,128)(2,1)S(1)}, bf16[1024,256]{1,0:T(8,128)(2,1)}, u32[]{:S(2)}, u32[]{:S(2)}) collective-permute-start(bf16[1024,256]{1,0:T(8,128)(2,1)S(1)} %pad_maximum_fusion.1.refs_0_), channel_id=1, source_target_pairs={{0,96},{2,26},{4,100},{6,30},{8,104},{10,2},{12,108},{14,6},{16,11... | collective-permute-start | bytes 1572872 | tf_op jit(solution)/shard_map/ppermute | solution.py:450
  29.3 1.1 query_prep.1.q_ref
  30.5 1.1 pad_maximum_fusion.refs_0_
  31.6 3.4 %copy-done = bf16[1024,4096]{1,0:T(8,128)(2,1)S(1)} copy-done((bf16[1024,4096]{1,0:T(8,128)(2,1)S(1)}, bf16[1024,4096]{1,0:T(8,128)(2,1)}, u32[]{:S(2)}) %copy-start) | copy-done | bytes 8388632
  35.0 3.7 %d_attn_product.1.do_ref = bf16[256,1024]{1,0:T(8,128)(2,1)S(1)} custom-call(s32[1]{0:T(128)} %bitcast.me_ref, bf16[256,1024]{1,0:T(8,128)(2,1)S(1)} %copy-done.2, bf16[256,1024]{1,0:T(8,128)(2,1)S(1)} %collective-permute-done.3.p1, bf16[256,1024]{1,0:T(8,128)(2,1)S(1)} %collective-permute-done.4.p2, bf16[256,1024]{1,0:T(8,128)(2,1)S(1)} %collective-permute-done.5.p3, ...), custom_call_target="tpu_custom_call" | custom-call | flops 2147483648 | bytes 12582912 | tf_op jit(solution)/shard_map/d_attn_product/pallas_call | solution.py:166
  38.7 3.4 %collective-permute-done.6.refs_1_ = bf16[1024,256]{1,0:T(8,128)(2,1)} collective-permute-done((bf16[1024,256]{1,0:T(8,128)(2,1)S(1)}, bf16[1024,256]{1,0:T(8,128)(2,1)}, u32[]{:S(2)}, u32[]{:S(2)}) %collective-permute-start.6) | collective-permute-done | bytes 524320 | tf_op jit(solution)/shard_map/ppermute | solution.py:450
  43.7 2.0 %collective-permute-start.11 = (bf16[1024,256]{1,0:T(8,128)(2,1)S(1)}, bf16[1024,256]{1,0:T(8,128)(2,1)S(1)}, u32[]{:S(2)}, u32[]{:S(2)}) collective-permute-start(bf16[1024,256]{1,0:T(8,128)(2,1)S(1)} %pad_maximum_fusion.refs_0_), channel_id=1, source_target_pairs={{0,96},{2,26},{4,100},{6,30},{8,104},{10,2},{12,108},{14,6},{16,11... | collective-permute-start | bytes 1572872 | tf_op jit(solution)/shard_map/ppermute | solution.py:450
  46.3 12.6 %attention.2 = (bf16[256,512]{1,0:T(8,128)(2,1)S(1)}, f32[256,512]{1,0:T(8,128)S(1)}, bf16[1024,256]{1,0:T(8,128)(2,1)S(1)}, bf16[1024,256]{1,0:T(8,128)(2,1)S(1...) custom-call(s32[64]{0:T(128)S(1)} %copy-done.11, bf16[256,1024]{1,0:T(8,128)(2,1)S(1)} %query_prep.1.q_ref, ...), custom_call_target="tpu_custom_call" | custom-call | flops 6442450944 | bytes 4194304 | tf_op jit(solution)/shard_map/attention/pallas_call | solution.py:347
  59.0 3.1 %collective-permute-start.12 = (bf16[1024,256]{1,0:T(8,128)(2,1)S(1)}, bf16[1024,256]{1,0:T(8,128)(2,1)S(1)}, u32[]{:S(2)}, u32[]{:S(2)}) collective-permute-start(bf16[1024,256]{1,0:T(8,128)(2,1)S(1)} %get-tuple-element.60), channel_id=1, source_target_pairs={{0,96},{2,26},{4,100},{6,30},{8,104},{10,2},{12,108},{14,6},{16,11... | collective-permute-start | bytes 1572872 | tf_op jit(solution)/shard_map/ppermute | solution.py:450
  62.0 1.3 %collective-permute-start.13 = (bf16[1024,256]{1,0:T(8,128)(2,1)S(1)}, bf16[1024,256]{1,0:T(8,128)(2,1)S(1)}, u32[]{:S(2)}, u32[]{:S(2)}) collective-permute-start(bf16[1024,256]{1,0:T(8,128)(2,1)S(1)} %get-tuple-element.61), channel_id=1, source_target_pairs={{0,64},{2,18},{4,68},{6,22},{8,72},{10,26},{12,76},{14,30},{16,80}... | collective-permute-start | bytes 1572872 | tf_op jit(solution)/shard_map/ppermute | solution.py:450
  63.3 11.8 %attention.3 = (bf16[256,512]{1,0:T(8,128)(2,1)S(1)}, f32[256,512]{1,0:T(8,128)S(1)}, bf16[1024,256]{1,0:T(8,128)(2,1)S(1)}, bf16[1024,256]{1,0:T(8,128)(2,1)S(1...) custom-call(s32[64]{0:T(128)S(1)} %copy-done.11, bf16[256,1024]{1,0:T(8,128)(2,1)S(1)} %query_prep.1.q_ref, ...), custom_call_target="tpu_custom_call" | custom-call | flops 6442450944 | bytes 4194304 | tf_op jit(solution)/shard_map/attention/pallas_call | solution.py:347
  75.2 3.1 %collective-permute-done.14.refs_3_ = bf16[1024,256]{1,0:T(8,128)(2,1)S(1)} collective-permute-done((bf16[1024,256]{1,0:T(8,128)(2,1)S(1)}, bf16[1024,256]{1,0:T(8,128)(2,1)S(1)}, u32[]{:S(2)}, u32[]{:S(2)}) %collective-permute-start.14) | collective-permute-done | bytes 524320 | tf_op jit(solution)/shard_map/ppermute | solution.py:450
  78.3 3.8 %out_product.1 = (bf16[2,256,1024]{2,1,0:T(8,128)(2,1)S(1)}, bf16[2,256,1024]{2,1,0:T(8,128)(2,1)S(1)}) custom-call(s32[1]{0:T(128)} %bitcast.me_ref, bf16[256,512]{1,0:T(8,128)(2,1)S(1)} %get-tuple-element.51.a0_ref, bf16[256,512]{1,0:T(8,128)(2,1)S(1)} %get-tuple-element.63.a1_ref, bf16[1024,4096]{1,0:T(8,128)(2,1)S(1)} %bitcast.28), custom_call_target="tpu_custom_call" | custom-call | flops 2147483648 | bytes 12582912 | tf_op jit(solution)/shard_map/out_product/pallas_call | solution.py:204
  82.9 1.3 %collective-permute-start.18 = (bf16[1024,256]{1,0:T(8,128)(2,1)S(1)}, bf16[1024,256]{1,0:T(8,128)(2,1)S(1)}, u32[]{:S(2)}, u32[]{:S(2)}) collective-permute-start(bf16[1024,256]{1,0:T(8,128)(2,1)S(1)} %get-tuple-element.74), channel_id=1, source_target_pairs={{0,64},{2,18},{4,68},{6,22},{8,72},{10,26},{12,76},{14,30},{16,80}... | collective-permute-start | bytes 1572872 | tf_op jit(solution)/shard_map/ppermute | solution.py:450
  86.0 5.5 %collective-permute-done.17.refs_5_ = bf16[1024,256]{1,0:T(8,128)(2,1)S(1)} collective-permute-done((bf16[1024,256]{1,0:T(8,128)(2,1)S(1)}, bf16[1024,256]{1,0:T(8,128)(2,1)S(1)}, u32[]{:S(2)}, u32[]{:S(2)}) %collective-permute-start.17) | collective-permute-done | bytes 524320 | tf_op jit(solution)/shard_map/ppermute | solution.py:450
  91.5 2.2 %collective-permute-done.18.refs_6_ = bf16[1024,256]{1,0:T(8,128)(2,1)S(1)} collective-permute-done((bf16[1024,256]{1,0:T(8,128)(2,1)S(1)}, bf16[1024,256]{1,0:T(8,128)(2,1)S(1)}, u32[]{:S(2)}, u32[]{:S(2)}) %collective-permute-start.18) | collective-permute-done | bytes 524320 | tf_op jit(solution)/shard_map/ppermute | solution.py:450
  93.7 5.5 %collective-permute-done.19.refs_7_ = bf16[1024,256]{1,0:T(8,128)(2,1)S(1)} collective-permute-done((bf16[1024,256]{1,0:T(8,128)(2,1)S(1)}, bf16[1024,256]{1,0:T(8,128)(2,1)S(1)}, u32[]{:S(2)}, u32[]{:S(2)}) %collective-permute-start.19) | collective-permute-done | bytes 524320 | tf_op jit(solution)/shard_map/ppermute | solution.py:450
  99.7 3.1 %collective-permute-start.20 = (bf16[2,256,256]{2,1,0:T(8,128)(2,1)S(1)}, bf16[2,256,256]{2,1,0:T(8,128)(2,1)S(1)}, u32[]{:S(2)}, u32[]{:S(2)}) collective-permute-start(bf16[2,256,256]{2,1,0:T(8,128)(2,1)S(1)} %get-tuple-element.77), channel_id=1, source_target_pairs={{0,24},{2,98},{4,28},{6,102},{8,0},{10,106},{12,4},{14,110},{16,8}... | collective-permute-start | bytes 786440 | tf_op jit(solution)/shard_map/ppermute | solution.py:450
  104.3 2.3 %query_back.1 = f32[256,1024]{1,0:T(8,128)} custom-call(bf16[256,1024]{1,0:T(8,128)(2,1)S(1)} %copy-done.1, f32[256,512]{1,0:T(8,128)S(1)} %get-tuple-element.66.a_ref, f32[256,512]{1,0:T(8,128)S(1)} %get-tuple-element.67.b_ref, f32[1,128]{1,0:T(1,128)S(1)} %bitcast.30, f32[256,128]{1,0:T(8,128)S(1)} %get-tuple-element.43.cos_ref, ...), custom_call_target="tpu_custom_call" | custom-call | bytes 8388608 | tf_op jit(solution)/shard_map/query_back/pallas_call | solution.py:381
  106.5 3.0 %collective-permute-done.20.b = bf16[2,256,256]{2,1,0:T(8,128)(2,1)S(1)} collective-permute-done((bf16[2,256,256]{2,1,0:T(8,128)(2,1)S(1)}, bf16[2,256,256]{2,1,0:T(8,128)(2,1)S(1)}, u32[]{:S(2)}, u32[]{:S(2)}) %collective-permute-start.20) | collective-permute-done | bytes 262176 | tf_op jit(solution)/shard_map/ppermute | solution.py:450
  109.6 1.3 %collective-permute-done.21.c = bf16[2,256,256]{2,1,0:T(8,128)(2,1)S(1)} collective-permute-done((bf16[2,256,256]{2,1,0:T(8,128)(2,1)S(1)}, bf16[2,256,256]{2,1,0:T(8,128)(2,1)S(1)}, u32[]{:S(2)}, u32[]{:S(2)}) %collective-permute-start.21) | collective-permute-done | bytes 262176 | tf_op jit(solution)/shard_map/ppermute | solution.py:450
  110.8 2.7 %collective-permute-done.22.d = bf16[2,256,256]{2,1,0:T(8,128)(2,1)S(1)} collective-permute-done((bf16[2,256,256]{2,1,0:T(8,128)(2,1)S(1)}, bf16[2,256,256]{2,1,0:T(8,128)(2,1)S(1)}, u32[]{:S(2)}, u32[]{:S(2)}) %collective-permute-start.22) | collective-permute-done | bytes 262176 | tf_op jit(solution)/shard_map/ppermute | solution.py:450
  113.5 1.1 key_back.1
  (61 shorter events, 14.1 us)
Async XLA Ops:
  0.6 28.7 %copy-start.1 = (bf16[256,1024]{1,0:T(8,128)(2,1)S(1)}, bf16[256,1024]{1,0:T(8,128)(2,1)}, u32[]{:S(2)}) copy-start(bf16[256,1024]{1,0:T(8,128)(2,1)} %q_ref.3) | copy-start | bytes 1572868
  4.7 24.6 %copy-start.7 = (f32[128]{0:T(128)S(1)}, f32[128]{0:T(128)}, u32[]{:S(2)}) copy-start(f32[128]{0:T(128)} %param.12) | copy-start | bytes 1540
  6.2 7.7 %collective-permute-start = (bf16[2,256,256]{2,1,0:T(8,128)(2,1)S(1)}, bf16[2,256,256]{2,1,0:T(8,128)(2,1)S(1)}, u32[]{:S(2)}, u32[]{:S(2)}) collective-permute-start(bf16[2,256,256]{2,1,0:T(8,128)(2,1)S(1)} %get-tuple-element.45), channel_id=1, source_target_pairs={{0,8},{2,34},{4,12},{6,38},{8,16},{10,42},{12,20},{14,46},{16,24},... | collective-permute-start | bytes 786440 | tf_op jit(solution)/shard_map/ppermute | solution.py:450
  7.7 9.9 %collective-permute-start.1 = (bf16[2,256,256]{2,1,0:T(8,128)(2,1)S(1)}, bf16[2,256,256]{2,1,0:T(8,128)(2,1)S(1)}, u32[]{:S(2)}, u32[]{:S(2)}) collective-permute-start(bf16[2,256,256]{2,1,0:T(8,128)(2,1)S(1)} %get-tuple-element.45), channel_id=1, source_target_pairs={{0,16},{2,66},{4,20},{6,70},{8,24},{10,74},{12,28},{14,78},{16,0},... | collective-permute-start | bytes 786440 | tf_op jit(solution)/shard_map/ppermute | solution.py:450
  10.5 14.6 %collective-permute-start.2 = (bf16[2,256,256]{2,1,0:T(8,128)(2,1)S(1)}, bf16[2,256,256]{2,1,0:T(8,128)(2,1)S(1)}, u32[]{:S(2)}, u32[]{:S(2)}) collective-permute-start(bf16[2,256,256]{2,1,0:T(8,128)(2,1)S(1)} %get-tuple-element.45), channel_id=1, source_target_pairs={{0,24},{2,98},{4,28},{6,102},{8,0},{10,106},{12,4},{14,110},{16,8}... | collective-permute-start | bytes 786440 | tf_op jit(solution)/shard_map/ppermute | solution.py:450
  11.9 13.2 %collective-permute-start.4 = (bf16[256,1024]{1,0:T(8,128)(2,1)}, bf16[256,1024]{1,0:T(8,128)(2,1)S(1)}, u32[]{:S(2)}, u32[]{:S(2)}) collective-permute-start(bf16[256,1024]{1,0:T(8,128)(2,1)} %p0.1), channel_id=1, source_target_pairs={{0,4},{2,6},{4,0},{6,2},{1,5},{3,7},{5,1},{7,3},{8,12},{10,14},{12... | collective-permute-start | bytes 1572872 | tf_op jit(solution)/shard_map/ppermute | solution.py:454
  12.3 19.3 %collective-permute-start.3 = (bf16[256,1024]{1,0:T(8,128)(2,1)}, bf16[256,1024]{1,0:T(8,128)(2,1)S(1)}, u32[]{:S(2)}, u32[]{:S(2)}) collective-permute-start(bf16[256,1024]{1,0:T(8,128)(2,1)} %p0.1), channel_id=1, source_target_pairs={{0,2},{2,0},{4,6},{6,4},{1,3},{3,1},{5,7},{7,5},{8,10},{10,8},{12,... | collective-permute-start | bytes 1572872 | tf_op jit(solution)/shard_map/ppermute | solution.py:454
  18.3 13.3 %copy-start.2 = (bf16[256,1024]{1,0:T(8,128)(2,1)S(1)}, bf16[256,1024]{1,0:T(8,128)(2,1)}, u32[]{:S(2)}) copy-start(bf16[256,1024]{1,0:T(8,128)(2,1)} %p0.1) | copy-start | bytes 1572868
  25.1 6.5 %collective-permute-start.5 = (bf16[256,1024]{1,0:T(8,128)(2,1)S(1)}, bf16[256,1024]{1,0:T(8,128)(2,1)S(1)}, u32[]{:S(2)}, u32[]{:S(2)}) collective-permute-start(bf16[256,1024]{1,0:T(8,128)(2,1)S(1)} %collective-permute-done.4.p2), channel_id=1, source_target_pairs={{0,2},{2,0},{4,6},{6,4},{1,3},{3,1},{5,7},{7,5},{8,10},{10,8},{12,... | collective-permute-start | bytes 1572872 | tf_op jit(solution)/shard_map/ppermute | solution.py:454
  25.8 16.2 %collective-permute-start.6 = (bf16[1024,256]{1,0:T(8,128)(2,1)S(1)}, bf16[1024,256]{1,0:T(8,128)(2,1)}, u32[]{:S(2)}, u32[]{:S(2)}) collective-permute-start(bf16[1024,256]{1,0:T(8,128)(2,1)S(1)} %pad_maximum_fusion.1.refs_0_), channel_id=1, source_target_pairs={{0,32},{2,10},{4,36},{6,14},{8,40},{10,18},{12,44},{14,22},{16,48}... | collective-permute-start | bytes 1572872 | tf_op jit(solution)/shard_map/ppermute | solution.py:450
  26.6 15.4 %collective-permute-start.7 = (bf16[1024,256]{1,0:T(8,128)(2,1)S(1)}, bf16[1024,256]{1,0:T(8,128)(2,1)}, u32[]{:S(2)}, u32[]{:S(2)}) collective-permute-start(bf16[1024,256]{1,0:T(8,128)(2,1)S(1)} %pad_maximum_fusion.1.refs_0_), channel_id=1, source_target_pairs={{0,64},{2,18},{4,68},{6,22},{8,72},{10,26},{12,76},{14,30},{16,80}... | collective-permute-start | bytes 1572872 | tf_op jit(solution)/shard_map/ppermute | solution.py:450
  27.6 15.3 %collective-permute-start.8 = (bf16[1024,256]{1,0:T(8,128)(2,1)S(1)}, bf16[1024,256]{1,0:T(8,128)(2,1)}, u32[]{:S(2)}, u32[]{:S(2)}) collective-permute-start(bf16[1024,256]{1,0:T(8,128)(2,1)S(1)} %pad_maximum_fusion.1.refs_0_), channel_id=1, source_target_pairs={{0,96},{2,26},{4,100},{6,30},{8,104},{10,2},{12,108},{14,6},{16,11... | collective-permute-start | bytes 1572872 | tf_op jit(solution)/shard_map/ppermute | solution.py:450
  31.6 3.4 %copy-start = (bf16[1024,4096]{1,0:T(8,128)(2,1)S(1)}, bf16[1024,4096]{1,0:T(8,128)(2,1)}, u32[]{:S(2)}) copy-start(bf16[1024,4096]{1,0:T(8,128)(2,1)} %w_ref.3) | copy-start | bytes 25165828
  35.0 11.3 %copy-start.11 = (s32[64]{0:T(128)S(1)}, s32[64]{0:T(128)}, u32[]{:S(2)}) copy-start(s32[64]{0:T(128)} %tags_ref.5) | copy-start | bytes 772
  42.9 20.4 %collective-permute-start.10 = (bf16[1024,256]{1,0:T(8,128)(2,1)S(1)}, bf16[1024,256]{1,0:T(8,128)(2,1)S(1)}, u32[]{:S(2)}, u32[]{:S(2)}) collective-permute-start(bf16[1024,256]{1,0:T(8,128)(2,1)S(1)} %pad_maximum_fusion.refs_0_), channel_id=1, source_target_pairs={{0,64},{2,18},{4,68},{6,22},{8,72},{10,26},{12,76},{14,30},{16,80}... | collective-permute-start | bytes 1572872 | tf_op jit(solution)/shard_map/ppermute | solution.py:450
  43.7 19.6 %collective-permute-start.11 = (bf16[1024,256]{1,0:T(8,128)(2,1)S(1)}, bf16[1024,256]{1,0:T(8,128)(2,1)S(1)}, u32[]{:S(2)}, u32[]{:S(2)}) collective-permute-start(bf16[1024,256]{1,0:T(8,128)(2,1)S(1)} %pad_maximum_fusion.refs_0_), channel_id=1, source_target_pairs={{0,96},{2,26},{4,100},{6,30},{8,104},{10,2},{12,108},{14,6},{16,11... | collective-permute-start | bytes 1572872 | tf_op jit(solution)/shard_map/ppermute | solution.py:450
  45.8 17.6 %collective-permute-start.9 = (bf16[1024,256]{1,0:T(8,128)(2,1)S(1)}, bf16[1024,256]{1,0:T(8,128)(2,1)S(1)}, u32[]{:S(2)}, u32[]{:S(2)}) collective-permute-start(bf16[1024,256]{1,0:T(8,128)(2,1)S(1)} %pad_maximum_fusion.refs_0_), channel_id=1, source_target_pairs={{0,32},{2,10},{4,36},{6,14},{8,40},{10,18},{12,44},{14,22},{16,48}... | collective-permute-start | bytes 1572872 | tf_op jit(solution)/shard_map/ppermute | solution.py:450
  59.0 16.2 %collective-permute-start.12 = (bf16[1024,256]{1,0:T(8,128)(2,1)S(1)}, bf16[1024,256]{1,0:T(8,128)(2,1)S(1)}, u32[]{:S(2)}, u32[]{:S(2)}) collective-permute-start(bf16[1024,256]{1,0:T(8,128)(2,1)S(1)} %get-tuple-element.60), channel_id=1, source_target_pairs={{0,96},{2,26},{4,100},{6,30},{8,104},{10,2},{12,108},{14,6},{16,11... | collective-permute-start | bytes 1572872 | tf_op jit(solution)/shard_map/ppermute | solution.py:450
  62.0 13.2 %collective-permute-start.13 = (bf16[1024,256]{1,0:T(8,128)(2,1)S(1)}, bf16[1024,256]{1,0:T(8,128)(2,1)S(1)}, u32[]{:S(2)}, u32[]{:S(2)}) collective-permute-start(bf16[1024,256]{1,0:T(8,128)(2,1)S(1)} %get-tuple-element.61), channel_id=1, source_target_pairs={{0,64},{2,18},{4,68},{6,22},{8,72},{10,26},{12,76},{14,30},{16,80}... | collective-permute-start | bytes 1572872 | tf_op jit(solution)/shard_map/ppermute | solution.py:450
  63.3 15.0 %slice-start = ((s8[8388608]{0:T(1024)(128)(4,1)}), s8[4194304]{0:T(1024)(128)(4,1)S(1)}, s32[]{:S(2)}) async-start(s8[8388608]{0:T(1024)(128)(4,1)} %bitcast.27), calls=%async_computation | async-start | bytes 8388608
  63.3 15.0 %slice-start.1 = ((s8[8388608]{0:T(1024)(128)(4,1)}), s8[4194304]{0:T(1024)(128)(4,1)S(1)}, s32[]{:S(2)}) async-start(s8[8388608]{0:T(1024)(128)(4,1)} %bitcast.27), calls=%async_computation.1 | async-start | bytes 8388608
  63.3 15.0 %collective-permute-start.14 = (bf16[1024,256]{1,0:T(8,128)(2,1)S(1)}, bf16[1024,256]{1,0:T(8,128)(2,1)S(1)}, u32[]{:S(2)}, u32[]{:S(2)}) collective-permute-start(bf16[1024,256]{1,0:T(8,128)(2,1)S(1)} %get-tuple-element.62), channel_id=1, source_target_pairs={{0,32},{2,10},{4,36},{6,14},{8,40},{10,18},{12,44},{14,22},{16,48}... | collective-permute-start | bytes 1572872 | tf_op jit(solution)/shard_map/ppermute | solution.py:450
  82.1 2.9 %collective-permute-start.15 = (bf16[2,256,1024]{2,1,0:T(8,128)(2,1)S(1)}, bf16[2,256,1024]{2,1,0:T(8,128)(2,1)S(1)}, u32[]{:S(2)}, u32[]{:S(2)}) collective-permute-start(bf16[2,256,1024]{2,1,0:T(8,128)(2,1)S(1)} %get-tuple-element.65), channel_id=1, source_target_pairs={{0,2},{2,0},{4,6},{6,4},{1,3},{3,1},{5,7},{7,5},{8,10},{10,8},{12,... | collective-permute-start | bytes 3145736 | tf_op jit(solution)/shard_map/ppermute | solution.py:454
  82.2 9.2 %collective-permute-start.17 = (bf16[1024,256]{1,0:T(8,128)(2,1)S(1)}, bf16[1024,256]{1,0:T(8,128)(2,1)S(1)}, u32[]{:S(2)}, u32[]{:S(2)}) collective-permute-start(bf16[1024,256]{1,0:T(8,128)(2,1)S(1)} %get-tuple-element.73), channel_id=1, source_target_pairs={{0,96},{2,26},{4,100},{6,30},{8,104},{10,2},{12,108},{14,6},{16,11... | collective-permute-start | bytes 1572872 | tf_op jit(solution)/shard_map/ppermute | solution.py:450
  82.9 10.8 %collective-permute-start.18 = (bf16[1024,256]{1,0:T(8,128)(2,1)S(1)}, bf16[1024,256]{1,0:T(8,128)(2,1)S(1)}, u32[]{:S(2)}, u32[]{:S(2)}) collective-permute-start(bf16[1024,256]{1,0:T(8,128)(2,1)S(1)} %get-tuple-element.74), channel_id=1, source_target_pairs={{0,64},{2,18},{4,68},{6,22},{8,72},{10,26},{12,76},{14,30},{16,80}... | collective-permute-start | bytes 1572872 | tf_op jit(solution)/shard_map/ppermute | solution.py:450
  84.2 15.0 %collective-permute-start.19 = (bf16[1024,256]{1,0:T(8,128)(2,1)S(1)}, bf16[1024,256]{1,0:T(8,128)(2,1)S(1)}, u32[]{:S(2)}, u32[]{:S(2)}) collective-permute-start(bf16[1024,256]{1,0:T(8,128)(2,1)S(1)} %get-tuple-element.75), channel_id=1, source_target_pairs={{0,32},{2,10},{4,36},{6,14},{8,40},{10,18},{12,44},{14,22},{16,48}... | collective-permute-start | bytes 1572872 | tf_op jit(solution)/shard_map/ppermute | solution.py:450
  85.5 29.2 %collective-permute-start.16 = (bf16[256,1024]{1,0:T(8,128)(2,1)S(1)}, bf16[256,1024]{1,0:T(8,128)(2,1)S(1)}, u32[]{:S(2)}, u32[]{:S(2)}) collective-permute-start(bf16[256,1024]{1,0:T(8,128)(2,1)S(1)} %fusion.2), channel_id=1, source_target_pairs={{0,4},{2,6},{4,0},{6,2},{1,5},{3,7},{5,1},{7,3},{8,12},{10,14},{12... | collective-permute-start | bytes 1572872 | tf_op jit(solution)/shard_map/ppermute | solution.py:454
  99.7 13.8 %copy-start.4 = (bf16[256,256]{1,0:T(8,128)(2,1)S(1)}, bf16[256,256]{1,0:T(8,128)(2,1)}, u32[]{:S(2)}) copy-start(bf16[256,256]{1,0:T(8,128)(2,1)} %key_ref.1) | copy-start | bytes 393220
  99.7 13.8 %copy-start.9 = (f32[128]{0:T(128)S(1)}, f32[128]{0:T(128)}, u32[]{:S(2)}) copy-start(f32[128]{0:T(128)} %param.13) | copy-start | bytes 1540
  99.7 9.8 %collective-permute-start.20 = (bf16[2,256,256]{2,1,0:T(8,128)(2,1)S(1)}, bf16[2,256,256]{2,1,0:T(8,128)(2,1)S(1)}, u32[]{:S(2)}, u32[]{:S(2)}) collective-permute-start(bf16[2,256,256]{2,1,0:T(8,128)(2,1)S(1)} %get-tuple-element.77), channel_id=1, source_target_pairs={{0,24},{2,98},{4,28},{6,102},{8,0},{10,106},{12,4},{14,110},{16,8}... | collective-permute-start | bytes 786440 | tf_op jit(solution)/shard_map/ppermute | solution.py:450
  102.9 8.0 %collective-permute-start.21 = (bf16[2,256,256]{2,1,0:T(8,128)(2,1)S(1)}, bf16[2,256,256]{2,1,0:T(8,128)(2,1)S(1)}, u32[]{:S(2)}, u32[]{:S(2)}) collective-permute-start(bf16[2,256,256]{2,1,0:T(8,128)(2,1)S(1)} %get-tuple-element.78), channel_id=1, source_target_pairs={{0,16},{2,66},{4,20},{6,70},{8,24},{10,74},{12,28},{14,78},{16,0},... | collective-permute-start | bytes 786440 | tf_op jit(solution)/shard_map/ppermute | solution.py:450
  103.5 10.0 %collective-permute-start.22 = (bf16[2,256,256]{2,1,0:T(8,128)(2,1)S(1)}, bf16[2,256,256]{2,1,0:T(8,128)(2,1)S(1)}, u32[]{:S(2)}, u32[]{:S(2)}) collective-permute-start(bf16[2,256,256]{2,1,0:T(8,128)(2,1)S(1)} %get-tuple-element.79), channel_id=1, source_target_pairs={{0,8},{2,34},{4,12},{6,38},{8,16},{10,42},{12,20},{14,46},{16,24},... | collective-permute-start | bytes 786440 | tf_op jit(solution)/shard_map/ppermute | solution.py:450
  (5 other events, 4.1 us)

commit v3 on v2

--- a/solution.py
+++ b/solution.py
@@ -27,8 +27,8 @@
     return jax.ShapeDtypeStruct(dims, dtype)
 
 
-def params():
-    return pltpu.CompilerParams(vmem_limit_bytes=LIMIT)
+def params(limit=LIMIT):
+    return pltpu.CompilerParams(vmem_limit_bytes=limit)
 
 
 def cost(flops, nbytes):
@@ -117,7 +117,7 @@
             pltpu.VMEM(table.shape, table.dtype),
             pltpu.SemaphoreType.DMA((3 + heads,)),
         ],
-        compiler_params=params(),
+        compiler_params=params(63 * 1024 * 1024),
         cost_estimate=cost(0, 1 << 20),
         name="key_prep",
     )(tags, keys, values, gain, table)
@@ -135,84 +135,99 @@
     return pl.pallas_call(
         query_kernel,
         grid=(1,),
-        in_specs=[whole(*q_raw.shape), whole(*gain.shape), VMEM, VMEM],
-        out_specs=VMEM,
+        in_specs=[whole(*q_raw.shape), whole(*gain.shape), whole(*cosine.shape), whole(*sine.shape)],
+        out_specs=whole(*q_raw.shape),
         out_shape=shape(q_raw.shape, jnp.bfloat16),
-        compiler_params=params(),
+        compiler_params=params(63 * 1024 * 1024),
         cost_estimate=cost(0, 4 << 20),
         name="query_prep",
     )(q_raw, gain, cosine, sine)
 
 
-def d_attn_kernel(me_ref, p0, p1, p2, p3, w_ref, out_ref, acc):
+def d_attn_kernel(me_ref, p0, p1, p2, p3a, p3b, w_ref, out_ref, acc):
     k = pl.program_id(0)
-    for i, piece in enumerate((p0, p1, p2, p3)):
-
-        @pl.when(k == i)
-        def _(i=i, piece=piece):
-            term = lax.dot_general(piece[...], w_ref[...], (((1,), (1,)), ((), ())), preferred_element_type=jnp.float32)
-            if i == 0:
-                acc[...] = term
-            elif i < 3:
-                acc[...] += term
-            else:
-                out_ref[...] = (acc[...] + term).astype(jnp.bfloat16)
+
+    def product(piece):
+        return lax.dot_general(piece[...], w_ref[...], (((1,), (1,)), ((), ())), preferred_element_type=jnp.float32)
+
+    @pl.when(k == 0)
+    def _():
+        acc[...] = product(p0)
+
+    @pl.when(k == 1)
+    def _():
+        acc[...] += product(p1)
+
+    @pl.when(k == 2)
+    def _():
+        acc[...] += product(p2)
+
+    @pl.when(k == 3)
+    def _():
+        rows = p3a.shape[0]
+        out_ref[:rows] = (acc[:rows] + product(p3a)).astype(jnp.bfloat16)
+        out_ref[rows:] = (acc[rows:] + product(p3b)).astype(jnp.bfloat16)
 
 
 def d_attn_product(me, pieces, w_out):
     tok, width = pieces[0].shape
     feats = w_out.shape[0]
-    whole = lambda k, me: (0, 0)
+    place = lambda k, me: (0, 0)
     return pl.pallas_call(
         d_attn_kernel,
         grid_spec=pltpu.PrefetchScalarGridSpec(
             num_scalar_prefetch=1,
             grid=(4,),
-            in_specs=[pl.BlockSpec((tok, width), whole)] * 4
+            in_specs=[pl.BlockSpec(piece.shape, place) for piece in pieces]
             + [pl.BlockSpec((feats, width), lambda k, me: (0, me[0] ^ k))],
-            out_specs=pl.BlockSpec((tok, feats), whole),
+            out_specs=pl.BlockSpec((tok, feats), place),
             scratch_shapes=[pltpu.VMEM((tok, feats), jnp.float32)],
         ),
         out_shape=shape((tok, feats), jnp.bfloat16),
         compiler_params=params(),
-        cost_estimate=cost(2 * tok * feats * width * 4, 12 << 20),
+        cost_estimate=cost(1, 1),
         name="d_attn_product",
     )(me, *pieces, w_out)
 
 
-def out_kernel(me_ref, a0_ref, a1_ref, w_ref, send_ref, keep_ref):
+def out_kernel(me_ref, a0_ref, a1_ref, w_ref, far_a, far_b, keep_far, near, keep_near):
     k = pl.program_id(0)
     half = a0_ref.shape[1]
     term = jnp.dot(a0_ref[...], w_ref[0:half, :], preferred_element_type=jnp.float32)
     term += jnp.dot(a1_ref[...], w_ref[half:, :], preferred_element_type=jnp.float32)
-
-    @pl.when(k < 2)
+    term = term.astype(jnp.bfloat16)
+    rows = far_a.shape[0]
+
+    @pl.when(k == 0)
     def _():
-        send_ref[pl.ds(k, 1)] = term.astype(jnp.bfloat16)[None]
-
-    @pl.when(k >= 2)
-    def _():
-        keep_ref[pl.ds(k - 2, 1)] = term.astype(jnp.bfloat16)[None]
+        far_a[...] = term[:rows]
+        far_b[...] = term[rows:]
+
+    for i, out in enumerate((keep_far, near, keep_near)):
+
+        @pl.when(k == i + 1)
+        def _(out=out):
+            out[...] = term
 
 
 def out_product(me, a0, a1, w_out):
     tok = a0.shape[0]
     feats, wide = w_out.shape
     width = wide // 4
-    whole = lambda k, me: (0, 0)
-    pair = lambda k, me: (0, 0, 0)
+    place = lambda k, me: (0, 0)
+    dims = [(tok // 2, width)] * 2 + [(tok, width)] * 3
     return pl.pallas_call(
         out_kernel,
         grid_spec=pltpu.PrefetchScalarGridSpec(
             num_scalar_prefetch=1,
             grid=(4,),
-            in_specs=[pl.BlockSpec(a0.shape, whole)] * 2
-            + [pl.BlockSpec((feats, width), lambda k, me: (0, me[0] ^ (2 * (k % 2) + 1 - k // 2)))],
-            out_specs=[pl.BlockSpec((2, tok, width), pair)] * 2,
+            in_specs=[pl.BlockSpec(a0.shape, place)] * 2
+            + [pl.BlockSpec((feats, width), lambda k, me: (0, me[0] ^ (3 - k)))],
+            out_specs=[pl.BlockSpec(d, place) for d in dims],
         ),
-        out_shape=[shape((2, tok, width), jnp.bfloat16)] * 2,
+        out_shape=[shape(d, jnp.bfloat16) for d in dims],
         compiler_params=params(),
-        cost_estimate=cost(2 * tok * feats * wide, 12 << 20),
+        cost_estimate=cost(1, 1),
         name="out_product",
     )(me, a0, a1, w_out)
 
@@ -282,19 +297,29 @@
         do = gather(do_ref, j)
         do_t = do.astype(jnp.float32).T
 
+        for c in range(nclean // WIDE):
+            st[c] = lax.dot_general(chunk(ks, c), q, (((1,), (1,)), ((), ())), preferred_element_type=jnp.float32)
+        hidden = [jnp.where(i > index, NEG, 0.0).astype(jnp.float32) for i in range(nclean)]
         top = jnp.full((8, rows), NEG, jnp.float32)
         for c in range(nclean // WIDE):
-            s = lax.dot_general(chunk(ks, c), q, (((1,), (1,)), ((), ())), preferred_element_type=jnp.float32)
             for i in range(WIDE):
-                part = s[i * BLK : (i + 1) * BLK] * SCALE2
-                part = part + jnp.where(WIDE * c + i > index, NEG, 0.0).astype(jnp.float32)
-                st[c, i * BLK : (i + 1) * BLK, :] = part
-                top = jnp.maximum(top, jnp.max(part.reshape(BLK // 8, 8, rows), axis=0))
-        top = jnp.max(top, axis=0, keepdims=True)
+                part = jnp.max(st[c, i * BLK : (i + 1) * BLK, :].reshape(BLK // 8, 8, rows), axis=0)
+                top = jnp.maximum(top, part + hidden[WIDE * c + i])
+        top = jnp.max(top, axis=0, keepdims=True) * SCALE2
+
+        def weight(c, shift):
+            return jnp.concatenate(
+                [
+                    jnp.exp2(st[c, i * BLK : (i + 1) * BLK, :] * SCALE2 + (hidden[WIDE * c + i] - shift))
+                    for i in range(WIDE)
+                ],
+                axis=0,
+            )
+
         total = jnp.zeros((8, rows), jnp.float32)
         acc = jnp.zeros((HEAD, rows), jnp.float32)
         for c in range(nclean // WIDE):
-            e = jnp.exp2(st[c] - top)
+            e = weight(c, top)
             total = total + jnp.sum(e.reshape(wide // 8, 8, rows), axis=0)
             acc = acc + jnp.dot(chunk_t(vt, c), e.astype(jnp.bfloat16), preferred_element_type=jnp.float32)
         total = jnp.sum(total, axis=0, keepdims=True)
@@ -306,7 +331,7 @@
         top = top + jnp.log2(total)
         acc = jnp.zeros((HEAD, rows), jnp.float32)
         for c in range(nclean // WIDE):
-            p = jnp.exp2(st[c] - top)
+            p = weight(c, top)
             dp = lax.dot_general(chunk(vs, c), do, (((1,), (1,)), ((), ())), preferred_element_type=jnp.float32)
             ds = (p * (dp - delta)).astype(jnp.bfloat16)
             dvc = jnp.dot(p.astype(jnp.bfloat16), do, preferred_element_type=jnp.float32)
@@ -385,12 +410,14 @@
         out_specs=whole(*q_raw.shape),
         out_shape=shape(q_raw.shape, jnp.float32),
         compiler_params=params(),
-        cost_estimate=cost(0, 8 << 20),
+        cost_estimate=cost(1, 1),
         name="query_back",
     )(q_raw, dq0, dq1, gain, cosine, sine)
 
 
-def key_back_kernel(key_ref, gain_ref, cos_ref, sin_ref, a, b, c, d, dk_ref, dv_ref):
+def finish_kernel(key_ref, gain_ref, cos_ref, sin_ref, a, b, c, d, keep, near, far, out_ref, dk_ref, dv_ref):
+    out = keep[...].astype(jnp.float32) + near[...].astype(jnp.float32) + far[...].astype(jnp.float32)
+    out_ref[...] = out.astype(jnp.bfloat16)
     gain, cosine, sine = gain_ref[...], cos_ref[...], sin_ref[...]
     for g in range(a.shape[0]):
         cols = slice(g * HEAD, (g + 1) * HEAD)
@@ -401,17 +428,17 @@
         dv_ref[:, cols] = total[:, HEAD:]
 
 
-def key_back(keys, gain, cosine, sine, parts):
-    return pl.pallas_call(
-        key_back_kernel,
+def finish(keys, gain, cosine, sine, parts, terms):
+    return pl.pallas_call(
+        finish_kernel,
         grid=(1,),
-        in_specs=[whole(*keys.shape), whole(*gain.shape)] + [VMEM] * 6,
-        out_specs=[whole(*keys.shape)] * 2,
-        out_shape=[shape(keys.shape, jnp.float32)] * 2,
+        in_specs=[whole(*keys.shape), whole(*gain.shape)] + [VMEM] * 9,
+        out_specs=[whole(*terms[0].shape)] + [whole(*keys.shape)] * 2,
+        out_shape=[shape(terms[0].shape, jnp.bfloat16)] + [shape(keys.shape, jnp.float32)] * 2,
         compiler_params=params(),
         cost_estimate=cost(0, 2 << 20),
-        name="key_back",
-    )(keys, gain, cosine, sine, *parts)
+        name="finish",
+    )(keys, gain, cosine, sine, *parts, *terms)
 
 
 def fold_kernel(*refs):
@@ -472,14 +499,17 @@
 
     kv, cosine, sine = key_prep(block_tags, keys, values, k_gain, table, heads)
     near = spread(kv, 0)
+    q = query_prep(q_raw, q_gain, cosine, sine)
+    lines = [jnp.concatenate([part[g] for part in near], axis=0) for g in range(heads)]
+    lines[0], q = lax.optimization_barrier((lines[0], q))
     far = across(d_out, 2)
-    d_pieces = [d_out, across(d_out, 1), far, across(far, 1)]
-    q = query_prep(q_raw, q_gain, cosine, sine)
+    half = far.shape[0] // 2
+    d_pieces = [d_out, across(d_out, 1), far, across(far[:half], 1), across(far[half:], 1)]
     do = d_attn_product(me, d_pieces, w_out)
 
     pieces = []
     for g in range(heads):
-        line = jnp.concatenate([part[g] for part in near], axis=0)
+        line = lines[g]
         if g:
             line, do, pieces[g - 1] = lax.optimization_barrier((line, do, pieces[g - 1]))
         pieces.append(spread(line, 1))
@@ -493,14 +523,14 @@
         attn.append(attn_g)
         dq.append(dq_g)
         sums.append(collect(grads, 1))
-    parts = collect(fold(sums), 0)
-
-    send, keep = out_product(me, attn[0], attn[1], w_out)
-    summed = keep.astype(jnp.float32) + across(send, 1).astype(jnp.float32)
-    other = across(summed[1].astype(jnp.bfloat16), 2)
-    attn_out = (summed[0] + other.astype(jnp.float32)).astype(jnp.bfloat16)
+    far_a, far_b, keep_far, near, keep_near = out_product(me, attn[0], attn[1], w_out)
+    far = jnp.concatenate([across(far_a, 1), across(far_b, 1)], axis=0)
+    far = (keep_far.astype(jnp.float32) + far.astype(jnp.float32)).astype(jnp.bfloat16)
+    shares, far, near = lax.optimization_barrier((fold(sums), far, near))
+    parts = collect(shares, 0)
+    terms = [keep_near, across(near, 1), across(far, 2)]
     d_q = query_back(q_raw, dq[0], dq[1], q_gain, cosine, sine)
-    key_gradient, value_gradient = key_back(keys, k_gain, cosine, sine, parts)
+    attn_out, key_gradient, value_gradient = finish(keys, k_gain, cosine, sine, parts, terms)
     return attn_out, d_q, key_gradient, value_gradient
 
 

time: 116 us -> 105 us (0.905)
  waiting for transfers between devices: 39.1 us -> 24.6 us
  Pallas kernels: 38.4 us -> 42.9 us
  other arithmetic: 2.44 us -> 0.26 us
  starting transfers between devices: 25.3 us -> 26.9 us
    ppermute x18, waiting for transfers between devices: 32.3 us -> 20.4 us  [hop(): return lax.ppermute(value, ('ctx', 'ffn'), pairs)]
    unnamed x28 -> x24, local copies, waits for them, and re-layouts: 7.47 us -> 4.48 us
    ppermute x5 -> x8, waiting for transfers between devices: 6.82 us -> 4.2 us  [across(): return lax.ppermute(value, 'ffn', [(s, s ^ mask) for s in range(4)])]
    pallas_call x1, Pallas kernels: 1.14 us -> 3.06 us  [query_prep(): pl.pallas_call(query_kernel, grid=(1,), in_specs=[whole(*q_raw.shape), wh...]
    squeeze x4, local copies, waits for them, and re-layouts: 2.04 us -> 3.94 us  [per_device(): part[g]]
    pallas_call x1, Pallas kernels: 3.66 us -> 5.35 us  [d_attn_product(): pl.pallas_call(d_attn_kernel, grid_spec=pltpu.PrefetchScalarGridSpec(num_...]
    pallas_call x1, Pallas kernels: 1.45 us -> 3.01 us  [key_prep(): pl.pallas_call(functools.partial(key_kernel, blocks=blocks), in_specs=[SM...]
  transfers between devices with their start and end apart: 23 -> 26, of which waited for: 12 -> 14; matrix products, arithmetic and copies ran while one was open for 3% -> 4% of each run, Pallas kernels for 29% -> 36%
where the time goes in v3:
time: 105 us; the launch traced here: 104 us
  Pallas kernels  42.9 us (41%)
  starting transfers between devices  26.9 us (26%)
  waiting for transfers between devices  24.6 us (23%)
  local copies, waits for them, and re-layouts  8.45 us (8%)
    ppermute x18, starting transfers between devices, hop(): return lax.ppermute(value, ('ctx', 'ffn'), pairs)  24.7 us
    pallas_call x2, Pallas kernels, attention(): pl.pallas_call(functools.partial(attention_kernel, first=g * group, nclea...  23.4 us
    ppermute x18, waiting for transfers between devices, hop(): return lax.ppermute(value, ('ctx', 'ffn'), pairs)  20.4 us
    pallas_call x1, Pallas kernels, d_attn_product(): pl.pallas_call(d_attn_kernel, grid_spec=pltpu.PrefetchScalarGridSpec(num_...  5.35 us
    unnamed x24, local copies, waits for them, and re-layouts  4.48 us
    ppermute x8, waiting for transfers between devices, across(): return lax.ppermute(value, 'ffn', [(s, s ^ mask) for s in range(4)])  4.2 us
    squeeze x4, local copies, waits for them, and re-layouts, per_device(): part[g]  3.94 us
    pallas_call x1, Pallas kernels, out_product(): pl.pallas_call(out_kernel, grid_spec=pltpu.PrefetchScalarGridSpec(num_sca...  3.71 us
  transfers between devices with their start and end apart: 26, of which 14 were waited for; matrix products, arithmetic and copies ran while one was open for 4% of the time, Pallas kernels for 36%

profile of v3, /device:TPU:96, one launch (start us, length us, event | category | flops | bytes accessed | tf_op | source)
XLA Modules:
  0.0 103.9 jit_solution(2493691440843243535)
XLA Ops:
  0.6 3.0 %key_prep.1 = (bf16[2,256,256]{2,1,0:T(8,128)(2,1)}, f32[256,128]{1,0:T(8,128)}, f32[256,128]{1,0:T(8,128)}) custom-call(s32[64]{0:T(128)} %tags_ref.5, bf16[256,256]{1,0:T(8,128)(2,1)} %key_ref.1, bf16[256,256]{1,0:T(8,128)(2,1)} %value_hbm.1, f32[1,128]{1,0:T(1,128)} %bitcast.23, f32[192,128]{1,0:T(8,128)} %constant.8.clone.table_hbm), custom_call_target="tpu_custom_call" | custom-call | bytes 1048576 | tf_op jit(solution)/shard_map/key_prep/pallas_call | solution.py:109
  3.6 2.8 %collective-permute-start.2 = (bf16[2,256,256]{2,1,0:T(8,128)(2,1)}, bf16[2,256,256]{2,1,0:T(8,128)(2,1)}, u32[]{:S(2)}, u32[]{:S(2)}) collective-permute-start(bf16[2,256,256]{2,1,0:T(8,128)(2,1)} %get-tuple-element.57), channel_id=1, source_target_pairs={{0,24},{2,98},{4,28},{6,102},{8,0},{10,106},{12,4},{14,110},{16,8}... | collective-permute-start | bytes 786440 | tf_op jit(solution)/shard_map/ppermute | solution.py:477
  9.6 3.1 %query_prep.1.q_ref = bf16[256,1024]{1,0:T(8,128)(2,1)} custom-call(bf16[256,1024]{1,0:T(8,128)(2,1)} %q_ref.3, f32[1,128]{1,0:T(1,128)} %bitcast.21, f32[256,128]{1,0:T(8,128)} %get-tuple-element.55.cos_ref, f32[256,128]{1,0:T(8,128)} %get-tuple-element.56.sin_ref), custom_call_target="tpu_custom_call" | custom-call | bytes 4194304 | tf_op jit(solution)/shard_map/query_prep/pallas_call | solution.py:135
  14.8 1.0 slice_bitcast_fusion.1
  15.8 1.7 %collective-permute-done = bf16[2,256,256]{2,1,0:T(8,128)(2,1)} collective-permute-done((bf16[2,256,256]{2,1,0:T(8,128)(2,1)}, bf16[2,256,256]{2,1,0:T(8,128)(2,1)}, u32[]{:S(2)}, u32[]{:S(2)}) %collective-permute-start) | collective-permute-done | bytes 262176 | tf_op jit(solution)/shard_map/ppermute | solution.py:477
  17.5 1.0 slice_bitcast_fusion.2
  18.5 1.6 %collective-permute-start.7 = (bf16[1024,256]{1,0:T(8,128)(2,1)S(1)}, bf16[1024,256]{1,0:T(8,128)(2,1)}, u32[]{:S(2)}, u32[]{:S(2)}) collective-permute-start(bf16[1024,256]{1,0:T(8,128)(2,1)S(1)} %pad_maximum_fusion.refs_0_), channel_id=1, source_target_pairs={{0,32},{2,10},{4,36},{6,14},{8,40},{10,18},{12,44},{14,22},{16,48}... | collective-permute-start | bytes 1572872 | tf_op jit(solution)/shard_map/ppermute | solution.py:477
  20.2 2.9 %collective-permute-start.8 = (bf16[1024,256]{1,0:T(8,128)(2,1)S(1)}, bf16[1024,256]{1,0:T(8,128)(2,1)}, u32[]{:S(2)}, u32[]{:S(2)}) collective-permute-start(bf16[1024,256]{1,0:T(8,128)(2,1)S(1)} %pad_maximum_fusion.refs_0_), channel_id=1, source_target_pairs={{0,64},{2,18},{4,68},{6,22},{8,72},{10,26},{12,76},{14,30},{16,80}... | collective-permute-start | bytes 1572872 | tf_op jit(solution)/shard_map/ppermute | solution.py:477
  23.1 1.3 %collective-permute-start.9 = (bf16[1024,256]{1,0:T(8,128)(2,1)S(1)}, bf16[1024,256]{1,0:T(8,128)(2,1)}, u32[]{:S(2)}, u32[]{:S(2)}) collective-permute-start(bf16[1024,256]{1,0:T(8,128)(2,1)S(1)} %pad_maximum_fusion.refs_0_), channel_id=1, source_target_pairs={{0,96},{2,26},{4,100},{6,30},{8,104},{10,2},{12,108},{14,6},{16,11... | collective-permute-start | bytes 1572872 | tf_op jit(solution)/shard_map/ppermute | solution.py:477
  26.4 3.4 %copy-done = bf16[1024,4096]{1,0:T(8,128)(2,1)S(1)} copy-done((bf16[1024,4096]{1,0:T(8,128)(2,1)S(1)}, bf16[1024,4096]{1,0:T(8,128)(2,1)}, u32[]{:S(2)}) %copy-start) | copy-done | bytes 8388632
  29.8 1.0 %copy-done.4 = bf16[256,1024]{1,0:T(8,128)(2,1)S(1)} copy-done((bf16[256,1024]{1,0:T(8,128)(2,1)S(1)}, bf16[256,1024]{1,0:T(8,128)(2,1)}, u32[]{:S(2)}) %copy-start.4) | copy-done | bytes 524312
  30.9 5.3 %d_attn_product.1.do_ref = bf16[256,1024]{1,0:T(8,128)(2,1)S(1)} custom-call(s32[1]{0:T(128)} %bitcast.10.me_ref, bf16[256,1024]{1,0:T(8,128)(2,1)S(1)} %copy-done.4, bf16[256,1024]{1,0:T(8,128)(2,1)} %collective-permute-done.3.p1, bf16[256,1024]{1,0:T(8,128)(2,1)S(1)} %collective-permute-done.4.p2, bf16[128,1024]{1,0:T(8,128)(2,1)S(1)} %collective-permute-done.5.p3a, ...), custom_call_target="tpu_custom_call" | custom-call | flops 1 | bytes 1 | tf_op jit(solution)/shard_map/d_attn_product/pallas_call | solution.py:176
  36.3 1.3 %collective-permute-start.10 = (bf16[1024,256]{1,0:T(8,128)(2,1)S(1)}, bf16[1024,256]{1,0:T(8,128)(2,1)S(1)}, u32[]{:S(2)}, u32[]{:S(2)}) collective-permute-start(bf16[1024,256]{1,0:T(8,128)(2,1)S(1)} %pad_maximum_fusion.1.refs_0_), channel_id=1, source_target_pairs={{0,32},{2,10},{4,36},{6,14},{8,40},{10,18},{12,44},{14,22},{16,48}... | collective-permute-start | bytes 1572872 | tf_op jit(solution)/shard_map/ppermute | solution.py:477
  37.6 2.1 %collective-permute-start.11 = (bf16[1024,256]{1,0:T(8,128)(2,1)S(1)}, bf16[1024,256]{1,0:T(8,128)(2,1)S(1)}, u32[]{:S(2)}, u32[]{:S(2)}) collective-permute-start(bf16[1024,256]{1,0:T(8,128)(2,1)S(1)} %pad_maximum_fusion.1.refs_0_), channel_id=1, source_target_pairs={{0,64},{2,18},{4,68},{6,22},{8,72},{10,26},{12,76},{14,30},{16,80}... | collective-permute-start | bytes 1572872 | tf_op jit(solution)/shard_map/ppermute | solution.py:477
  39.7 1.7 %collective-permute-start.12 = (bf16[1024,256]{1,0:T(8,128)(2,1)S(1)}, bf16[1024,256]{1,0:T(8,128)(2,1)S(1)}, u32[]{:S(2)}, u32[]{:S(2)}) collective-permute-start(bf16[1024,256]{1,0:T(8,128)(2,1)S(1)} %pad_maximum_fusion.1.refs_0_), channel_id=1, source_target_pairs={{0,96},{2,26},{4,100},{6,30},{8,104},{10,2},{12,108},{14,6},{16,11... | collective-permute-start | bytes 1572872 | tf_op jit(solution)/shard_map/ppermute | solution.py:477
  41.4 12.1 %attention.3 = (bf16[256,512]{1,0:T(8,128)(2,1)S(1)}, f32[256,512]{1,0:T(8,128)S(1)}, bf16[1024,256]{1,0:T(8,128)(2,1)S(1)}, bf16[1024,256]{1,0:T(8,128)(2,1)S(1...) custom-call(s32[64]{0:T(128)S(1)} %copy-done.9, bf16[256,1024]{1,0:T(8,128)(2,1)S(1)} %copy-done.5, ...), custom_call_target="tpu_custom_call" | custom-call | flops 6442450944 | bytes 4194304 | tf_op jit(solution)/shard_map/attention/pallas_call | solution.py:372
  53.9 2.0 %collective-permute-start.14 = (bf16[1024,256]{1,0:T(8,128)(2,1)S(1)}, bf16[1024,256]{1,0:T(8,128)(2,1)S(1)}, u32[]{:S(2)}, u32[]{:S(2)}) collective-permute-start(bf16[1024,256]{1,0:T(8,128)(2,1)S(1)} %get-tuple-element.74), channel_id=1, source_target_pairs={{0,64},{2,18},{4,68},{6,22},{8,72},{10,26},{12,76},{14,30},{16,80}... | collective-permute-start | bytes 1572872 | tf_op jit(solution)/shard_map/ppermute | solution.py:477
  56.4 11.3 %attention.2 = (bf16[256,512]{1,0:T(8,128)(2,1)S(1)}, f32[256,512]{1,0:T(8,128)S(1)}, bf16[1024,256]{1,0:T(8,128)(2,1)S(1)}, bf16[1024,256]{1,0:T(8,128)(2,1)S(1...) custom-call(s32[64]{0:T(128)S(1)} %copy-done.9, bf16[256,1024]{1,0:T(8,128)(2,1)S(1)} %copy-done.5, ...), custom_call_target="tpu_custom_call" | custom-call | flops 6442450944 | bytes 4194304 | tf_op jit(solution)/shard_map/attention/pallas_call | solution.py:372
  67.8 2.4 %collective-permute-done.15.refs_3_ = bf16[1024,256]{1,0:T(8,128)(2,1)S(1)} collective-permute-done((bf16[1024,256]{1,0:T(8,128)(2,1)S(1)}, bf16[1024,256]{1,0:T(8,128)(2,1)S(1)}, u32[]{:S(2)}, u32[]{:S(2)}) %collective-permute-start.15) | collective-permute-done | bytes 524320 | tf_op jit(solution)/shard_map/ppermute | solution.py:477
  71.1 1.7 %collective-permute-start.17 = (bf16[1024,256]{1,0:T(8,128)(2,1)S(1)}, bf16[1024,256]{1,0:T(8,128)(2,1)S(1)}, u32[]{:S(2)}, u32[]{:S(2)}) collective-permute-start(bf16[1024,256]{1,0:T(8,128)(2,1)S(1)} %get-tuple-element.82), channel_id=1, source_target_pairs={{0,64},{2,18},{4,68},{6,22},{8,72},{10,26},{12,76},{14,30},{16,80}... | collective-permute-start | bytes 1572872 | tf_op jit(solution)/shard_map/ppermute | solution.py:477
  73.6 3.7 %out_product.1 = (bf16[128,1024]{1,0:T(8,128)(2,1)S(1)}, bf16[128,1024]{1,0:T(8,128)(2,1)S(1)}, bf16[256,1024]{1,0:T(8,128)(2,1)S(1)}, bf16[256,1024]{1,0:T(8,128)(2,1)S(1)}, bf16[256,1024]{1,0:T(8,128)(2,1)S(1)}) custom-call(s32[1]{0:T(128)} %bitcast.10.me_ref, bf16[256,512]{1,0:T(8,128)(2,1)S(1)} %get-tuple-element.88.a0_ref, ...), custom_call_target="tpu_custom_call" | custom-call | flops 1 | bytes 1 | tf_op jit(solution)/shard_map/out_product/pallas_call | solution.py:219
  77.9 1.0 collective-permute-done.20
  79.6 2.4 %collective-permute-done.17.refs_6_ = bf16[1024,256]{1,0:T(8,128)(2,1)S(1)} collective-permute-done((bf16[1024,256]{1,0:T(8,128)(2,1)S(1)}, bf16[1024,256]{1,0:T(8,128)(2,1)S(1)}, u32[]{:S(2)}, u32[]{:S(2)}) %collective-permute-start.17) | collective-permute-done | bytes 524320 | tf_op jit(solution)/shard_map/ppermute | solution.py:477
  81.9 5.5 %collective-permute-done.18.refs_7_ = bf16[1024,256]{1,0:T(8,128)(2,1)S(1)} collective-permute-done((bf16[1024,256]{1,0:T(8,128)(2,1)S(1)}, bf16[1024,256]{1,0:T(8,128)(2,1)S(1)}, u32[]{:S(2)}, u32[]{:S(2)}) %collective-permute-start.18) | collective-permute-done | bytes 524320 | tf_op jit(solution)/shard_map/ppermute | solution.py:477
  88.5 1.7 %collective-permute-start.21 = (bf16[2,256,256]{2,1,0:T(8,128)(2,1)S(1)}, bf16[2,256,256]{2,1,0:T(8,128)(2,1)S(1)}, u32[]{:S(2)}, u32[]{:S(2)}) collective-permute-start(bf16[2,256,256]{2,1,0:T(8,128)(2,1)S(1)} %get-tuple-element.95), channel_id=1, source_target_pairs={{0,24},{2,98},{4,28},{6,102},{8,0},{10,106},{12,4},{14,110},{16,8}... | collective-permute-start | bytes 786440 | tf_op jit(solution)/shard_map/ppermute | solution.py:477
  90.3 1.2 %collective-permute-start.22 = (bf16[2,256,256]{2,1,0:T(8,128)(2,1)S(1)}, bf16[2,256,256]{2,1,0:T(8,128)(2,1)S(1)}, u32[]{:S(2)}, u32[]{:S(2)}) collective-permute-start(bf16[2,256,256]{2,1,0:T(8,128)(2,1)S(1)} %get-tuple-element.96), channel_id=1, source_target_pairs={{0,16},{2,66},{4,20},{6,70},{8,24},{10,74},{12,28},{14,78},{16,0},... | collective-permute-start | bytes 786440 | tf_op jit(solution)/shard_map/ppermute | solution.py:477
  91.5 2.2 %query_back.1 = f32[256,1024]{1,0:T(8,128)} custom-call(bf16[256,1024]{1,0:T(8,128)(2,1)S(1)} %copy-done.1, f32[256,512]{1,0:T(8,128)S(1)} %get-tuple-element.102.a_ref, f32[256,512]{1,0:T(8,128)S(1)} %get-tuple-element.103.b_ref, f32[1,128]{1,0:T(1,128)S(1)} %bitcast.22, f32[256,128]{1,0:T(8,128)S(1)} %copy-done.2, f32[256,128]{1,0:T(8,128)S(1)} %copy-done.3), custom_call_target="tpu_custom_call" | custom-call | flops 1 | bytes 1 | tf_op jit(solution)/shard_map/query_back/pallas_call | solution.py:406
  93.7 1.2 %collective-permute-done.21.b = bf16[2,256,256]{2,1,0:T(8,128)(2,1)S(1)} collective-permute-done((bf16[2,256,256]{2,1,0:T(8,128)(2,1)S(1)}, bf16[2,256,256]{2,1,0:T(8,128)(2,1)S(1)}, u32[]{:S(2)}, u32[]{:S(2)}) %collective-permute-start.21) | collective-permute-done | bytes 262176 | tf_op jit(solution)/shard_map/ppermute | solution.py:477
  94.9 3.3 %collective-permute-done.22.c = bf16[2,256,256]{2,1,0:T(8,128)(2,1)S(1)} collective-permute-done((bf16[2,256,256]{2,1,0:T(8,128)(2,1)S(1)}, bf16[2,256,256]{2,1,0:T(8,128)(2,1)S(1)}, u32[]{:S(2)}, u32[]{:S(2)}) %collective-permute-start.22) | collective-permute-done | bytes 262176 | tf_op jit(solution)/shard_map/ppermute | solution.py:477
  98.2 2.7 %collective-permute-done.23.d = bf16[2,256,256]{2,1,0:T(8,128)(2,1)S(1)} collective-permute-done((bf16[2,256,256]{2,1,0:T(8,128)(2,1)S(1)}, bf16[2,256,256]{2,1,0:T(8,128)(2,1)S(1)}, u32[]{:S(2)}, u32[]{:S(2)}) %collective-permute-start.23) | collective-permute-done | bytes 262176 | tf_op jit(solution)/shard_map/ppermute | solution.py:477
  101.0 1.4 %collective-permute-done.25.far = bf16[256,1024]{1,0:T(8,128)(2,1)S(1)} collective-permute-done((bf16[256,1024]{1,0:T(8,128)(2,1)S(1)}, bf16[256,1024]{1,0:T(8,128)(2,1)S(1)}, u32[]{:S(2)}, u32[]{:S(2)}) %collective-permute-start.25) | collective-permute-done | bytes 524320 | tf_op jit(solution)/shard_map/ppermute | solution.py:481
  102.4 1.6 %finish.1 = (bf16[256,1024]{1,0:T(8,128)(2,1)}, f32[256,256]{1,0:T(8,128)}, f32[256,256]{1,0:T(8,128)}) custom-call(bf16[256,256]{1,0:T(8,128)(2,1)S(1)} %copy-done.6, f32[1,128]{1,0:T(1,128)S(1)} %bitcast.24, f32[256,128]{1,0:T(8,128)S(1)} %copy-done.2, f32[256,128]{1,0:T(8,128)S(1)} %copy-done.3, bf16[2,256,256]{2,1,0:T(8,128)(2,1)S(1)} %get-tuple-element.94.a, ...), custom_call_target="tpu_custom_call" | custom-call | bytes 2097152 | tf_op jit(solution)/shard_map/finish/pallas_call | solution.py:432
  (62 shorter events, 12.1 us)
Async XLA Ops:
  3.6 9.9 %collective-permute-start.2 = (bf16[2,256,256]{2,1,0:T(8,128)(2,1)}, bf16[2,256,256]{2,1,0:T(8,128)(2,1)}, u32[]{:S(2)}, u32[]{:S(2)}) collective-permute-start(bf16[2,256,256]{2,1,0:T(8,128)(2,1)} %get-tuple-element.57), channel_id=1, source_target_pairs={{0,24},{2,98},{4,28},{6,102},{8,0},{10,106},{12,4},{14,110},{16,8}... | collective-permute-start | bytes 786440 | tf_op jit(solution)/shard_map/ppermute | solution.py:477
  6.5 8.3 %collective-permute-start.1 = (bf16[2,256,256]{2,1,0:T(8,128)(2,1)}, bf16[2,256,256]{2,1,0:T(8,128)(2,1)}, u32[]{:S(2)}, u32[]{:S(2)}) collective-permute-start(bf16[2,256,256]{2,1,0:T(8,128)(2,1)} %get-tuple-element.57), channel_id=1, source_target_pairs={{0,16},{2,66},{4,20},{6,70},{8,24},{10,74},{12,28},{14,78},{16,0},... | collective-permute-start | bytes 786440 | tf_op jit(solution)/shard_map/ppermute | solution.py:477
  7.3 10.2 %collective-permute-start = (bf16[2,256,256]{2,1,0:T(8,128)(2,1)}, bf16[2,256,256]{2,1,0:T(8,128)(2,1)}, u32[]{:S(2)}, u32[]{:S(2)}) collective-permute-start(bf16[2,256,256]{2,1,0:T(8,128)(2,1)} %get-tuple-element.57), channel_id=1, source_target_pairs={{0,8},{2,34},{4,12},{6,38},{8,16},{10,42},{12,20},{14,46},{16,24},... | collective-permute-start | bytes 786440 | tf_op jit(solution)/shard_map/ppermute | solution.py:477
  8.2 16.4 %collective-permute-start.3 = (bf16[256,1024]{1,0:T(8,128)(2,1)}, bf16[256,1024]{1,0:T(8,128)(2,1)}, u32[]{:S(2)}, u32[]{:S(2)}) collective-permute-start(bf16[256,1024]{1,0:T(8,128)(2,1)} %p0.1), channel_id=1, source_target_pairs={{0,2},{2,0},{4,6},{6,4},{1,3},{3,1},{5,7},{7,5},{8,10},{10,8},{12,... | collective-permute-start | bytes 1572872 | tf_op jit(solution)/shard_map/ppermute | solution.py:481
  8.2 16.2 %collective-permute-start.4 = (bf16[256,1024]{1,0:T(8,128)(2,1)}, bf16[256,1024]{1,0:T(8,128)(2,1)S(1)}, u32[]{:S(2)}, u32[]{:S(2)}) collective-permute-start(bf16[256,1024]{1,0:T(8,128)(2,1)} %p0.1), channel_id=1, source_target_pairs={{0,4},{2,6},{4,0},{6,2},{1,5},{3,7},{5,1},{7,3},{8,12},{10,14},{12... | collective-permute-start | bytes 1572872 | tf_op jit(solution)/shard_map/ppermute | solution.py:481
  9.6 31.9 %copy-start.9 = (s32[64]{0:T(128)S(1)}, s32[64]{0:T(128)}, u32[]{:S(2)}) copy-start(s32[64]{0:T(128)} %tags_ref.5) | copy-start | bytes 772
  12.6 28.8 %copy-start.5 = (bf16[256,1024]{1,0:T(8,128)(2,1)S(1)}, bf16[256,1024]{1,0:T(8,128)(2,1)}, u32[]{:S(2)}) copy-start(bf16[256,1024]{1,0:T(8,128)(2,1)} %query_prep.1.q_ref) | copy-start | bytes 1572868
  18.5 17.7 %collective-permute-start.7 = (bf16[1024,256]{1,0:T(8,128)(2,1)S(1)}, bf16[1024,256]{1,0:T(8,128)(2,1)}, u32[]{:S(2)}, u32[]{:S(2)}) collective-permute-start(bf16[1024,256]{1,0:T(8,128)(2,1)S(1)} %pad_maximum_fusion.refs_0_), channel_id=1, source_target_pairs={{0,32},{2,10},{4,36},{6,14},{8,40},{10,18},{12,44},{14,22},{16,48}... | collective-permute-start | bytes 1572872 | tf_op jit(solution)/shard_map/ppermute | solution.py:477
  20.2 16.1 %collective-permute-start.8 = (bf16[1024,256]{1,0:T(8,128)(2,1)S(1)}, bf16[1024,256]{1,0:T(8,128)(2,1)}, u32[]{:S(2)}, u32[]{:S(2)}) collective-permute-start(bf16[1024,256]{1,0:T(8,128)(2,1)S(1)} %pad_maximum_fusion.refs_0_), channel_id=1, source_target_pairs={{0,64},{2,18},{4,68},{6,22},{8,72},{10,26},{12,76},{14,30},{16,80}... | collective-permute-start | bytes 1572872 | tf_op jit(solution)/shard_map/ppermute | solution.py:477
  23.1 13.2 %collective-permute-start.9 = (bf16[1024,256]{1,0:T(8,128)(2,1)S(1)}, bf16[1024,256]{1,0:T(8,128)(2,1)}, u32[]{:S(2)}, u32[]{:S(2)}) collective-permute-start(bf16[1024,256]{1,0:T(8,128)(2,1)S(1)} %pad_maximum_fusion.refs_0_), channel_id=1, source_target_pairs={{0,96},{2,26},{4,100},{6,30},{8,104},{10,2},{12,108},{14,6},{16,11... | collective-permute-start | bytes 1572872 | tf_op jit(solution)/shard_map/ppermute | solution.py:477
  24.4 1.6 %collective-permute-start.5 = (bf16[128,1024]{1,0:T(8,128)(2,1)S(1)}, bf16[128,1024]{1,0:T(8,128)(2,1)S(1)}, u32[]{:S(2)}, u32[]{:S(2)}) collective-permute-start(bf16[128,1024]{1,0:T(8,128)(2,1)S(1)} %get-tuple-element.107), channel_id=1, source_target_pairs={{0,2},{2,0},{4,6},{6,4},{1,3},{3,1},{5,7},{7,5},{8,10},{10,8},{12,... | collective-permute-start | bytes 786440 | tf_op jit(solution)/shard_map/ppermute | solution.py:481
  24.6 1.9 %collective-permute-start.6 = (bf16[128,1024]{1,0:T(8,128)(2,1)S(1)}, bf16[128,1024]{1,0:T(8,128)(2,1)S(1)}, u32[]{:S(2)}, u32[]{:S(2)}) collective-permute-start(bf16[128,1024]{1,0:T(8,128)(2,1)S(1)} %get-tuple-element.106), channel_id=1, source_target_pairs={{0,2},{2,0},{4,6},{6,4},{1,3},{3,1},{5,7},{7,5},{8,10},{10,8},{12,... | collective-permute-start | bytes 786440 | tf_op jit(solution)/shard_map/ppermute | solution.py:481
  36.3 19.6 %collective-permute-start.10 = (bf16[1024,256]{1,0:T(8,128)(2,1)S(1)}, bf16[1024,256]{1,0:T(8,128)(2,1)S(1)}, u32[]{:S(2)}, u32[]{:S(2)}) collective-permute-start(bf16[1024,256]{1,0:T(8,128)(2,1)S(1)} %pad_maximum_fusion.1.refs_0_), channel_id=1, source_target_pairs={{0,32},{2,10},{4,36},{6,14},{8,40},{10,18},{12,44},{14,22},{16,48}... | collective-permute-start | bytes 1572872 | tf_op jit(solution)/shard_map/ppermute | solution.py:477
  37.6 18.8 %collective-permute-start.11 = (bf16[1024,256]{1,0:T(8,128)(2,1)S(1)}, bf16[1024,256]{1,0:T(8,128)(2,1)S(1)}, u32[]{:S(2)}, u32[]{:S(2)}) collective-permute-start(bf16[1024,256]{1,0:T(8,128)(2,1)S(1)} %pad_maximum_fusion.1.refs_0_), channel_id=1, source_target_pairs={{0,64},{2,18},{4,68},{6,22},{8,72},{10,26},{12,76},{14,30},{16,80}... | collective-permute-start | bytes 1572872 | tf_op jit(solution)/shard_map/ppermute | solution.py:477
  39.7 16.7 %collective-permute-start.12 = (bf16[1024,256]{1,0:T(8,128)(2,1)S(1)}, bf16[1024,256]{1,0:T(8,128)(2,1)S(1)}, u32[]{:S(2)}, u32[]{:S(2)}) collective-permute-start(bf16[1024,256]{1,0:T(8,128)(2,1)S(1)} %pad_maximum_fusion.1.refs_0_), channel_id=1, source_target_pairs={{0,96},{2,26},{4,100},{6,30},{8,104},{10,2},{12,108},{14,6},{16,11... | collective-permute-start | bytes 1572872 | tf_op jit(solution)/shard_map/ppermute | solution.py:477
  53.6 14.2 %collective-permute-start.13 = (bf16[1024,256]{1,0:T(8,128)(2,1)S(1)}, bf16[1024,256]{1,0:T(8,128)(2,1)S(1)}, u32[]{:S(2)}, u32[]{:S(2)}) collective-permute-start(bf16[1024,256]{1,0:T(8,128)(2,1)S(1)} %get-tuple-element.73), channel_id=1, source_target_pairs={{0,96},{2,26},{4,100},{6,30},{8,104},{10,2},{12,108},{14,6},{16,11... | collective-permute-start | bytes 1572872 | tf_op jit(solution)/shard_map/ppermute | solution.py:477
  53.9 13.9 %collective-permute-start.14 = (bf16[1024,256]{1,0:T(8,128)(2,1)S(1)}, bf16[1024,256]{1,0:T(8,128)(2,1)S(1)}, u32[]{:S(2)}, u32[]{:S(2)}) collective-permute-start(bf16[1024,256]{1,0:T(8,128)(2,1)S(1)} %get-tuple-element.74), channel_id=1, source_target_pairs={{0,64},{2,18},{4,68},{6,22},{8,72},{10,26},{12,76},{14,30},{16,80}... | collective-permute-start | bytes 1572872 | tf_op jit(solution)/shard_map/ppermute | solution.py:477
  55.9 14.3 %collective-permute-start.15 = (bf16[1024,256]{1,0:T(8,128)(2,1)S(1)}, bf16[1024,256]{1,0:T(8,128)(2,1)S(1)}, u32[]{:S(2)}, u32[]{:S(2)}) collective-permute-start(bf16[1024,256]{1,0:T(8,128)(2,1)S(1)} %get-tuple-element.75), channel_id=1, source_target_pairs={{0,32},{2,10},{4,36},{6,14},{8,40},{10,18},{12,44},{14,22},{16,48}... | collective-permute-start | bytes 1572872 | tf_op jit(solution)/shard_map/ppermute | solution.py:477
  67.7 23.7 %copy-start.1 = (bf16[256,1024]{1,0:T(8,128)(2,1)S(1)}, bf16[256,1024]{1,0:T(8,128)(2,1)}, u32[]{:S(2)}) copy-start(bf16[256,1024]{1,0:T(8,128)(2,1)} %q_ref.3) | copy-start | bytes 1572868
  67.7 23.7 %copy-start.2 = (f32[256,128]{1,0:T(8,128)S(1)}, f32[256,128]{1,0:T(8,128)}, u32[]{:S(2)}) copy-start(f32[256,128]{1,0:T(8,128)} %get-tuple-element.55.cos_ref) | copy-start | bytes 393220
  70.2 9.3 %collective-permute-start.16 = (bf16[1024,256]{1,0:T(8,128)(2,1)S(1)}, bf16[1024,256]{1,0:T(8,128)(2,1)S(1)}, u32[]{:S(2)}, u32[]{:S(2)}) collective-permute-start(bf16[1024,256]{1,0:T(8,128)(2,1)S(1)} %get-tuple-element.81), channel_id=1, source_target_pairs={{0,96},{2,26},{4,100},{6,30},{8,104},{10,2},{12,108},{14,6},{16,11... | collective-permute-start | bytes 1572872 | tf_op jit(solution)/shard_map/ppermute | solution.py:477
  71.1 10.8 %collective-permute-start.17 = (bf16[1024,256]{1,0:T(8,128)(2,1)S(1)}, bf16[1024,256]{1,0:T(8,128)(2,1)S(1)}, u32[]{:S(2)}, u32[]{:S(2)}) collective-permute-start(bf16[1024,256]{1,0:T(8,128)(2,1)S(1)} %get-tuple-element.82), channel_id=1, source_target_pairs={{0,64},{2,18},{4,68},{6,22},{8,72},{10,26},{12,76},{14,30},{16,80}... | collective-permute-start | bytes 1572872 | tf_op jit(solution)/shard_map/ppermute | solution.py:477
  72.8 14.6 %collective-permute-start.18 = (bf16[1024,256]{1,0:T(8,128)(2,1)S(1)}, bf16[1024,256]{1,0:T(8,128)(2,1)S(1)}, u32[]{:S(2)}, u32[]{:S(2)}) collective-permute-start(bf16[1024,256]{1,0:T(8,128)(2,1)S(1)} %get-tuple-element.83), channel_id=1, source_target_pairs={{0,32},{2,10},{4,36},{6,14},{8,40},{10,18},{12,44},{14,22},{16,48}... | collective-permute-start | bytes 1572872 | tf_op jit(solution)/shard_map/ppermute | solution.py:477
  73.6 28.8 %copy-start.6 = (bf16[256,256]{1,0:T(8,128)(2,1)S(1)}, bf16[256,256]{1,0:T(8,128)(2,1)}, u32[]{:S(2)}) copy-start(bf16[256,256]{1,0:T(8,128)(2,1)} %key_ref.1) | copy-start | bytes 393220
  73.6 28.8 %copy-start.8 = (f32[128]{0:T(128)S(1)}, f32[128]{0:T(128)}, u32[]{:S(2)}) copy-start(f32[128]{0:T(128)} %param.13) | copy-start | bytes 1540
  77.4 1.6 %collective-permute-start.20 = (bf16[128,1024]{1,0:T(8,128)(2,1)S(1)}, bf16[128,1024]{1,0:T(8,128)(2,1)S(1)}, u32[]{:S(2)}, u32[]{:S(2)}) collective-permute-start(bf16[128,1024]{1,0:T(8,128)(2,1)S(1)} %get-tuple-element.92), channel_id=1, source_target_pairs={{0,2},{2,0},{4,6},{6,4},{1,3},{3,1},{5,7},{7,5},{8,10},{10,8},{12,... | collective-permute-start | bytes 786440 | tf_op jit(solution)/shard_map/ppermute | solution.py:481
  77.5 1.9 %collective-permute-start.19 = (bf16[128,1024]{1,0:T(8,128)(2,1)S(1)}, bf16[128,1024]{1,0:T(8,128)(2,1)S(1)}, u32[]{:S(2)}, u32[]{:S(2)}) collective-permute-start(bf16[128,1024]{1,0:T(8,128)(2,1)S(1)} %get-tuple-element.91), channel_id=1, source_target_pairs={{0,2},{2,0},{4,6},{6,4},{1,3},{3,1},{5,7},{7,5},{8,10},{10,8},{12,... | collective-permute-start | bytes 786440 | tf_op jit(solution)/shard_map/ppermute | solution.py:481
  88.0 13.0 %collective-permute-start.24 = (bf16[256,1024]{1,0:T(8,128)(2,1)S(1)}, bf16[256,1024]{1,0:T(8,128)(2,1)S(1)}, u32[]{:S(2)}, u32[]{:S(2)}) collective-permute-start(bf16[256,1024]{1,0:T(8,128)(2,1)S(1)} %get-tuple-element.99), channel_id=1, source_target_pairs={{0,2},{2,0},{4,6},{6,4},{1,3},{3,1},{5,7},{7,5},{8,10},{10,8},{12,... | collective-permute-start | bytes 1572872 | tf_op jit(solution)/shard_map/ppermute | solution.py:481
  88.0 14.3 %collective-permute-start.25 = (bf16[256,1024]{1,0:T(8,128)(2,1)S(1)}, bf16[256,1024]{1,0:T(8,128)(2,1)S(1)}, u32[]{:S(2)}, u32[]{:S(2)}) collective-permute-start(bf16[256,1024]{1,0:T(8,128)(2,1)S(1)} %add_convert_fusion), channel_id=1, source_target_pairs={{0,4},{2,6},{4,0},{6,2},{1,5},{3,7},{5,1},{7,3},{8,12},{10,14},{12... | collective-permute-start | bytes 1572872 | tf_op jit(solution)/shard_map/ppermute | solution.py:481
  88.5 6.4 %collective-permute-start.21 = (bf16[2,256,256]{2,1,0:T(8,128)(2,1)S(1)}, bf16[2,256,256]{2,1,0:T(8,128)(2,1)S(1)}, u32[]{:S(2)}, u32[]{:S(2)}) collective-permute-start(bf16[2,256,256]{2,1,0:T(8,128)(2,1)S(1)} %get-tuple-element.95), channel_id=1, source_target_pairs={{0,24},{2,98},{4,28},{6,102},{8,0},{10,106},{12,4},{14,110},{16,8}... | collective-permute-start | bytes 786440 | tf_op jit(solution)/shard_map/ppermute | solution.py:477
  90.3 8.0 %collective-permute-start.22 = (bf16[2,256,256]{2,1,0:T(8,128)(2,1)S(1)}, bf16[2,256,256]{2,1,0:T(8,128)(2,1)S(1)}, u32[]{:S(2)}, u32[]{:S(2)}) collective-permute-start(bf16[2,256,256]{2,1,0:T(8,128)(2,1)S(1)} %get-tuple-element.96), channel_id=1, source_target_pairs={{0,16},{2,66},{4,20},{6,70},{8,24},{10,74},{12,28},{14,78},{16,0},... | collective-permute-start | bytes 786440 | tf_op jit(solution)/shard_map/ppermute | solution.py:477
  91.5 9.5 %collective-permute-start.23 = (bf16[2,256,256]{2,1,0:T(8,128)(2,1)S(1)}, bf16[2,256,256]{2,1,0:T(8,128)(2,1)S(1)}, u32[]{:S(2)}, u32[]{:S(2)}) collective-permute-start(bf16[2,256,256]{2,1,0:T(8,128)(2,1)S(1)} %get-tuple-element.97), channel_id=1, source_target_pairs={{0,8},{2,34},{4,12},{6,38},{8,16},{10,42},{12,20},{14,46},{16,24},... | collective-permute-start | bytes 786440 | tf_op jit(solution)/shard_map/ppermute | solution.py:477
  (6 other events, 87.3 us)

commit v4 on v3

--- a/solution.py
+++ b/solution.py
@@ -16,6 +16,8 @@
 SCALE = HEAD ** (-0.5)
 SCALE2 = SCALE * 1.4426950408889634
 WIDE = 8
+SCORE_WIDE = 4
+WEIGH_WIDE = 16
 SIDE = 4
 VMEM = pl.BlockSpec(memory_space=pltpu.VMEM)
 SMEM = pl.BlockSpec(memory_space=pltpu.SMEM)
@@ -148,25 +150,24 @@
     k = pl.program_id(0)
 
     def product(piece):
-        return lax.dot_general(piece[...], w_ref[...], (((1,), (1,)), ((), ())), preferred_element_type=jnp.float32)
+        return lax.dot_general(piece, w_ref[...], (((1,), (1,)), ((), ())), preferred_element_type=jnp.float32)
 
     @pl.when(k == 0)
     def _():
-        acc[...] = product(p0)
+        acc[...] = product(p0[...])
 
     @pl.when(k == 1)
     def _():
-        acc[...] += product(p1)
+        acc[...] += product(p1[...])
 
     @pl.when(k == 2)
     def _():
-        acc[...] += product(p2)
+        acc[...] += product(p2[...])
 
     @pl.when(k == 3)
     def _():
-        rows = p3a.shape[0]
-        out_ref[:rows] = (acc[:rows] + product(p3a)).astype(jnp.bfloat16)
-        out_ref[rows:] = (acc[rows:] + product(p3b)).astype(jnp.bfloat16)
+        both = jnp.concatenate([p3a[...], p3b[...]], axis=0)
+        out_ref[...] = (acc[...] + product(both)).astype(jnp.bfloat16)
 
 
 def d_attn_product(me, pieces, w_out):
@@ -242,10 +243,8 @@
 
 def attention_kernel(tags_ref, q_ref, do_ref, *refs, first, nclean, own_blocks, group):
     pieces, (attn_ref, dq_ref), outs = refs[0:4], refs[4:6], refs[6:10]
-    ks, vs, kt, vt, dk, dv, st = refs[10:]
-    spare = 2 * nclean
+    ks, vs, kt, vt, dk, dv, dk_own, dv_own, st = refs[10:]
     rows = group * BLK
-    wide = WIDE * BLK
     own_base = place_of(0, 0) * own_blocks
     for far in range(SIDE):
         for near in range(SIDE):
@@ -259,116 +258,119 @@
     def flip(ref, pair):
         return ref[pl.ds(nclean + 2 * pair, 2)].reshape(2 * BLK, HEAD).astype(jnp.float32).T.astype(jnp.bfloat16)
 
-    def chunk(ref, c):
-        return ref[pl.ds(nclean + WIDE * c, WIDE)].reshape(wide, HEAD)
-
-    def chunk_t(ref, c):
-        return jnp.concatenate([ref[WIDE // 2 * c + i] for i in range(WIDE // 2)], axis=1)
+    def blocks_of(ref, c, many):
+        return ref[pl.ds(nclean + many * c, many)].reshape(many * BLK, HEAD)
+
+    def chunk_t(ref, c, many):
+        return jnp.concatenate([ref[many // 2 * c + i] for i in range(many // 2)], axis=1)
 
     for pair in range(nclean // 2):
         kt[pair] = flip(ks, pair)
         vt[pair] = flip(vs, pair)
-    dk[...] = jnp.zeros_like(dk)
-    dv[...] = jnp.zeros_like(dv)
+    for grad in (dk, dv):
+        grad[pl.ds(nclean, nclean)] = jnp.zeros((nclean, BLK, HEAD), jnp.float32)
 
     def gather(ref, j):
         return jnp.concatenate(
-            [ref[pl.ds(j * BLK, BLK), (first + h) * HEAD : (first + h + 1) * HEAD] for h in range(group)], axis=0
+            [ref[j * BLK : (j + 1) * BLK, (first + h) * HEAD : (first + h + 1) * HEAD] for h in range(group)], axis=0
         )
 
-    def one_block(j, unused):
+    def weight(score, bias):
+        return jnp.exp2(score * SCALE2 + bias)
+
+    def nt(left, right):
+        return lax.dot_general(left, right, (((1,), (1,)), ((), ())), preferred_element_type=jnp.float32)
+
+    def tn(left, right):
+        return lax.dot_general(left, right, (((0,), (0,)), ((), ())), preferred_element_type=jnp.float32)
+
+    def scores(j, st):
         own = tags_ref[own_base + j]
         noisy = own < nclean
-        index = own % nclean
-        slot = nclean + index
-        pair = index // 2
-
-        @pl.when(noisy)
-        def _():
-            for ref, ref_t, grad in ((ks, kt, dk), (vs, vt, dv)):
-                ref[spare] = ref[slot]
-                ref[slot] = ref[own]
-                ref_t[nclean // 2] = ref_t[pair]
-                ref_t[pair] = flip(ref, pair)
-                grad[spare] = grad[slot]
-                grad[slot] = jnp.zeros((BLK, HEAD), jnp.float32)
-
-        q = gather(q_ref, j)
-        do = gather(do_ref, j)
-        do_t = do.astype(jnp.float32).T
-
-        for c in range(nclean // WIDE):
-            st[c] = lax.dot_general(chunk(ks, c), q, (((1,), (1,)), ((), ())), preferred_element_type=jnp.float32)
-        hidden = [jnp.where(i > index, NEG, 0.0).astype(jnp.float32) for i in range(nclean)]
-        top = jnp.full((8, rows), NEG, jnp.float32)
-        for c in range(nclean // WIDE):
-            for i in range(WIDE):
-                part = jnp.max(st[c, i * BLK : (i + 1) * BLK, :].reshape(BLK // 8, 8, rows), axis=0)
-                top = jnp.maximum(top, part + hidden[WIDE * c + i])
+        limit = own % nclean + jnp.where(noisy, 0, 1)
+        hidden = [jnp.where(i >= limit, NEG, 0.0).astype(jnp.float32) for i in range(nclean)]
+        alone = jnp.where(noisy, 0.0, NEG).astype(jnp.float32)
+        q, do = gather(q_ref, j), gather(do_ref, j)
+        step = SCORE_WIDE * BLK
+        for c in range(nclean // SCORE_WIDE):
+            st[c * step : (c + 1) * step, :] = nt(blocks_of(ks, c, SCORE_WIDE), q)
+        own_score = nt(ks[own], q)
+        top = jnp.max(own_score.reshape(BLK // 8, 8, rows), axis=0) + alone
+        for i in range(nclean):
+            part = jnp.max(st[i * BLK : (i + 1) * BLK, :].reshape(BLK // 8, 8, rows), axis=0)
+            top = jnp.maximum(top, part + hidden[i])
         top = jnp.max(top, axis=0, keepdims=True) * SCALE2
-
-        def weight(c, shift):
-            return jnp.concatenate(
-                [
-                    jnp.exp2(st[c, i * BLK : (i + 1) * BLK, :] * SCALE2 + (hidden[WIDE * c + i] - shift))
-                    for i in range(WIDE)
-                ],
-                axis=0,
-            )
-
-        total = jnp.zeros((8, rows), jnp.float32)
-        acc = jnp.zeros((HEAD, rows), jnp.float32)
-        for c in range(nclean // WIDE):
-            e = weight(c, top)
-            total = total + jnp.sum(e.reshape(wide // 8, 8, rows), axis=0)
-            acc = acc + jnp.dot(chunk_t(vt, c), e.astype(jnp.bfloat16), preferred_element_type=jnp.float32)
+        return own, hidden, alone, q, do, own_score, top
+
+    def weights(c, many, st, hidden, shift):
+        return jnp.concatenate(
+            [weight(st[i * BLK : (i + 1) * BLK, :], hidden[i] - shift) for i in range(c * many, (c + 1) * many)], axis=0
+        )
+
+    def forward(j, st, state):
+        own, hidden, alone, q, do, own_score, top = state
+        e = weight(own_score, alone - top)
+        total = jnp.sum(e.reshape(BLK // 8, 8, rows), axis=0)
+        acc = tn(vs[own], e.astype(jnp.bfloat16))
+        for c in range(nclean // WEIGH_WIDE):
+            e = weights(c, WEIGH_WIDE, st, hidden, top)
+            total = total + jnp.sum(e.reshape(WEIGH_WIDE * BLK // 8, 8, rows), axis=0)
+            acc = acc + jnp.dot(chunk_t(vt, c, WEIGH_WIDE), e.astype(jnp.bfloat16), preferred_element_type=jnp.float32)
         total = jnp.sum(total, axis=0, keepdims=True)
         attn_t = (acc / total).astype(jnp.bfloat16).astype(jnp.float32)
-        delta = jnp.sum(do_t * attn_t, axis=0, keepdims=True)
+        delta = jnp.sum(do.astype(jnp.float32).T * attn_t, axis=0, keepdims=True)
         attn = attn_t.T.astype(jnp.bfloat16)
         for h in range(group):
-            attn_ref[pl.ds(j * BLK, BLK), h * HEAD : (h + 1) * HEAD] = attn[h * BLK : (h + 1) * BLK]
-        top = top + jnp.log2(total)
-        acc = jnp.zeros((HEAD, rows), jnp.float32)
-        for c in range(nclean // WIDE):
-            p = weight(c, top)
-            dp = lax.dot_general(chunk(vs, c), do, (((1,), (1,)), ((), ())), preferred_element_type=jnp.float32)
-            ds = (p * (dp - delta)).astype(jnp.bfloat16)
+            attn_ref[j * BLK : (j + 1) * BLK, h * HEAD : (h + 1) * HEAD] = attn[h * BLK : (h + 1) * BLK]
+        return top + jnp.log2(total), delta
+
+    def backward(j, st, state, top, delta):
+        own, hidden, alone, q, do, own_score, unused = state
+
+        def gradients(p, v):
+            ds = (p * (nt(v, do) - delta)).astype(jnp.bfloat16)
             dvc = jnp.dot(p.astype(jnp.bfloat16), do, preferred_element_type=jnp.float32)
             dkc = jnp.dot(ds, q, preferred_element_type=jnp.float32)
+            return ds, dkc, dvc
+
+        ds, dkc, dvc = gradients(weight(own_score, alone - top), vs[own])
+        dv_own[j] = dvc
+        dk_own[j] = dkc
+        acc = tn(ks[own], ds)
+        for c in range(nclean // WIDE):
+            ds, dkc, dvc = gradients(weights(c, WIDE, st, hidden, top), blocks_of(vs, c, WIDE))
             dv[pl.ds(nclean + WIDE * c, WIDE)] += dvc.reshape(WIDE, BLK, HEAD)
             dk[pl.ds(nclean + WIDE * c, WIDE)] += dkc.reshape(WIDE, BLK, HEAD)
-            acc = acc + jnp.dot(chunk_t(kt, c), ds, preferred_element_type=jnp.float32)
+            acc = acc + jnp.dot(chunk_t(kt, c, WIDE), ds, preferred_element_type=jnp.float32)
         dq = (acc * SCALE).T
         for h in range(group):
-            dq_ref[pl.ds(j * BLK, BLK), h * HEAD : (h + 1) * HEAD] = dq[h * BLK : (h + 1) * BLK]
-
-        @pl.when(noisy)
-        def _():
-            for ref, ref_t, grad in ((ks, kt, dk), (vs, vt, dv)):
-                ref[slot] = ref[spare]
-                ref_t[pair] = ref_t[nclean // 2]
-                grad[own] = grad[slot]
-                grad[slot] = grad[spare]
-
-        return unused
-
-    lax.fori_loop(0, own_blocks, one_block, 0)
+            dq_ref[j * BLK : (j + 1) * BLK, h * HEAD : (h + 1) * HEAD] = dq[h * BLK : (h + 1) * BLK]
+
+    states, sums = {}, {}
+    for turn in range(own_blocks + 2):
+        if 0 <= turn - 2 < own_blocks:
+            backward(turn - 2, st.at[turn - 2], states[turn - 2], *sums[turn - 2])
+        if 0 <= turn - 1 < own_blocks:
+            sums[turn - 1] = forward(turn - 1, st.at[turn - 1], states[turn - 1])
+        if turn < own_blocks:
+            states[turn] = scores(turn, st.at[turn])
     for far in range(SIDE):
         for near in range(SIDE):
             base = place_of(far, near) * own_blocks
             for b in range(own_blocks):
                 tag = tags_ref[base + b]
                 part = slice((near * own_blocks + b) * BLK, (near * own_blocks + b + 1) * BLK)
-                outs[far][part, 0:HEAD] = (dk[tag] * SCALE).astype(jnp.bfloat16)
-                outs[far][part, HEAD:] = dv[tag].astype(jnp.bfloat16)
+                for grad, own_grad, cols, factor in ((dk, dk_own, slice(0, HEAD), SCALE), (dv, dv_own, slice(HEAD, None), 1.0)):
+                    alone = 0.0 if far or near else own_grad[b]
+                    value = jnp.where(tag < nclean, alone, grad[tag])
+                    outs[far][part, cols] = (value * factor).astype(jnp.bfloat16)
 
 
 def attention(tags, q, do, pieces, g, group):
     tok = q.shape[0]
     nclean = tags.shape[0] // 2
     rows = group * BLK
-    blocks = 2 * nclean + 1
+    blocks = 2 * nclean
     return pl.pallas_call(
         functools.partial(
             attention_kernel, first=g * group, nclean=nclean, own_blocks=tok // BLK, group=group
@@ -380,11 +382,13 @@
         scratch_shapes=[
             pltpu.VMEM((blocks, BLK, HEAD), jnp.bfloat16),
             pltpu.VMEM((blocks, BLK, HEAD), jnp.bfloat16),
-            pltpu.VMEM((nclean // 2 + 1, HEAD, 2 * BLK), jnp.bfloat16),
-            pltpu.VMEM((nclean // 2 + 1, HEAD, 2 * BLK), jnp.bfloat16),
+            pltpu.VMEM((nclean // 2, HEAD, 2 * BLK), jnp.bfloat16),
+            pltpu.VMEM((nclean // 2, HEAD, 2 * BLK), jnp.bfloat16),
             pltpu.VMEM((blocks, BLK, HEAD), jnp.float32),
             pltpu.VMEM((blocks, BLK, HEAD), jnp.float32),
-            pltpu.VMEM((nclean // WIDE, WIDE * BLK, rows), jnp.float32),
+            pltpu.VMEM((tok // BLK, BLK, HEAD), jnp.float32),
+            pltpu.VMEM((tok // BLK, BLK, HEAD), jnp.float32),
+            pltpu.VMEM((tok // BLK, nclean * BLK, rows), jnp.float32),
         ],
         compiler_params=params(),
         cost_estimate=cost(6 << 30, 4 << 20),

time: 105 us -> 103 us (0.981)
  Pallas kernels: 42.9 us -> 37.1 us
  waiting for transfers between devices: 24.6 us -> 28.2 us
    pallas_call x2, Pallas kernels: 23.4 us -> 18.4 us  [attention(): pl.pallas_call(functools.partial(attention_kernel, first=g * group, nclea...]
    ppermute x18, waiting for transfers between devices: 20.4 us -> 24 us  [hop(): return lax.ppermute(value, ('ctx', 'ffn'), pairs)]
  transfers between devices with their start and end apart: 26 -> 26, of which waited for: 14 -> 15; matrix products, arithmetic and copies ran while one was open for 4% -> 4% of each run, Pallas kernels for 36% -> 32%
where the time goes in v4:
time: 103 us; the launch traced here: 101 us
  Pallas kernels  37.1 us (36%)
  waiting for transfers between devices  28.2 us (27%)
  starting transfers between devices  26.5 us (26%)
  local copies, waits for them, and re-layouts  8.45 us (8%)
    ppermute x18, starting transfers between devices, hop(): return lax.ppermute(value, ('ctx', 'ffn'), pairs)  24.4 us
    ppermute x18, waiting for transfers between devices, hop(): return lax.ppermute(value, ('ctx', 'ffn'), pairs)  24 us
    pallas_call x2, Pallas kernels, attention(): pl.pallas_call(functools.partial(attention_kernel, first=g * group, nclea...  18.4 us
    pallas_call x1, Pallas kernels, d_attn_product(): pl.pallas_call(d_attn_kernel, grid_spec=pltpu.PrefetchScalarGridSpec(num_...  4.58 us
    unnamed x24, local copies, waits for them, and re-layouts  4.47 us
    ppermute x8, waiting for transfers between devices, across(): return lax.ppermute(value, 'ffn', [(s, s ^ mask) for s in range(4)])  4.22 us
    squeeze x4, local copies, waits for them, and re-layouts, per_device(): part[g]  3.94 us
    pallas_call x1, Pallas kernels, out_product(): pl.pallas_call(out_kernel, grid_spec=pltpu.PrefetchScalarGridSpec(num_sca...  3.7 us
  transfers between devices with their start and end apart: 26, of which 15 were waited for; matrix products, arithmetic and copies ran while one was open for 4% of the time, Pallas kernels for 32%

profile of v4, /device:TPU:96, one launch (start us, length us, event | category | flops | bytes accessed | tf_op | source)
XLA Modules:
  0.0 101.4 jit_solution(9461406220308685431)
XLA Ops:
  0.6 3.0 %key_prep.1 = (bf16[2,256,256]{2,1,0:T(8,128)(2,1)}, f32[256,128]{1,0:T(8,128)}, f32[256,128]{1,0:T(8,128)}) custom-call(s32[64]{0:T(128)} %tags_ref.5, bf16[256,256]{1,0:T(8,128)(2,1)} %key_ref.1, bf16[256,256]{1,0:T(8,128)(2,1)} %value_hbm.1, f32[1,128]{1,0:T(1,128)} %bitcast.23, f32[192,128]{1,0:T(8,128)} %constant.8.clone.table_hbm), custom_call_target="tpu_custom_call" | custom-call | bytes 1048576 | tf_op jit(solution)/shard_map/key_prep/pallas_call | solution.py:111
  3.6 2.8 %collective-permute-start.2 = (bf16[2,256,256]{2,1,0:T(8,128)(2,1)}, bf16[2,256,256]{2,1,0:T(8,128)(2,1)}, u32[]{:S(2)}, u32[]{:S(2)}) collective-permute-start(bf16[2,256,256]{2,1,0:T(8,128)(2,1)} %get-tuple-element.57), channel_id=1, source_target_pairs={{0,24},{2,98},{4,28},{6,102},{8,0},{10,106},{12,4},{14,110},{16,8}... | collective-permute-start | bytes 786440 | tf_op jit(solution)/shard_map/ppermute | solution.py:481
  8.6 1.0 slice_bitcast_fusion.6
  9.6 3.1 %query_prep.1.q_ref = bf16[256,1024]{1,0:T(8,128)(2,1)} custom-call(bf16[256,1024]{1,0:T(8,128)(2,1)} %q_ref.3, f32[1,128]{1,0:T(1,128)} %bitcast.21, f32[256,128]{1,0:T(8,128)} %get-tuple-element.55.cos_ref, f32[256,128]{1,0:T(8,128)} %get-tuple-element.56.sin_ref), custom_call_target="tpu_custom_call" | custom-call | bytes 4194304 | tf_op jit(solution)/shard_map/query_prep/pallas_call | solution.py:137
  14.8 1.0 slice_bitcast_fusion.1
  15.8 1.7 %collective-permute-done = bf16[2,256,256]{2,1,0:T(8,128)(2,1)} collective-permute-done((bf16[2,256,256]{2,1,0:T(8,128)(2,1)}, bf16[2,256,256]{2,1,0:T(8,128)(2,1)}, u32[]{:S(2)}, u32[]{:S(2)}) %collective-permute-start) | collective-permute-done | bytes 262176 | tf_op jit(solution)/shard_map/ppermute | solution.py:481
  17.5 1.0 slice_bitcast_fusion.2
  18.5 1.6 %collective-permute-start.7 = (bf16[1024,256]{1,0:T(8,128)(2,1)S(1)}, bf16[1024,256]{1,0:T(8,128)(2,1)}, u32[]{:S(2)}, u32[]{:S(2)}) collective-permute-start(bf16[1024,256]{1,0:T(8,128)(2,1)S(1)} %pad_maximum_fusion.refs_0_), channel_id=1, source_target_pairs={{0,32},{2,10},{4,36},{6,14},{8,40},{10,18},{12,44},{14,22},{16,48}... | collective-permute-start | bytes 1572872 | tf_op jit(solution)/shard_map/ppermute | solution.py:481
  20.2 2.9 %collective-permute-start.8 = (bf16[1024,256]{1,0:T(8,128)(2,1)S(1)}, bf16[1024,256]{1,0:T(8,128)(2,1)}, u32[]{:S(2)}, u32[]{:S(2)}) collective-permute-start(bf16[1024,256]{1,0:T(8,128)(2,1)S(1)} %pad_maximum_fusion.refs_0_), channel_id=1, source_target_pairs={{0,64},{2,18},{4,68},{6,22},{8,72},{10,26},{12,76},{14,30},{16,80}... | collective-permute-start | bytes 1572872 | tf_op jit(solution)/shard_map/ppermute | solution.py:481
  23.1 1.3 %collective-permute-start.9 = (bf16[1024,256]{1,0:T(8,128)(2,1)S(1)}, bf16[1024,256]{1,0:T(8,128)(2,1)}, u32[]{:S(2)}, u32[]{:S(2)}) collective-permute-start(bf16[1024,256]{1,0:T(8,128)(2,1)S(1)} %pad_maximum_fusion.refs_0_), channel_id=1, source_target_pairs={{0,96},{2,26},{4,100},{6,30},{8,104},{10,2},{12,108},{14,6},{16,11... | collective-permute-start | bytes 1572872 | tf_op jit(solution)/shard_map/ppermute | solution.py:481
  26.4 3.4 %copy-done = bf16[1024,4096]{1,0:T(8,128)(2,1)S(1)} copy-done((bf16[1024,4096]{1,0:T(8,128)(2,1)S(1)}, bf16[1024,4096]{1,0:T(8,128)(2,1)}, u32[]{:S(2)}) %copy-start) | copy-done | bytes 8388632
  29.8 1.0 %copy-done.4 = bf16[256,1024]{1,0:T(8,128)(2,1)S(1)} copy-done((bf16[256,1024]{1,0:T(8,128)(2,1)S(1)}, bf16[256,1024]{1,0:T(8,128)(2,1)}, u32[]{:S(2)}) %copy-start.4) | copy-done | bytes 524312
  30.9 4.6 %d_attn_product.1.do_ref = bf16[256,1024]{1,0:T(8,128)(2,1)S(1)} custom-call(s32[1]{0:T(128)} %bitcast.10.me_ref, bf16[256,1024]{1,0:T(8,128)(2,1)S(1)} %copy-done.4, bf16[256,1024]{1,0:T(8,128)(2,1)} %collective-permute-done.3.p1, bf16[256,1024]{1,0:T(8,128)(2,1)S(1)} %collective-permute-done.4.p2, bf16[128,1024]{1,0:T(8,128)(2,1)S(1)} %collective-permute-done.5.p3a, ...), custom_call_target="tpu_custom_call" | custom-call | flops 1 | bytes 1 | tf_op jit(solution)/shard_map/d_attn_product/pallas_call | solution.py:177
  35.9 1.6 %collective-permute-start.10 = (bf16[1024,256]{1,0:T(8,128)(2,1)S(1)}, bf16[1024,256]{1,0:T(8,128)(2,1)S(1)}, u32[]{:S(2)}, u32[]{:S(2)}) collective-permute-start(bf16[1024,256]{1,0:T(8,128)(2,1)S(1)} %pad_maximum_fusion.1.refs_0_), channel_id=1, source_target_pairs={{0,32},{2,10},{4,36},{6,14},{8,40},{10,18},{12,44},{14,22},{16,48}... | collective-permute-start | bytes 1572872 | tf_op jit(solution)/shard_map/ppermute | solution.py:481
  37.6 2.1 %collective-permute-start.11 = (bf16[1024,256]{1,0:T(8,128)(2,1)S(1)}, bf16[1024,256]{1,0:T(8,128)(2,1)S(1)}, u32[]{:S(2)}, u32[]{:S(2)}) collective-permute-start(bf16[1024,256]{1,0:T(8,128)(2,1)S(1)} %pad_maximum_fusion.1.refs_0_), channel_id=1, source_target_pairs={{0,64},{2,18},{4,68},{6,22},{8,72},{10,26},{12,76},{14,30},{16,80}... | collective-permute-start | bytes 1572872 | tf_op jit(solution)/shard_map/ppermute | solution.py:481
  39.7 1.7 %collective-permute-start.12 = (bf16[1024,256]{1,0:T(8,128)(2,1)S(1)}, bf16[1024,256]{1,0:T(8,128)(2,1)S(1)}, u32[]{:S(2)}, u32[]{:S(2)}) collective-permute-start(bf16[1024,256]{1,0:T(8,128)(2,1)S(1)} %pad_maximum_fusion.1.refs_0_), channel_id=1, source_target_pairs={{0,96},{2,26},{4,100},{6,30},{8,104},{10,2},{12,108},{14,6},{16,11... | collective-permute-start | bytes 1572872 | tf_op jit(solution)/shard_map/ppermute | solution.py:481
  41.4 9.6 %attention.3 = (bf16[256,512]{1,0:T(8,128)(2,1)S(1)}, f32[256,512]{1,0:T(8,128)S(1)}, bf16[1024,256]{1,0:T(8,128)(2,1)S(1)}, bf16[1024,256]{1,0:T(8,128)(2,1)S(1...) custom-call(s32[64]{0:T(128)S(1)} %copy-done.9, bf16[256,1024]{1,0:T(8,128)(2,1)S(1)} %copy-done.5, ...), custom_call_target="tpu_custom_call" | custom-call | flops 6442450944 | bytes 4194304 | tf_op jit(solution)/shard_map/attention/pallas_call | solution.py:374
  51.4 2.1 %collective-permute-start.14 = (bf16[1024,256]{1,0:T(8,128)(2,1)S(1)}, bf16[1024,256]{1,0:T(8,128)(2,1)S(1)}, u32[]{:S(2)}, u32[]{:S(2)}) collective-permute-start(bf16[1024,256]{1,0:T(8,128)(2,1)S(1)} %get-tuple-element.74), channel_id=1, source_target_pairs={{0,64},{2,18},{4,68},{6,22},{8,72},{10,26},{12,76},{14,30},{16,80}... | collective-permute-start | bytes 1572872 | tf_op jit(solution)/shard_map/ppermute | solution.py:481
  53.5 8.8 %attention.2 = (bf16[256,512]{1,0:T(8,128)(2,1)S(1)}, f32[256,512]{1,0:T(8,128)S(1)}, bf16[1024,256]{1,0:T(8,128)(2,1)S(1)}, bf16[1024,256]{1,0:T(8,128)(2,1)S(1...) custom-call(s32[64]{0:T(128)S(1)} %copy-done.9, bf16[256,1024]{1,0:T(8,128)(2,1)S(1)} %copy-done.5, ...), custom_call_target="tpu_custom_call" | custom-call | flops 6442450944 | bytes 4194304 | tf_op jit(solution)/shard_map/attention/pallas_call | solution.py:374
  62.4 5.3 %collective-permute-done.15.refs_3_ = bf16[1024,256]{1,0:T(8,128)(2,1)S(1)} collective-permute-done((bf16[1024,256]{1,0:T(8,128)(2,1)S(1)}, bf16[1024,256]{1,0:T(8,128)(2,1)S(1)}, u32[]{:S(2)}, u32[]{:S(2)}) %collective-permute-start.15) | collective-permute-done | bytes 524320 | tf_op jit(solution)/shard_map/ppermute | solution.py:481
  68.6 1.8 %collective-permute-start.17 = (bf16[1024,256]{1,0:T(8,128)(2,1)S(1)}, bf16[1024,256]{1,0:T(8,128)(2,1)S(1)}, u32[]{:S(2)}, u32[]{:S(2)}) collective-permute-start(bf16[1024,256]{1,0:T(8,128)(2,1)S(1)} %get-tuple-element.82), channel_id=1, source_target_pairs={{0,64},{2,18},{4,68},{6,22},{8,72},{10,26},{12,76},{14,30},{16,80}... | collective-permute-start | bytes 1572872 | tf_op jit(solution)/shard_map/ppermute | solution.py:481
  71.1 3.7 %out_product.1 = (bf16[128,1024]{1,0:T(8,128)(2,1)S(1)}, bf16[128,1024]{1,0:T(8,128)(2,1)S(1)}, bf16[256,1024]{1,0:T(8,128)(2,1)S(1)}, bf16[256,1024]{1,0:T(8,128)(2,1)S(1)}, bf16[256,1024]{1,0:T(8,128)(2,1)S(1)}) custom-call(s32[1]{0:T(128)} %bitcast.10.me_ref, bf16[256,512]{1,0:T(8,128)(2,1)S(1)} %get-tuple-element.88.a0_ref, ...), custom_call_target="tpu_custom_call" | custom-call | flops 1 | bytes 1 | tf_op jit(solution)/shard_map/out_product/pallas_call | solution.py:220
  75.4 1.0 %collective-permute-done.20 = bf16[128,1024]{1,0:T(8,128)(2,1)S(1)} collective-permute-done((bf16[128,1024]{1,0:T(8,128)(2,1)S(1)}, bf16[128,1024]{1,0:T(8,128)(2,1)S(1)}, u32[]{:S(2)}, u32[]{:S(2)}) %collective-permute-start.20) | collective-permute-done | bytes 262176 | tf_op jit(solution)/shard_map/ppermute | solution.py:485
  77.1 2.3 %collective-permute-done.17.refs_6_ = bf16[1024,256]{1,0:T(8,128)(2,1)S(1)} collective-permute-done((bf16[1024,256]{1,0:T(8,128)(2,1)S(1)}, bf16[1024,256]{1,0:T(8,128)(2,1)S(1)}, u32[]{:S(2)}, u32[]{:S(2)}) %collective-permute-start.17) | collective-permute-done | bytes 524320 | tf_op jit(solution)/shard_map/ppermute | solution.py:481
  79.4 5.5 %collective-permute-done.18.refs_7_ = bf16[1024,256]{1,0:T(8,128)(2,1)S(1)} collective-permute-done((bf16[1024,256]{1,0:T(8,128)(2,1)S(1)}, bf16[1024,256]{1,0:T(8,128)(2,1)S(1)}, u32[]{:S(2)}, u32[]{:S(2)}) %collective-permute-start.18) | collective-permute-done | bytes 524320 | tf_op jit(solution)/shard_map/ppermute | solution.py:481
  86.0 1.7 %collective-permute-start.21 = (bf16[2,256,256]{2,1,0:T(8,128)(2,1)S(1)}, bf16[2,256,256]{2,1,0:T(8,128)(2,1)S(1)}, u32[]{:S(2)}, u32[]{:S(2)}) collective-permute-start(bf16[2,256,256]{2,1,0:T(8,128)(2,1)S(1)} %get-tuple-element.95), channel_id=1, source_target_pairs={{0,24},{2,98},{4,28},{6,102},{8,0},{10,106},{12,4},{14,110},{16,8}... | collective-permute-start | bytes 786440 | tf_op jit(solution)/shard_map/ppermute | solution.py:481
  88.6 2.2 %query_back.1 = f32[256,1024]{1,0:T(8,128)} custom-call(bf16[256,1024]{1,0:T(8,128)(2,1)S(1)} %copy-done.1, f32[256,512]{1,0:T(8,128)S(1)} %get-tuple-element.102.a_ref, f32[256,512]{1,0:T(8,128)S(1)} %get-tuple-element.103.b_ref, f32[1,128]{1,0:T(1,128)S(1)} %bitcast.22, f32[256,128]{1,0:T(8,128)S(1)} %copy-done.2, f32[256,128]{1,0:T(8,128)S(1)} %copy-done.3), custom_call_target="tpu_custom_call" | custom-call | flops 1 | bytes 1 | tf_op jit(solution)/shard_map/query_back/pallas_call | solution.py:410
  90.9 1.5 %collective-permute-done.21.b = bf16[2,256,256]{2,1,0:T(8,128)(2,1)S(1)} collective-permute-done((bf16[2,256,256]{2,1,0:T(8,128)(2,1)S(1)}, bf16[2,256,256]{2,1,0:T(8,128)(2,1)S(1)}, u32[]{:S(2)}, u32[]{:S(2)}) %collective-permute-start.21) | collective-permute-done | bytes 262176 | tf_op jit(solution)/shard_map/ppermute | solution.py:481
  92.4 3.3 %collective-permute-done.22.c = bf16[2,256,256]{2,1,0:T(8,128)(2,1)S(1)} collective-permute-done((bf16[2,256,256]{2,1,0:T(8,128)(2,1)S(1)}, bf16[2,256,256]{2,1,0:T(8,128)(2,1)S(1)}, u32[]{:S(2)}, u32[]{:S(2)}) %collective-permute-start.22) | collective-permute-done | bytes 262176 | tf_op jit(solution)/shard_map/ppermute | solution.py:481
  95.7 2.7 %collective-permute-done.23.d = bf16[2,256,256]{2,1,0:T(8,128)(2,1)S(1)} collective-permute-done((bf16[2,256,256]{2,1,0:T(8,128)(2,1)S(1)}, bf16[2,256,256]{2,1,0:T(8,128)(2,1)S(1)}, u32[]{:S(2)}, u32[]{:S(2)}) %collective-permute-start.23) | collective-permute-done | bytes 262176 | tf_op jit(solution)/shard_map/ppermute | solution.py:481
  98.4 1.5 %collective-permute-done.25.far = bf16[256,1024]{1,0:T(8,128)(2,1)S(1)} collective-permute-done((bf16[256,1024]{1,0:T(8,128)(2,1)S(1)}, bf16[256,1024]{1,0:T(8,128)(2,1)S(1)}, u32[]{:S(2)}, u32[]{:S(2)}) %collective-permute-start.25) | collective-permute-done | bytes 524320 | tf_op jit(solution)/shard_map/ppermute | solution.py:485
  99.9 1.6 %finish.1 = (bf16[256,1024]{1,0:T(8,128)(2,1)}, f32[256,256]{1,0:T(8,128)}, f32[256,256]{1,0:T(8,128)}) custom-call(bf16[256,256]{1,0:T(8,128)(2,1)S(1)} %copy-done.6, f32[1,128]{1,0:T(1,128)S(1)} %bitcast.24, f32[256,128]{1,0:T(8,128)S(1)} %copy-done.2, f32[256,128]{1,0:T(8,128)S(1)} %copy-done.3, bf16[2,256,256]{2,1,0:T(8,128)(2,1)S(1)} %get-tuple-element.94.a, ...), custom_call_target="tpu_custom_call" | custom-call | bytes 2097152 | tf_op jit(solution)/shard_map/finish/pallas_call | solution.py:436
  (62 shorter events, 11.9 us)
Async XLA Ops:
  3.6 9.9 %collective-permute-start.2 = (bf16[2,256,256]{2,1,0:T(8,128)(2,1)}, bf16[2,256,256]{2,1,0:T(8,128)(2,1)}, u32[]{:S(2)}, u32[]{:S(2)}) collective-permute-start(bf16[2,256,256]{2,1,0:T(8,128)(2,1)} %get-tuple-element.57), channel_id=1, source_target_pairs={{0,24},{2,98},{4,28},{6,102},{8,0},{10,106},{12,4},{14,110},{16,8}... | collective-permute-start | bytes 786440 | tf_op jit(solution)/shard_map/ppermute | solution.py:481
  6.5 8.3 %collective-permute-start.1 = (bf16[2,256,256]{2,1,0:T(8,128)(2,1)}, bf16[2,256,256]{2,1,0:T(8,128)(2,1)}, u32[]{:S(2)}, u32[]{:S(2)}) collective-permute-start(bf16[2,256,256]{2,1,0:T(8,128)(2,1)} %get-tuple-element.57), channel_id=1, source_target_pairs={{0,16},{2,66},{4,20},{6,70},{8,24},{10,74},{12,28},{14,78},{16,0},... | collective-permute-start | bytes 786440 | tf_op jit(solution)/shard_map/ppermute | solution.py:481
  7.3 10.2 %collective-permute-start = (bf16[2,256,256]{2,1,0:T(8,128)(2,1)}, bf16[2,256,256]{2,1,0:T(8,128)(2,1)}, u32[]{:S(2)}, u32[]{:S(2)}) collective-permute-start(bf16[2,256,256]{2,1,0:T(8,128)(2,1)} %get-tuple-element.57), channel_id=1, source_target_pairs={{0,8},{2,34},{4,12},{6,38},{8,16},{10,42},{12,20},{14,46},{16,24},... | collective-permute-start | bytes 786440 | tf_op jit(solution)/shard_map/ppermute | solution.py:481
  8.2 16.4 %collective-permute-start.3 = (bf16[256,1024]{1,0:T(8,128)(2,1)}, bf16[256,1024]{1,0:T(8,128)(2,1)}, u32[]{:S(2)}, u32[]{:S(2)}) collective-permute-start(bf16[256,1024]{1,0:T(8,128)(2,1)} %p0.1), channel_id=1, source_target_pairs={{0,2},{2,0},{4,6},{6,4},{1,3},{3,1},{5,7},{7,5},{8,10},{10,8},{12,... | collective-permute-start | bytes 1572872 | tf_op jit(solution)/shard_map/ppermute | solution.py:485
  8.2 16.2 %collective-permute-start.4 = (bf16[256,1024]{1,0:T(8,128)(2,1)}, bf16[256,1024]{1,0:T(8,128)(2,1)S(1)}, u32[]{:S(2)}, u32[]{:S(2)}) collective-permute-start(bf16[256,1024]{1,0:T(8,128)(2,1)} %p0.1), channel_id=1, source_target_pairs={{0,4},{2,6},{4,0},{6,2},{1,5},{3,7},{5,1},{7,3},{8,12},{10,14},{12... | collective-permute-start | bytes 1572872 | tf_op jit(solution)/shard_map/ppermute | solution.py:485
  9.6 31.9 %copy-start.9 = (s32[64]{0:T(128)S(1)}, s32[64]{0:T(128)}, u32[]{:S(2)}) copy-start(s32[64]{0:T(128)} %tags_ref.5) | copy-start | bytes 772
  12.6 28.8 %copy-start.5 = (bf16[256,1024]{1,0:T(8,128)(2,1)S(1)}, bf16[256,1024]{1,0:T(8,128)(2,1)}, u32[]{:S(2)}) copy-start(bf16[256,1024]{1,0:T(8,128)(2,1)} %query_prep.1.q_ref) | copy-start | bytes 1572868
  18.5 16.9 %collective-permute-start.7 = (bf16[1024,256]{1,0:T(8,128)(2,1)S(1)}, bf16[1024,256]{1,0:T(8,128)(2,1)}, u32[]{:S(2)}, u32[]{:S(2)}) collective-permute-start(bf16[1024,256]{1,0:T(8,128)(2,1)S(1)} %pad_maximum_fusion.refs_0_), channel_id=1, source_target_pairs={{0,32},{2,10},{4,36},{6,14},{8,40},{10,18},{12,44},{14,22},{16,48}... | collective-permute-start | bytes 1572872 | tf_op jit(solution)/shard_map/ppermute | solution.py:481
  20.2 15.8 %collective-permute-start.8 = (bf16[1024,256]{1,0:T(8,128)(2,1)S(1)}, bf16[1024,256]{1,0:T(8,128)(2,1)}, u32[]{:S(2)}, u32[]{:S(2)}) collective-permute-start(bf16[1024,256]{1,0:T(8,128)(2,1)S(1)} %pad_maximum_fusion.refs_0_), channel_id=1, source_target_pairs={{0,64},{2,18},{4,68},{6,22},{8,72},{10,26},{12,76},{14,30},{16,80}... | collective-permute-start | bytes 1572872 | tf_op jit(solution)/shard_map/ppermute | solution.py:481
  23.1 12.9 %collective-permute-start.9 = (bf16[1024,256]{1,0:T(8,128)(2,1)S(1)}, bf16[1024,256]{1,0:T(8,128)(2,1)}, u32[]{:S(2)}, u32[]{:S(2)}) collective-permute-start(bf16[1024,256]{1,0:T(8,128)(2,1)S(1)} %pad_maximum_fusion.refs_0_), channel_id=1, source_target_pairs={{0,96},{2,26},{4,100},{6,30},{8,104},{10,2},{12,108},{14,6},{16,11... | collective-permute-start | bytes 1572872 | tf_op jit(solution)/shard_map/ppermute | solution.py:481
  24.4 1.6 %collective-permute-start.5 = (bf16[128,1024]{1,0:T(8,128)(2,1)S(1)}, bf16[128,1024]{1,0:T(8,128)(2,1)S(1)}, u32[]{:S(2)}, u32[]{:S(2)}) collective-permute-start(bf16[128,1024]{1,0:T(8,128)(2,1)S(1)} %get-tuple-element.107), channel_id=1, source_target_pairs={{0,2},{2,0},{4,6},{6,4},{1,3},{3,1},{5,7},{7,5},{8,10},{10,8},{12,... | collective-permute-start | bytes 786440 | tf_op jit(solution)/shard_map/ppermute | solution.py:485
  24.6 1.9 %collective-permute-start.6 = (bf16[128,1024]{1,0:T(8,128)(2,1)S(1)}, bf16[128,1024]{1,0:T(8,128)(2,1)S(1)}, u32[]{:S(2)}, u32[]{:S(2)}) collective-permute-start(bf16[128,1024]{1,0:T(8,128)(2,1)S(1)} %get-tuple-element.106), channel_id=1, source_target_pairs={{0,2},{2,0},{4,6},{6,4},{1,3},{3,1},{5,7},{7,5},{8,10},{10,8},{12,... | collective-permute-start | bytes 786440 | tf_op jit(solution)/shard_map/ppermute | solution.py:485
  35.9 17.5 %collective-permute-start.10 = (bf16[1024,256]{1,0:T(8,128)(2,1)S(1)}, bf16[1024,256]{1,0:T(8,128)(2,1)S(1)}, u32[]{:S(2)}, u32[]{:S(2)}) collective-permute-start(bf16[1024,256]{1,0:T(8,128)(2,1)S(1)} %pad_maximum_fusion.1.refs_0_), channel_id=1, source_target_pairs={{0,32},{2,10},{4,36},{6,14},{8,40},{10,18},{12,44},{14,22},{16,48}... | collective-permute-start | bytes 1572872 | tf_op jit(solution)/shard_map/ppermute | solution.py:481
  37.6 15.9 %collective-permute-start.11 = (bf16[1024,256]{1,0:T(8,128)(2,1)S(1)}, bf16[1024,256]{1,0:T(8,128)(2,1)S(1)}, u32[]{:S(2)}, u32[]{:S(2)}) collective-permute-start(bf16[1024,256]{1,0:T(8,128)(2,1)S(1)} %pad_maximum_fusion.1.refs_0_), channel_id=1, source_target_pairs={{0,64},{2,18},{4,68},{6,22},{8,72},{10,26},{12,76},{14,30},{16,80}... | collective-permute-start | bytes 1572872 | tf_op jit(solution)/shard_map/ppermute | solution.py:481
  39.7 13.8 %collective-permute-start.12 = (bf16[1024,256]{1,0:T(8,128)(2,1)S(1)}, bf16[1024,256]{1,0:T(8,128)(2,1)S(1)}, u32[]{:S(2)}, u32[]{:S(2)}) collective-permute-start(bf16[1024,256]{1,0:T(8,128)(2,1)S(1)} %pad_maximum_fusion.1.refs_0_), channel_id=1, source_target_pairs={{0,96},{2,26},{4,100},{6,30},{8,104},{10,2},{12,108},{14,6},{16,11... | collective-permute-start | bytes 1572872 | tf_op jit(solution)/shard_map/ppermute | solution.py:481
  51.0 11.3 %collective-permute-start.13 = (bf16[1024,256]{1,0:T(8,128)(2,1)S(1)}, bf16[1024,256]{1,0:T(8,128)(2,1)S(1)}, u32[]{:S(2)}, u32[]{:S(2)}) collective-permute-start(bf16[1024,256]{1,0:T(8,128)(2,1)S(1)} %get-tuple-element.73), channel_id=1, source_target_pairs={{0,96},{2,26},{4,100},{6,30},{8,104},{10,2},{12,108},{14,6},{16,11... | collective-permute-start | bytes 1572872 | tf_op jit(solution)/shard_map/ppermute | solution.py:481
  51.4 11.0 %collective-permute-start.14 = (bf16[1024,256]{1,0:T(8,128)(2,1)S(1)}, bf16[1024,256]{1,0:T(8,128)(2,1)S(1)}, u32[]{:S(2)}, u32[]{:S(2)}) collective-permute-start(bf16[1024,256]{1,0:T(8,128)(2,1)S(1)} %get-tuple-element.74), channel_id=1, source_target_pairs={{0,64},{2,18},{4,68},{6,22},{8,72},{10,26},{12,76},{14,30},{16,80}... | collective-permute-start | bytes 1572872 | tf_op jit(solution)/shard_map/ppermute | solution.py:481
  53.5 14.2 %collective-permute-start.15 = (bf16[1024,256]{1,0:T(8,128)(2,1)S(1)}, bf16[1024,256]{1,0:T(8,128)(2,1)S(1)}, u32[]{:S(2)}, u32[]{:S(2)}) collective-permute-start(bf16[1024,256]{1,0:T(8,128)(2,1)S(1)} %get-tuple-element.75), channel_id=1, source_target_pairs={{0,32},{2,10},{4,36},{6,14},{8,40},{10,18},{12,44},{14,22},{16,48}... | collective-permute-start | bytes 1572872 | tf_op jit(solution)/shard_map/ppermute | solution.py:481
  62.3 26.3 %copy-start.1 = (bf16[256,1024]{1,0:T(8,128)(2,1)S(1)}, bf16[256,1024]{1,0:T(8,128)(2,1)}, u32[]{:S(2)}) copy-start(bf16[256,1024]{1,0:T(8,128)(2,1)} %q_ref.3) | copy-start | bytes 1572868
  62.3 26.3 %copy-start.2 = (f32[256,128]{1,0:T(8,128)S(1)}, f32[256,128]{1,0:T(8,128)}, u32[]{:S(2)}) copy-start(f32[256,128]{1,0:T(8,128)} %get-tuple-element.55.cos_ref) | copy-start | bytes 393220
  67.7 9.4 %collective-permute-start.16 = (bf16[1024,256]{1,0:T(8,128)(2,1)S(1)}, bf16[1024,256]{1,0:T(8,128)(2,1)S(1)}, u32[]{:S(2)}, u32[]{:S(2)}) collective-permute-start(bf16[1024,256]{1,0:T(8,128)(2,1)S(1)} %get-tuple-element.81), channel_id=1, source_target_pairs={{0,96},{2,26},{4,100},{6,30},{8,104},{10,2},{12,108},{14,6},{16,11... | collective-permute-start | bytes 1572872 | tf_op jit(solution)/shard_map/ppermute | solution.py:481
  68.6 10.8 %collective-permute-start.17 = (bf16[1024,256]{1,0:T(8,128)(2,1)S(1)}, bf16[1024,256]{1,0:T(8,128)(2,1)S(1)}, u32[]{:S(2)}, u32[]{:S(2)}) collective-permute-start(bf16[1024,256]{1,0:T(8,128)(2,1)S(1)} %get-tuple-element.82), channel_id=1, source_target_pairs={{0,64},{2,18},{4,68},{6,22},{8,72},{10,26},{12,76},{14,30},{16,80}... | collective-permute-start | bytes 1572872 | tf_op jit(solution)/shard_map/ppermute | solution.py:481
  70.4 14.5 %collective-permute-start.18 = (bf16[1024,256]{1,0:T(8,128)(2,1)S(1)}, bf16[1024,256]{1,0:T(8,128)(2,1)S(1)}, u32[]{:S(2)}, u32[]{:S(2)}) collective-permute-start(bf16[1024,256]{1,0:T(8,128)(2,1)S(1)} %get-tuple-element.83), channel_id=1, source_target_pairs={{0,32},{2,10},{4,36},{6,14},{8,40},{10,18},{12,44},{14,22},{16,48}... | collective-permute-start | bytes 1572872 | tf_op jit(solution)/shard_map/ppermute | solution.py:481
  71.1 28.7 %copy-start.6 = (bf16[256,256]{1,0:T(8,128)(2,1)S(1)}, bf16[256,256]{1,0:T(8,128)(2,1)}, u32[]{:S(2)}) copy-start(bf16[256,256]{1,0:T(8,128)(2,1)} %key_ref.1) | copy-start | bytes 393220
  71.1 28.7 %copy-start.8 = (f32[128]{0:T(128)S(1)}, f32[128]{0:T(128)}, u32[]{:S(2)}) copy-start(f32[128]{0:T(128)} %param.13) | copy-start | bytes 1540
  74.9 1.6 %collective-permute-start.20 = (bf16[128,1024]{1,0:T(8,128)(2,1)S(1)}, bf16[128,1024]{1,0:T(8,128)(2,1)S(1)}, u32[]{:S(2)}, u32[]{:S(2)}) collective-permute-start(bf16[128,1024]{1,0:T(8,128)(2,1)S(1)} %get-tuple-element.92), channel_id=1, source_target_pairs={{0,2},{2,0},{4,6},{6,4},{1,3},{3,1},{5,7},{7,5},{8,10},{10,8},{12,... | collective-permute-start | bytes 786440 | tf_op jit(solution)/shard_map/ppermute | solution.py:485
  74.9 1.9 %collective-permute-start.19 = (bf16[128,1024]{1,0:T(8,128)(2,1)S(1)}, bf16[128,1024]{1,0:T(8,128)(2,1)S(1)}, u32[]{:S(2)}, u32[]{:S(2)}) collective-permute-start(bf16[128,1024]{1,0:T(8,128)(2,1)S(1)} %get-tuple-element.91), channel_id=1, source_target_pairs={{0,2},{2,0},{4,6},{6,4},{1,3},{3,1},{5,7},{7,5},{8,10},{10,8},{12,... | collective-permute-start | bytes 786440 | tf_op jit(solution)/shard_map/ppermute | solution.py:485
  85.4 13.0 %collective-permute-start.24 = (bf16[256,1024]{1,0:T(8,128)(2,1)S(1)}, bf16[256,1024]{1,0:T(8,128)(2,1)S(1)}, u32[]{:S(2)}, u32[]{:S(2)}) collective-permute-start(bf16[256,1024]{1,0:T(8,128)(2,1)S(1)} %get-tuple-element.99), channel_id=1, source_target_pairs={{0,2},{2,0},{4,6},{6,4},{1,3},{3,1},{5,7},{7,5},{8,10},{10,8},{12,... | collective-permute-start | bytes 1572872 | tf_op jit(solution)/shard_map/ppermute | solution.py:485
  85.5 14.3 %collective-permute-start.25 = (bf16[256,1024]{1,0:T(8,128)(2,1)S(1)}, bf16[256,1024]{1,0:T(8,128)(2,1)S(1)}, u32[]{:S(2)}, u32[]{:S(2)}) collective-permute-start(bf16[256,1024]{1,0:T(8,128)(2,1)S(1)} %add_convert_fusion), channel_id=1, source_target_pairs={{0,4},{2,6},{4,0},{6,2},{1,5},{3,7},{5,1},{7,3},{8,12},{10,14},{12... | collective-permute-start | bytes 1572872 | tf_op jit(solution)/shard_map/ppermute | solution.py:485
  86.0 6.4 %collective-permute-start.21 = (bf16[2,256,256]{2,1,0:T(8,128)(2,1)S(1)}, bf16[2,256,256]{2,1,0:T(8,128)(2,1)S(1)}, u32[]{:S(2)}, u32[]{:S(2)}) collective-permute-start(bf16[2,256,256]{2,1,0:T(8,128)(2,1)S(1)} %get-tuple-element.95), channel_id=1, source_target_pairs={{0,24},{2,98},{4,28},{6,102},{8,0},{10,106},{12,4},{14,110},{16,8}... | collective-permute-start | bytes 786440 | tf_op jit(solution)/shard_map/ppermute | solution.py:481
  87.7 8.0 %collective-permute-start.22 = (bf16[2,256,256]{2,1,0:T(8,128)(2,1)S(1)}, bf16[2,256,256]{2,1,0:T(8,128)(2,1)S(1)}, u32[]{:S(2)}, u32[]{:S(2)}) collective-permute-start(bf16[2,256,256]{2,1,0:T(8,128)(2,1)S(1)} %get-tuple-element.96), channel_id=1, source_target_pairs={{0,16},{2,66},{4,20},{6,70},{8,24},{10,74},{12,28},{14,78},{16,0},... | collective-permute-start | bytes 786440 | tf_op jit(solution)/shard_map/ppermute | solution.py:481
  88.3 10.1 %collective-permute-start.23 = (bf16[2,256,256]{2,1,0:T(8,128)(2,1)S(1)}, bf16[2,256,256]{2,1,0:T(8,128)(2,1)S(1)}, u32[]{:S(2)}, u32[]{:S(2)}) collective-permute-start(bf16[2,256,256]{2,1,0:T(8,128)(2,1)S(1)} %get-tuple-element.97), channel_id=1, source_target_pairs={{0,8},{2,34},{4,12},{6,38},{8,16},{10,42},{12,20},{14,46},{16,24},... | collective-permute-start | bytes 786440 | tf_op jit(solution)/shard_map/ppermute | solution.py:481
  (6 other events, 92.3 us)

commit v5 on v4

--- a/solution.py
+++ b/solution.py
@@ -522,17 +522,17 @@
     for g in range(heads):
         results = attention(block_tags, q, do, pieces[g], g, group)
         if g:
-            results, sums[g - 1] = lax.optimization_barrier((results, sums[g - 1]))
+            shares = out_product(me, attn[0], results[0], w_out)
+            results, shares, sums[g - 1] = lax.optimization_barrier((results, shares, sums[g - 1]))
         attn_g, dq_g, *grads = results
         attn.append(attn_g)
         dq.append(dq_g)
         sums.append(collect(grads, 1))
-    far_a, far_b, keep_far, near, keep_near = out_product(me, attn[0], attn[1], w_out)
+    far_a, far_b, keep_far, near, keep_near = shares
     far = jnp.concatenate([across(far_a, 1), across(far_b, 1)], axis=0)
     far = (keep_far.astype(jnp.float32) + far.astype(jnp.float32)).astype(jnp.bfloat16)
-    shares, far, near = lax.optimization_barrier((fold(sums), far, near))
-    parts = collect(shares, 0)
     terms = [keep_near, across(near, 1), across(far, 2)]
+    parts = collect(fold(sums), 0)
     d_q = query_back(q_raw, dq[0], dq[1], q_gain, cosine, sine)
     attn_out, key_gradient, value_gradient = finish(keys, k_gain, cosine, sine, parts, terms)
     return attn_out, d_q, key_gradient, value_gradient

time: 103 us -> 102 us (level)
    ppermute x8, waiting for transfers between devices: 4.22 us -> 1.37 us  [across(): return lax.ppermute(value, 'ffn', [(s, s ^ mask) for s in range(4)])]
    ppermute x18, waiting for transfers between devices: 24 us -> 25.9 us  [hop(): return lax.ppermute(value, ('ctx', 'ffn'), pairs)]
  transfers between devices with their start and end apart: 26 -> 26, of which waited for: 15 -> 12; matrix products, arithmetic and copies ran while one was open for 4% -> 4% of each run, Pallas kernels for 32% -> 32%
where the time goes in v5:
time: 102 us; the launch traced here: 101 us
  Pallas kernels  37.1 us (36%)
  waiting for transfers between devices  27.3 us (27%)
  starting transfers between devices  27 us (26%)
  local copies, waits for them, and re-layouts  8.45 us (8%)
    ppermute x18, waiting for transfers between devices, hop(): return lax.ppermute(value, ('ctx', 'ffn'), pairs)  25.9 us
    ppermute x18, starting transfers between devices, hop(): return lax.ppermute(value, ('ctx', 'ffn'), pairs)  25.1 us
    pallas_call x2, Pallas kernels, attention(): pl.pallas_call(functools.partial(attention_kernel, first=g * group, nclea...  18.4 us
    pallas_call x1, Pallas kernels, d_attn_product(): pl.pallas_call(d_attn_kernel, grid_spec=pltpu.PrefetchScalarGridSpec(num_...  4.59 us
    unnamed x24, local copies, waits for them, and re-layouts  4.48 us
    squeeze x4, local copies, waits for them, and re-layouts, per_device(): part[g]  3.94 us
    pallas_call x1, Pallas kernels, out_product(): pl.pallas_call(out_kernel, grid_spec=pltpu.PrefetchScalarGridSpec(num_sca...  3.7 us
    pallas_call x1, Pallas kernels, query_prep(): pl.pallas_call(query_kernel, grid=(1,), in_specs=[whole(*q_raw.shape), wh...  3.06 us
  transfers between devices with their start and end apart: 26, of which 12 were waited for; matrix products, arithmetic and copies ran while one was open for 4% of the time, Pallas kernels for 32%

profile of v5, /device:TPU:96, one launch (start us, length us, event | category | flops | bytes accessed | tf_op | source)
XLA Modules:
  0.0 101.1 jit_solution(17737156588200044543)
XLA Ops:
  0.6 3.0 %key_prep.1 = (bf16[2,256,256]{2,1,0:T(8,128)(2,1)}, f32[256,128]{1,0:T(8,128)}, f32[256,128]{1,0:T(8,128)}) custom-call(s32[64]{0:T(128)} %tags_ref.5, bf16[256,256]{1,0:T(8,128)(2,1)} %key_ref.1, bf16[256,256]{1,0:T(8,128)(2,1)} %value_hbm.1, f32[1,128]{1,0:T(1,128)} %bitcast.23, f32[192,128]{1,0:T(8,128)} %constant.8.clone.table_hbm), custom_call_target="tpu_custom_call" | custom-call | bytes 1048576 | tf_op jit(solution)/shard_map/key_prep/pallas_call | solution.py:111
  3.6 2.8 %collective-permute-start.2 = (bf16[2,256,256]{2,1,0:T(8,128)(2,1)}, bf16[2,256,256]{2,1,0:T(8,128)(2,1)}, u32[]{:S(2)}, u32[]{:S(2)}) collective-permute-start(bf16[2,256,256]{2,1,0:T(8,128)(2,1)} %get-tuple-element.55), channel_id=1, source_target_pairs={{0,24},{2,98},{4,28},{6,102},{8,0},{10,106},{12,4},{14,110},{16,8}... | collective-permute-start | bytes 786440 | tf_op jit(solution)/shard_map/ppermute | solution.py:481
  8.6 1.0 slice_bitcast_fusion.6
  9.6 3.1 %query_prep.1.q_ref = bf16[256,1024]{1,0:T(8,128)(2,1)} custom-call(bf16[256,1024]{1,0:T(8,128)(2,1)} %q_ref.3, f32[1,128]{1,0:T(1,128)} %bitcast.21, f32[256,128]{1,0:T(8,128)} %get-tuple-element.53.cos_ref, f32[256,128]{1,0:T(8,128)} %get-tuple-element.54.sin_ref), custom_call_target="tpu_custom_call" | custom-call | bytes 4194304 | tf_op jit(solution)/shard_map/query_prep/pallas_call | solution.py:137
  13.5 1.0 slice_bitcast_fusion
  14.8 1.0 slice_bitcast_fusion.1
  15.8 1.7 %collective-permute-done = bf16[2,256,256]{2,1,0:T(8,128)(2,1)} collective-permute-done((bf16[2,256,256]{2,1,0:T(8,128)(2,1)}, bf16[2,256,256]{2,1,0:T(8,128)(2,1)}, u32[]{:S(2)}, u32[]{:S(2)}) %collective-permute-start) | collective-permute-done | bytes 262176 | tf_op jit(solution)/shard_map/ppermute | solution.py:481
  17.5 1.0 slice_bitcast_fusion.2
  18.5 1.6 %collective-permute-start.7 = (bf16[1024,256]{1,0:T(8,128)(2,1)S(1)}, bf16[1024,256]{1,0:T(8,128)(2,1)}, u32[]{:S(2)}, u32[]{:S(2)}) collective-permute-start(bf16[1024,256]{1,0:T(8,128)(2,1)S(1)} %pad_maximum_fusion.refs_0_), channel_id=1, source_target_pairs={{0,32},{2,10},{4,36},{6,14},{8,40},{10,18},{12,44},{14,22},{16,48}... | collective-permute-start | bytes 1572872 | tf_op jit(solution)/shard_map/ppermute | solution.py:481
  20.2 2.9 %collective-permute-start.8 = (bf16[1024,256]{1,0:T(8,128)(2,1)S(1)}, bf16[1024,256]{1,0:T(8,128)(2,1)}, u32[]{:S(2)}, u32[]{:S(2)}) collective-permute-start(bf16[1024,256]{1,0:T(8,128)(2,1)S(1)} %pad_maximum_fusion.refs_0_), channel_id=1, source_target_pairs={{0,64},{2,18},{4,68},{6,22},{8,72},{10,26},{12,76},{14,30},{16,80}... | collective-permute-start | bytes 1572872 | tf_op jit(solution)/shard_map/ppermute | solution.py:481
  23.1 1.3 %collective-permute-start.9 = (bf16[1024,256]{1,0:T(8,128)(2,1)S(1)}, bf16[1024,256]{1,0:T(8,128)(2,1)}, u32[]{:S(2)}, u32[]{:S(2)}) collective-permute-start(bf16[1024,256]{1,0:T(8,128)(2,1)S(1)} %pad_maximum_fusion.refs_0_), channel_id=1, source_target_pairs={{0,96},{2,26},{4,100},{6,30},{8,104},{10,2},{12,108},{14,6},{16,11... | collective-permute-start | bytes 1572872 | tf_op jit(solution)/shard_map/ppermute | solution.py:481
  26.4 3.4 %copy-done = bf16[1024,4096]{1,0:T(8,128)(2,1)S(1)} copy-done((bf16[1024,4096]{1,0:T(8,128)(2,1)S(1)}, bf16[1024,4096]{1,0:T(8,128)(2,1)}, u32[]{:S(2)}) %copy-start) | copy-done | bytes 8388632
  29.8 1.0 %copy-done.4 = bf16[256,1024]{1,0:T(8,128)(2,1)S(1)} copy-done((bf16[256,1024]{1,0:T(8,128)(2,1)S(1)}, bf16[256,1024]{1,0:T(8,128)(2,1)}, u32[]{:S(2)}) %copy-start.4) | copy-done | bytes 524312
  30.9 4.6 %d_attn_product.1.do_ref = bf16[256,1024]{1,0:T(8,128)(2,1)S(1)} custom-call(s32[1]{0:T(128)} %bitcast.10.me_ref, bf16[256,1024]{1,0:T(8,128)(2,1)S(1)} %copy-done.4, bf16[256,1024]{1,0:T(8,128)(2,1)} %collective-permute-done.3.p1, bf16[256,1024]{1,0:T(8,128)(2,1)S(1)} %collective-permute-done.4.p2, bf16[128,1024]{1,0:T(8,128)(2,1)S(1)} %collective-permute-done.5.p3a, ...), custom_call_target="tpu_custom_call" | custom-call | flops 1 | bytes 1 | tf_op jit(solution)/shard_map/d_attn_product/pallas_call | solution.py:177
  35.9 1.6 %collective-permute-start.10 = (bf16[1024,256]{1,0:T(8,128)(2,1)S(1)}, bf16[1024,256]{1,0:T(8,128)(2,1)S(1)}, u32[]{:S(2)}, u32[]{:S(2)}) collective-permute-start(bf16[1024,256]{1,0:T(8,128)(2,1)S(1)} %pad_maximum_fusion.1.refs_0_), channel_id=1, source_target_pairs={{0,32},{2,10},{4,36},{6,14},{8,40},{10,18},{12,44},{14,22},{16,48}... | collective-permute-start | bytes 1572872 | tf_op jit(solution)/shard_map/ppermute | solution.py:481
  37.6 2.1 %collective-permute-start.11 = (bf16[1024,256]{1,0:T(8,128)(2,1)S(1)}, bf16[1024,256]{1,0:T(8,128)(2,1)S(1)}, u32[]{:S(2)}, u32[]{:S(2)}) collective-permute-start(bf16[1024,256]{1,0:T(8,128)(2,1)S(1)} %pad_maximum_fusion.1.refs_0_), channel_id=1, source_target_pairs={{0,64},{2,18},{4,68},{6,22},{8,72},{10,26},{12,76},{14,30},{16,80}... | collective-permute-start | bytes 1572872 | tf_op jit(solution)/shard_map/ppermute | solution.py:481
  39.7 1.7 %collective-permute-start.12 = (bf16[1024,256]{1,0:T(8,128)(2,1)S(1)}, bf16[1024,256]{1,0:T(8,128)(2,1)S(1)}, u32[]{:S(2)}, u32[]{:S(2)}) collective-permute-start(bf16[1024,256]{1,0:T(8,128)(2,1)S(1)} %pad_maximum_fusion.1.refs_0_), channel_id=1, source_target_pairs={{0,96},{2,26},{4,100},{6,30},{8,104},{10,2},{12,108},{14,6},{16,11... | collective-permute-start | bytes 1572872 | tf_op jit(solution)/shard_map/ppermute | solution.py:481
  41.4 9.6 %attention.3 = (bf16[256,512]{1,0:T(8,128)(2,1)S(1)}, f32[256,512]{1,0:T(8,128)S(1)}, bf16[1024,256]{1,0:T(8,128)(2,1)S(1)}, bf16[1024,256]{1,0:T(8,128)(2,1)S(1...) custom-call(s32[64]{0:T(128)S(1)} %copy-done.9, bf16[256,1024]{1,0:T(8,128)(2,1)S(1)} %copy-done.5, ...), custom_call_target="tpu_custom_call" | custom-call | flops 6442450944 | bytes 4194304 | tf_op jit(solution)/shard_map/attention/pallas_call | solution.py:374
  51.4 2.1 %collective-permute-start.14 = (bf16[1024,256]{1,0:T(8,128)(2,1)S(1)}, bf16[1024,256]{1,0:T(8,128)(2,1)S(1)}, u32[]{:S(2)}, u32[]{:S(2)}) collective-permute-start(bf16[1024,256]{1,0:T(8,128)(2,1)S(1)} %get-tuple-element.78), channel_id=1, source_target_pairs={{0,64},{2,18},{4,68},{6,22},{8,72},{10,26},{12,76},{14,30},{16,80}... | collective-permute-start | bytes 1572872 | tf_op jit(solution)/shard_map/ppermute | solution.py:481
  53.5 8.8 %attention.2 = (bf16[256,512]{1,0:T(8,128)(2,1)S(1)}, f32[256,512]{1,0:T(8,128)S(1)}, bf16[1024,256]{1,0:T(8,128)(2,1)S(1)}, bf16[1024,256]{1,0:T(8,128)(2,1)S(1...) custom-call(s32[64]{0:T(128)S(1)} %copy-done.9, bf16[256,1024]{1,0:T(8,128)(2,1)S(1)} %copy-done.5, ...), custom_call_target="tpu_custom_call" | custom-call | flops 6442450944 | bytes 4194304 | tf_op jit(solution)/shard_map/attention/pallas_call | solution.py:374
  62.4 3.7 %out_product.1 = (bf16[128,1024]{1,0:T(8,128)(2,1)S(1)}, bf16[128,1024]{1,0:T(8,128)(2,1)S(1)}, bf16[256,1024]{1,0:T(8,128)(2,1)S(1)}, bf16[256,1024]{1,0:T(8,128)(2,1)S(1)}, bf16[256,1024]{1,0:T(8,128)(2,1)S(1)}) custom-call(s32[1]{0:T(128)} %bitcast.10.me_ref, bf16[256,512]{1,0:T(8,128)(2,1)S(1)} %get-tuple-element.70.a0_ref, ...), custom_call_target="tpu_custom_call" | custom-call | flops 1 | bytes 1 | tf_op jit(solution)/shard_map/out_product/pallas_call | solution.py:220
  66.1 1.5 %collective-permute-done.15.refs_3_ = bf16[1024,256]{1,0:T(8,128)(2,1)S(1)} collective-permute-done((bf16[1024,256]{1,0:T(8,128)(2,1)S(1)}, bf16[1024,256]{1,0:T(8,128)(2,1)S(1)}, u32[]{:S(2)}, u32[]{:S(2)}) %collective-permute-start.15) | collective-permute-done | bytes 524320 | tf_op jit(solution)/shard_map/ppermute | solution.py:481
  68.2 1.8 %collective-permute-start.16 = (bf16[1024,256]{1,0:T(8,128)(2,1)S(1)}, bf16[1024,256]{1,0:T(8,128)(2,1)S(1)}, u32[]{:S(2)}, u32[]{:S(2)}) collective-permute-start(bf16[1024,256]{1,0:T(8,128)(2,1)S(1)} %get-tuple-element.85), channel_id=1, source_target_pairs={{0,96},{2,26},{4,100},{6,30},{8,104},{10,2},{12,108},{14,6},{16,11... | collective-permute-start | bytes 1572872 | tf_op jit(solution)/shard_map/ppermute | solution.py:481
  70.9 1.0 %collective-permute-start.18 = (bf16[1024,256]{1,0:T(8,128)(2,1)S(1)}, bf16[1024,256]{1,0:T(8,128)(2,1)S(1)}, u32[]{:S(2)}, u32[]{:S(2)}) collective-permute-start(bf16[1024,256]{1,0:T(8,128)(2,1)S(1)} %get-tuple-element.87), channel_id=1, source_target_pairs={{0,32},{2,10},{4,36},{6,14},{8,40},{10,18},{12,44},{14,22},{16,48}... | collective-permute-start | bytes 1572872 | tf_op jit(solution)/shard_map/ppermute | solution.py:481
  72.6 9.7 %collective-permute-done.16.refs_5_ = bf16[1024,256]{1,0:T(8,128)(2,1)S(1)} collective-permute-done((bf16[1024,256]{1,0:T(8,128)(2,1)S(1)}, bf16[1024,256]{1,0:T(8,128)(2,1)S(1)}, u32[]{:S(2)}, u32[]{:S(2)}) %collective-permute-start.16) | collective-permute-done | bytes 524320 | tf_op jit(solution)/shard_map/ppermute | solution.py:481
  82.3 3.9 %collective-permute-done.18.refs_7_ = bf16[1024,256]{1,0:T(8,128)(2,1)S(1)} collective-permute-done((bf16[1024,256]{1,0:T(8,128)(2,1)S(1)}, bf16[1024,256]{1,0:T(8,128)(2,1)S(1)}, u32[]{:S(2)}, u32[]{:S(2)}) %collective-permute-start.18) | collective-permute-done | bytes 524320 | tf_op jit(solution)/shard_map/ppermute | solution.py:481
  86.8 2.0 %collective-permute-start.19 = (bf16[2,256,256]{2,1,0:T(8,128)(2,1)S(1)}, bf16[2,256,256]{2,1,0:T(8,128)(2,1)S(1)}, u32[]{:S(2)}, u32[]{:S(2)}) collective-permute-start(bf16[2,256,256]{2,1,0:T(8,128)(2,1)S(1)} %get-tuple-element.89), channel_id=1, source_target_pairs={{0,24},{2,98},{4,28},{6,102},{8,0},{10,106},{12,4},{14,110},{16,8}... | collective-permute-start | bytes 786440 | tf_op jit(solution)/shard_map/ppermute | solution.py:481
  89.8 2.3 %query_back.1 = f32[256,1024]{1,0:T(8,128)} custom-call(bf16[256,1024]{1,0:T(8,128)(2,1)S(1)} %copy-done.1, f32[256,512]{1,0:T(8,128)S(1)} %get-tuple-element.98.a_ref, f32[256,512]{1,0:T(8,128)S(1)} %get-tuple-element.99.b_ref, f32[1,128]{1,0:T(1,128)S(1)} %bitcast.22, f32[256,128]{1,0:T(8,128)S(1)} %copy-done.2, f32[256,128]{1,0:T(8,128)S(1)} %copy-done.3), custom_call_target="tpu_custom_call" | custom-call | flops 1 | bytes 1 | tf_op jit(solution)/shard_map/query_back/pallas_call | solution.py:410
  92.0 1.4 %collective-permute-done.19.b = bf16[2,256,256]{2,1,0:T(8,128)(2,1)S(1)} collective-permute-done((bf16[2,256,256]{2,1,0:T(8,128)(2,1)S(1)}, bf16[2,256,256]{2,1,0:T(8,128)(2,1)S(1)}, u32[]{:S(2)}, u32[]{:S(2)}) %collective-permute-start.19) | collective-permute-done | bytes 262176 | tf_op jit(solution)/shard_map/ppermute | solution.py:481
  93.5 3.3 %collective-permute-done.20.c = bf16[2,256,256]{2,1,0:T(8,128)(2,1)S(1)} collective-permute-done((bf16[2,256,256]{2,1,0:T(8,128)(2,1)S(1)}, bf16[2,256,256]{2,1,0:T(8,128)(2,1)S(1)}, u32[]{:S(2)}, u32[]{:S(2)}) %collective-permute-start.20) | collective-permute-done | bytes 262176 | tf_op jit(solution)/shard_map/ppermute | solution.py:481
  96.8 2.7 %collective-permute-done.21.d = bf16[2,256,256]{2,1,0:T(8,128)(2,1)S(1)} collective-permute-done((bf16[2,256,256]{2,1,0:T(8,128)(2,1)S(1)}, bf16[2,256,256]{2,1,0:T(8,128)(2,1)S(1)}, u32[]{:S(2)}, u32[]{:S(2)}) %collective-permute-start.21) | collective-permute-done | bytes 262176 | tf_op jit(solution)/shard_map/ppermute | solution.py:481
  99.5 1.6 %finish.1 = (bf16[256,1024]{1,0:T(8,128)(2,1)}, f32[256,256]{1,0:T(8,128)}, f32[256,256]{1,0:T(8,128)}) custom-call(bf16[256,256]{1,0:T(8,128)(2,1)S(1)} %copy-done.6, f32[1,128]{1,0:T(1,128)S(1)} %bitcast.24, f32[256,128]{1,0:T(8,128)S(1)} %copy-done.2, f32[256,128]{1,0:T(8,128)S(1)} %copy-done.3, bf16[2,256,256]{2,1,0:T(8,128)(2,1)S(1)} %get-tuple-element.88.a, ...), custom_call_target="tpu_custom_call" | custom-call | bytes 2097152 | tf_op jit(solution)/shard_map/finish/pallas_call | solution.py:436
  (62 shorter events, 9.8 us)
Async XLA Ops:
  3.6 9.9 %collective-permute-start.2 = (bf16[2,256,256]{2,1,0:T(8,128)(2,1)}, bf16[2,256,256]{2,1,0:T(8,128)(2,1)}, u32[]{:S(2)}, u32[]{:S(2)}) collective-permute-start(bf16[2,256,256]{2,1,0:T(8,128)(2,1)} %get-tuple-element.55), channel_id=1, source_target_pairs={{0,24},{2,98},{4,28},{6,102},{8,0},{10,106},{12,4},{14,110},{16,8}... | collective-permute-start | bytes 786440 | tf_op jit(solution)/shard_map/ppermute | solution.py:481
  6.5 8.3 %collective-permute-start.1 = (bf16[2,256,256]{2,1,0:T(8,128)(2,1)}, bf16[2,256,256]{2,1,0:T(8,128)(2,1)}, u32[]{:S(2)}, u32[]{:S(2)}) collective-permute-start(bf16[2,256,256]{2,1,0:T(8,128)(2,1)} %get-tuple-element.55), channel_id=1, source_target_pairs={{0,16},{2,66},{4,20},{6,70},{8,24},{10,74},{12,28},{14,78},{16,0},... | collective-permute-start | bytes 786440 | tf_op jit(solution)/shard_map/ppermute | solution.py:481
  7.3 10.2 %collective-permute-start = (bf16[2,256,256]{2,1,0:T(8,128)(2,1)}, bf16[2,256,256]{2,1,0:T(8,128)(2,1)}, u32[]{:S(2)}, u32[]{:S(2)}) collective-permute-start(bf16[2,256,256]{2,1,0:T(8,128)(2,1)} %get-tuple-element.55), channel_id=1, source_target_pairs={{0,8},{2,34},{4,12},{6,38},{8,16},{10,42},{12,20},{14,46},{16,24},... | collective-permute-start | bytes 786440 | tf_op jit(solution)/shard_map/ppermute | solution.py:481
  8.2 16.4 %collective-permute-start.3 = (bf16[256,1024]{1,0:T(8,128)(2,1)}, bf16[256,1024]{1,0:T(8,128)(2,1)}, u32[]{:S(2)}, u32[]{:S(2)}) collective-permute-start(bf16[256,1024]{1,0:T(8,128)(2,1)} %p0.1), channel_id=1, source_target_pairs={{0,2},{2,0},{4,6},{6,4},{1,3},{3,1},{5,7},{7,5},{8,10},{10,8},{12,... | collective-permute-start | bytes 1572872 | tf_op jit(solution)/shard_map/ppermute | solution.py:485
  8.2 16.2 %collective-permute-start.4 = (bf16[256,1024]{1,0:T(8,128)(2,1)}, bf16[256,1024]{1,0:T(8,128)(2,1)S(1)}, u32[]{:S(2)}, u32[]{:S(2)}) collective-permute-start(bf16[256,1024]{1,0:T(8,128)(2,1)} %p0.1), channel_id=1, source_target_pairs={{0,4},{2,6},{4,0},{6,2},{1,5},{3,7},{5,1},{7,3},{8,12},{10,14},{12... | collective-permute-start | bytes 1572872 | tf_op jit(solution)/shard_map/ppermute | solution.py:485
  9.6 31.9 %copy-start.9 = (s32[64]{0:T(128)S(1)}, s32[64]{0:T(128)}, u32[]{:S(2)}) copy-start(s32[64]{0:T(128)} %tags_ref.5) | copy-start | bytes 772
  12.6 28.8 %copy-start.5 = (bf16[256,1024]{1,0:T(8,128)(2,1)S(1)}, bf16[256,1024]{1,0:T(8,128)(2,1)}, u32[]{:S(2)}) copy-start(bf16[256,1024]{1,0:T(8,128)(2,1)} %query_prep.1.q_ref) | copy-start | bytes 1572868
  18.5 17.0 %collective-permute-start.7 = (bf16[1024,256]{1,0:T(8,128)(2,1)S(1)}, bf16[1024,256]{1,0:T(8,128)(2,1)}, u32[]{:S(2)}, u32[]{:S(2)}) collective-permute-start(bf16[1024,256]{1,0:T(8,128)(2,1)S(1)} %pad_maximum_fusion.refs_0_), channel_id=1, source_target_pairs={{0,32},{2,10},{4,36},{6,14},{8,40},{10,18},{12,44},{14,22},{16,48}... | collective-permute-start | bytes 1572872 | tf_op jit(solution)/shard_map/ppermute | solution.py:481
  20.2 15.8 %collective-permute-start.8 = (bf16[1024,256]{1,0:T(8,128)(2,1)S(1)}, bf16[1024,256]{1,0:T(8,128)(2,1)}, u32[]{:S(2)}, u32[]{:S(2)}) collective-permute-start(bf16[1024,256]{1,0:T(8,128)(2,1)S(1)} %pad_maximum_fusion.refs_0_), channel_id=1, source_target_pairs={{0,64},{2,18},{4,68},{6,22},{8,72},{10,26},{12,76},{14,30},{16,80}... | collective-permute-start | bytes 1572872 | tf_op jit(solution)/shard_map/ppermute | solution.py:481
  23.1 12.9 %collective-permute-start.9 = (bf16[1024,256]{1,0:T(8,128)(2,1)S(1)}, bf16[1024,256]{1,0:T(8,128)(2,1)}, u32[]{:S(2)}, u32[]{:S(2)}) collective-permute-start(bf16[1024,256]{1,0:T(8,128)(2,1)S(1)} %pad_maximum_fusion.refs_0_), channel_id=1, source_target_pairs={{0,96},{2,26},{4,100},{6,30},{8,104},{10,2},{12,108},{14,6},{16,11... | collective-permute-start | bytes 1572872 | tf_op jit(solution)/shard_map/ppermute | solution.py:481
  24.4 1.6 %collective-permute-start.5 = (bf16[128,1024]{1,0:T(8,128)(2,1)S(1)}, bf16[128,1024]{1,0:T(8,128)(2,1)S(1)}, u32[]{:S(2)}, u32[]{:S(2)}) collective-permute-start(bf16[128,1024]{1,0:T(8,128)(2,1)S(1)} %get-tuple-element.103), channel_id=1, source_target_pairs={{0,2},{2,0},{4,6},{6,4},{1,3},{3,1},{5,7},{7,5},{8,10},{10,8},{12,... | collective-permute-start | bytes 786440 | tf_op jit(solution)/shard_map/ppermute | solution.py:485
  24.6 1.9 %collective-permute-start.6 = (bf16[128,1024]{1,0:T(8,128)(2,1)S(1)}, bf16[128,1024]{1,0:T(8,128)(2,1)S(1)}, u32[]{:S(2)}, u32[]{:S(2)}) collective-permute-start(bf16[128,1024]{1,0:T(8,128)(2,1)S(1)} %get-tuple-element.102), channel_id=1, source_target_pairs={{0,2},{2,0},{4,6},{6,4},{1,3},{3,1},{5,7},{7,5},{8,10},{10,8},{12,... | collective-permute-start | bytes 786440 | tf_op jit(solution)/shard_map/ppermute | solution.py:485
  35.9 17.5 %collective-permute-start.10 = (bf16[1024,256]{1,0:T(8,128)(2,1)S(1)}, bf16[1024,256]{1,0:T(8,128)(2,1)S(1)}, u32[]{:S(2)}, u32[]{:S(2)}) collective-permute-start(bf16[1024,256]{1,0:T(8,128)(2,1)S(1)} %pad_maximum_fusion.1.refs_0_), channel_id=1, source_target_pairs={{0,32},{2,10},{4,36},{6,14},{8,40},{10,18},{12,44},{14,22},{16,48}... | collective-permute-start | bytes 1572872 | tf_op jit(solution)/shard_map/ppermute | solution.py:481
  37.6 15.9 %collective-permute-start.11 = (bf16[1024,256]{1,0:T(8,128)(2,1)S(1)}, bf16[1024,256]{1,0:T(8,128)(2,1)S(1)}, u32[]{:S(2)}, u32[]{:S(2)}) collective-permute-start(bf16[1024,256]{1,0:T(8,128)(2,1)S(1)} %pad_maximum_fusion.1.refs_0_), channel_id=1, source_target_pairs={{0,64},{2,18},{4,68},{6,22},{8,72},{10,26},{12,76},{14,30},{16,80}... | collective-permute-start | bytes 1572872 | tf_op jit(solution)/shard_map/ppermute | solution.py:481
  39.7 13.8 %collective-permute-start.12 = (bf16[1024,256]{1,0:T(8,128)(2,1)S(1)}, bf16[1024,256]{1,0:T(8,128)(2,1)S(1)}, u32[]{:S(2)}, u32[]{:S(2)}) collective-permute-start(bf16[1024,256]{1,0:T(8,128)(2,1)S(1)} %pad_maximum_fusion.1.refs_0_), channel_id=1, source_target_pairs={{0,96},{2,26},{4,100},{6,30},{8,104},{10,2},{12,108},{14,6},{16,11... | collective-permute-start | bytes 1572872 | tf_op jit(solution)/shard_map/ppermute | solution.py:481
  51.0 15.1 %collective-permute-start.13 = (bf16[1024,256]{1,0:T(8,128)(2,1)S(1)}, bf16[1024,256]{1,0:T(8,128)(2,1)S(1)}, u32[]{:S(2)}, u32[]{:S(2)}) collective-permute-start(bf16[1024,256]{1,0:T(8,128)(2,1)S(1)} %get-tuple-element.77), channel_id=1, source_target_pairs={{0,96},{2,26},{4,100},{6,30},{8,104},{10,2},{12,108},{14,6},{16,11... | collective-permute-start | bytes 1572872 | tf_op jit(solution)/shard_map/ppermute | solution.py:481
  51.4 14.8 %collective-permute-start.14 = (bf16[1024,256]{1,0:T(8,128)(2,1)S(1)}, bf16[1024,256]{1,0:T(8,128)(2,1)S(1)}, u32[]{:S(2)}, u32[]{:S(2)}) collective-permute-start(bf16[1024,256]{1,0:T(8,128)(2,1)S(1)} %get-tuple-element.78), channel_id=1, source_target_pairs={{0,64},{2,18},{4,68},{6,22},{8,72},{10,26},{12,76},{14,30},{16,80}... | collective-permute-start | bytes 1572872 | tf_op jit(solution)/shard_map/ppermute | solution.py:481
  53.5 14.2 %collective-permute-start.15 = (bf16[1024,256]{1,0:T(8,128)(2,1)S(1)}, bf16[1024,256]{1,0:T(8,128)(2,1)S(1)}, u32[]{:S(2)}, u32[]{:S(2)}) collective-permute-start(bf16[1024,256]{1,0:T(8,128)(2,1)S(1)} %get-tuple-element.79), channel_id=1, source_target_pairs={{0,32},{2,10},{4,36},{6,14},{8,40},{10,18},{12,44},{14,22},{16,48}... | collective-permute-start | bytes 1572872 | tf_op jit(solution)/shard_map/ppermute | solution.py:481
  62.3 27.5 %copy-start.1 = (bf16[256,1024]{1,0:T(8,128)(2,1)S(1)}, bf16[256,1024]{1,0:T(8,128)(2,1)}, u32[]{:S(2)}) copy-start(bf16[256,1024]{1,0:T(8,128)(2,1)} %q_ref.3) | copy-start | bytes 1572868
  62.3 27.4 %copy-start.2 = (f32[256,128]{1,0:T(8,128)S(1)}, f32[256,128]{1,0:T(8,128)}, u32[]{:S(2)}) copy-start(f32[256,128]{1,0:T(8,128)} %get-tuple-element.53.cos_ref) | copy-start | bytes 393220
  62.4 37.1 %copy-start.6 = (bf16[256,256]{1,0:T(8,128)(2,1)S(1)}, bf16[256,256]{1,0:T(8,128)(2,1)}, u32[]{:S(2)}) copy-start(bf16[256,256]{1,0:T(8,128)(2,1)} %key_ref.1) | copy-start | bytes 393220
  62.4 37.1 %copy-start.8 = (f32[128]{0:T(128)S(1)}, f32[128]{0:T(128)}, u32[]{:S(2)}) copy-start(f32[128]{0:T(128)} %param.13) | copy-start | bytes 1540
  67.7 4.3 %collective-permute-start.24 = (bf16[128,1024]{1,0:T(8,128)(2,1)S(1)}, bf16[128,1024]{1,0:T(8,128)(2,1)S(1)}, u32[]{:S(2)}, u32[]{:S(2)}) collective-permute-start(bf16[128,1024]{1,0:T(8,128)(2,1)S(1)} %get-tuple-element.96), channel_id=1, source_target_pairs={{0,2},{2,0},{4,6},{6,4},{1,3},{3,1},{5,7},{7,5},{8,10},{10,8},{12,... | collective-permute-start | bytes 786440 | tf_op jit(solution)/shard_map/ppermute | solution.py:485
  67.7 4.3 %collective-permute-start.23 = (bf16[128,1024]{1,0:T(8,128)(2,1)S(1)}, bf16[128,1024]{1,0:T(8,128)(2,1)S(1)}, u32[]{:S(2)}, u32[]{:S(2)}) collective-permute-start(bf16[128,1024]{1,0:T(8,128)(2,1)S(1)} %get-tuple-element.95), channel_id=1, source_target_pairs={{0,2},{2,0},{4,6},{6,4},{1,3},{3,1},{5,7},{7,5},{8,10},{10,8},{12,... | collective-permute-start | bytes 786440 | tf_op jit(solution)/shard_map/ppermute | solution.py:485
  68.2 14.1 %collective-permute-start.16 = (bf16[1024,256]{1,0:T(8,128)(2,1)S(1)}, bf16[1024,256]{1,0:T(8,128)(2,1)S(1)}, u32[]{:S(2)}, u32[]{:S(2)}) collective-permute-start(bf16[1024,256]{1,0:T(8,128)(2,1)S(1)} %get-tuple-element.85), channel_id=1, source_target_pairs={{0,96},{2,26},{4,100},{6,30},{8,104},{10,2},{12,108},{14,6},{16,11... | collective-permute-start | bytes 1572872 | tf_op jit(solution)/shard_map/ppermute | solution.py:481
  69.9 12.4 %collective-permute-start.17 = (bf16[1024,256]{1,0:T(8,128)(2,1)S(1)}, bf16[1024,256]{1,0:T(8,128)(2,1)S(1)}, u32[]{:S(2)}, u32[]{:S(2)}) collective-permute-start(bf16[1024,256]{1,0:T(8,128)(2,1)S(1)} %get-tuple-element.86), channel_id=1, source_target_pairs={{0,64},{2,18},{4,68},{6,22},{8,72},{10,26},{12,76},{14,30},{16,80}... | collective-permute-start | bytes 1572872 | tf_op jit(solution)/shard_map/ppermute | solution.py:481
  70.9 15.4 %collective-permute-start.18 = (bf16[1024,256]{1,0:T(8,128)(2,1)S(1)}, bf16[1024,256]{1,0:T(8,128)(2,1)S(1)}, u32[]{:S(2)}, u32[]{:S(2)}) collective-permute-start(bf16[1024,256]{1,0:T(8,128)(2,1)S(1)} %get-tuple-element.87), channel_id=1, source_target_pairs={{0,32},{2,10},{4,36},{6,14},{8,40},{10,18},{12,44},{14,22},{16,48}... | collective-permute-start | bytes 1572872 | tf_op jit(solution)/shard_map/ppermute | solution.py:481
  71.9 20.1 %collective-permute-start.22 = (bf16[256,1024]{1,0:T(8,128)(2,1)S(1)}, bf16[256,1024]{1,0:T(8,128)(2,1)S(1)}, u32[]{:S(2)}, u32[]{:S(2)}) collective-permute-start(bf16[256,1024]{1,0:T(8,128)(2,1)S(1)} %get-tuple-element.93), channel_id=1, source_target_pairs={{0,2},{2,0},{4,6},{6,4},{1,3},{3,1},{5,7},{7,5},{8,10},{10,8},{12,... | collective-permute-start | bytes 1572872 | tf_op jit(solution)/shard_map/ppermute | solution.py:485
  72.1 27.4 %collective-permute-start.25 = (bf16[256,1024]{1,0:T(8,128)(2,1)S(1)}, bf16[256,1024]{1,0:T(8,128)(2,1)S(1)}, u32[]{:S(2)}, u32[]{:S(2)}) collective-permute-start(bf16[256,1024]{1,0:T(8,128)(2,1)S(1)} %add_convert_fusion), channel_id=1, source_target_pairs={{0,4},{2,6},{4,0},{6,2},{1,5},{3,7},{5,1},{7,3},{8,12},{10,14},{12... | collective-permute-start | bytes 1572872 | tf_op jit(solution)/shard_map/ppermute | solution.py:485
  86.8 6.7 %collective-permute-start.19 = (bf16[2,256,256]{2,1,0:T(8,128)(2,1)S(1)}, bf16[2,256,256]{2,1,0:T(8,128)(2,1)S(1)}, u32[]{:S(2)}, u32[]{:S(2)}) collective-permute-start(bf16[2,256,256]{2,1,0:T(8,128)(2,1)S(1)} %get-tuple-element.89), channel_id=1, source_target_pairs={{0,24},{2,98},{4,28},{6,102},{8,0},{10,106},{12,4},{14,110},{16,8}... | collective-permute-start | bytes 786440 | tf_op jit(solution)/shard_map/ppermute | solution.py:481
  88.8 8.0 %collective-permute-start.20 = (bf16[2,256,256]{2,1,0:T(8,128)(2,1)S(1)}, bf16[2,256,256]{2,1,0:T(8,128)(2,1)S(1)}, u32[]{:S(2)}, u32[]{:S(2)}) collective-permute-start(bf16[2,256,256]{2,1,0:T(8,128)(2,1)S(1)} %get-tuple-element.90), channel_id=1, source_target_pairs={{0,16},{2,66},{4,20},{6,70},{8,24},{10,74},{12,28},{14,78},{16,0},... | collective-permute-start | bytes 786440 | tf_op jit(solution)/shard_map/ppermute | solution.py:481
  89.6 9.9 %collective-permute-start.21 = (bf16[2,256,256]{2,1,0:T(8,128)(2,1)S(1)}, bf16[2,256,256]{2,1,0:T(8,128)(2,1)S(1)}, u32[]{:S(2)}, u32[]{:S(2)}) collective-permute-start(bf16[2,256,256]{2,1,0:T(8,128)(2,1)S(1)} %get-tuple-element.91), channel_id=1, source_target_pairs={{0,8},{2,34},{4,12},{6,38},{8,16},{10,42},{12,20},{14,46},{16,24},... | collective-permute-start | bytes 786440 | tf_op jit(solution)/shard_map/ppermute | solution.py:481
  (6 other events, 77.1 us)
